TPU v7x, 32 devices: a whole 2x2x4 slice. The times are simulated.
32 devices in a mesh: seq: 4 (over y, x), tm: 8 (over z, core).
Axes of the slice: x: 2, y: 2, z: 4, core: 2. Of those that a mesh axis runs over, the one named last changes fastest.
Arguments:
- tokens: float32 [4, 3584, 768], P('seq', 'tm'), may hold values from -6 to 6
- cotangent: float32 [4, 3584, 768], P('seq', 'tm'), may hold values from -6 to 6
- qkv_weights: bfloat16 [11520, 768], P(('seq', 'tm')), may hold values from -0.21875 to 0.21875
- out_weights: bfloat16 [3840, 768], P(('seq', 'tm')), may hold values from -0.875 to 0.875
- up_weights: bfloat16 [2304, 3072], P(('seq', 'tm')), may hold values from -0.21875 to 0.21875
- down_weights: bfloat16 [9216, 768], P(('seq', 'tm')), may hold values from -0.109375 to 0.109375
- gains: bfloat16 [7680], P(('seq', 'tm')), may hold values from 0.5 to 1.5
Outputs:
- layer_out: float32 [4, 3584, 768], P('seq', 'tm')
- token_grad: float32 [4, 3584, 768], P('seq', 'tm')
- qkv_grad: float32 [11520, 768], P(('seq', 'tm'))
- out_grad: float32 [3840, 768], P(('seq', 'tm'))
- up_grad: float32 [2304, 3072], P(('seq', 'tm'))
- down_grad: float32 [9216, 768], P(('seq', 'tm'))
- gain_grad: float32 [7680], P(('seq', 'tm'))
All inputs are finite; a program needn't handle non-finite values.
Results may differ from a plain program's by a relative error of at most 0.015.
Values may be sent and summed in bfloat16 or wider, within the bound.
A program may use at most 320 MiB of HBM per device.

v0:
```python
import jax
import jax.numpy as jnp
from jax import lax
from jax.sharding import PartitionSpec as P

D = 768
HEADS = 12
FF = 3072


EPS = 1e-06
FAR = -1e30


def extended(cells, sides, width):
    for axis, dim in sides:
        count = lax.axis_size(axis)
        ends = count - 1
        head = lax.slice_in_dim(cells, 0, width, axis=dim)
        tail = lax.slice_in_dim(cells, cells.shape[dim] - width, cells.shape[dim], axis=dim)
        cells = jnp.concatenate(
            [
                lax.ppermute(tail, axis, [(i, (i + 1) % count) for i in range(ends)]),
                cells,
                lax.ppermute(head, axis, [((i + 1) % count, i) for i in range(ends)]),
            ],
            axis=dim,
        )
    return cells


def from_behind(block, axis, distance):
    devices = range(lax.axis_size(axis))
    route = [(i - distance, i) for i in devices if i - distance in devices]
    return lax.ppermute(block, axis, route)


def norm_rows(x, gain):
    mean = jnp.mean(x, axis=-1, keepdims=True)
    centered = x - mean
    spread = jnp.mean(centered * centered, axis=-1, keepdims=True)
    return centered * lax.rsqrt(spread + EPS) * gain


def norm_back(x, gain, grad):
    unused, pull = jax.vjp(norm_rows, x, gain)
    return pull(grad)


def gelu_back(hidden_pre, grad):
    unused, pull = jax.vjp(lambda value: jax.nn.gelu(value, approximate=False), hidden_pre)
    return pull(grad)[0]


def lowered(value):
    return value.astype(jnp.bfloat16)


def product(left, right):
    return jnp.dot(left, right, preferred_element_type=jnp.float32)


def product_tn(left, right):
    return lax.dot_general(
        left, right, (((0,), (0,)), ((), ())), preferred_element_type=jnp.float32
    )


def product_nt(left, right):
    return lax.dot_general(
        left, right, (((1,), (1,)), ((), ())), preferred_element_type=jnp.float32
    )


def unstack(parts):
    qkv_flat, out_flat, up_flat, down_flat, gain_flat = parts
    return (
        qkv_flat.reshape(5, 3, D, D),
        out_flat.reshape(5, D, D),
        up_flat.reshape(3, D, FF),
        down_flat.reshape(3, FF, D),
        gain_flat.reshape(5, 2, D),
    )


def attend(query, keys, values, bias):
    rows, width = query.shape
    depth = width // HEADS
    qh = query.reshape(rows, HEADS, depth)
    kh = keys.reshape(keys.shape[0], HEADS, depth)
    vh = values.reshape(values.shape[0], HEADS, depth)
    scores = (
        jnp.einsum("qhd,khd->hqk", qh, kh, preferred_element_type=jnp.float32) * depth ** (-0.5)
        + bias
    )
    top = jnp.max(scores, axis=-1, keepdims=True)
    expo = jnp.exp(scores - top)
    probs = expo / jnp.sum(expo, axis=-1, keepdims=True)
    mixed = jnp.einsum("hqk,khd->qhd", lowered(probs), vh, preferred_element_type=jnp.float32)
    return (lowered(mixed.reshape(rows, width)), probs)


def attend_back(query, keys, values, probs, grad_mixed):
    rows, width = query.shape
    depth = width // HEADS
    qh = query.reshape(rows, HEADS, depth)
    kh = keys.reshape(keys.shape[0], HEADS, depth)
    vh = values.reshape(values.shape[0], HEADS, depth)
    gh = grad_mixed.reshape(rows, HEADS, depth)
    dprobs = jnp.einsum("qhd,khd->hqk", gh, vh, preferred_element_type=jnp.float32)
    dvalues = jnp.einsum("hqk,qhd->khd", lowered(probs), gh, preferred_element_type=jnp.float32)
    inner = jnp.sum(dprobs * probs, axis=-1, keepdims=True)
    dscores = lowered(probs * (dprobs - inner))
    scale = depth ** (-0.5)
    dquery = jnp.einsum("hqk,khd->qhd", dscores, kh, preferred_element_type=jnp.float32) * scale
    dkeys = jnp.einsum("hqk,qhd->khd", dscores, qh, preferred_element_type=jnp.float32) * scale
    return (dquery.reshape(rows, width), dkeys.reshape(-1, width), dvalues.reshape(-1, width))


def per_device(tokens, cotangent, qkv_weights, out_weights, up_weights, down_weights, gains):
    rows = tokens[0]
    incoming = cotangent[0]
    spatial = rows.shape[0] // 7
    bounds = ((0, 4 * spatial), (4 * spatial, 6 * spatial), (6 * spatial, 7 * spatial))
    qkv, outw, upw, downw, gain_low = unstack(
        (
            lax.all_gather(qkv_weights, ("seq", "tm"), axis=0, tiled=True),
            lax.all_gather(out_weights, ("seq", "tm"), axis=0, tiled=True),
            lax.all_gather(up_weights, ("seq", "tm"), axis=0, tiled=True),
            lax.all_gather(down_weights, ("seq", "tm"), axis=0, tiled=True),
            lax.all_gather(gains, ("seq", "tm"), axis=0, tiled=True),
        )
    )
    gain = gain_low.astype(jnp.float32)
    place = lax.axis_index("tm")
    count = lax.axis_size("tm")
    below_bias = jnp.where(place > 0, 0.0, FAR).astype(jnp.float32)
    above_bias = jnp.where(place < count - 1, 0.0, FAR).astype(jnp.float32)
    views = [rows[start:stop] for start, stop in bounds]
    cross_keep = []
    joined = []
    for view in range(2):
        first = lowered(norm_rows(views[view], gain[3 + view, 0]))
        second = lowered(norm_rows(views[view + 1], gain[3 + view, 1]))
        query = lowered(product(first, qkv[3 + view, 0]))
        keys = lowered(product(second, qkv[3 + view, 1]))
        values = lowered(product(second, qkv[3 + view, 2]))
        mixed, probs = attend(query, keys, values, 0.0)
        joined.append(views[view] + product(mixed, outw[3 + view]))
        cross_keep.append((first, second, query, keys, values, mixed, probs))
    joined.append(views[2])
    local_keep = []
    edges = []
    for view in range(3):
        normed = lowered(norm_rows(joined[view], gain[view, 0]))
        query = lowered(product(normed, qkv[view, 0]))
        keys = lowered(product(normed, qkv[view, 1]))
        values = lowered(product(normed, qkv[view, 2]))
        local_keep.append((normed, query, keys, values))
        paired = jnp.stack([keys, values])
        edges.append(jnp.concatenate([paired[:, :spatial], paired[:, -spatial:]], axis=1))
    rim = extended(jnp.stack(edges, axis=1), (("tm", 2),), spatial)
    self_keep = []
    outputs = []
    for view in range(3):
        normed, query, keys, values = local_keep[view]
        length = keys.shape[0]
        keys_all = jnp.concatenate(
            [rim[0, view, :spatial], keys, rim[0, view, 3 * spatial :]], axis=0
        )
        values_all = jnp.concatenate(
            [rim[1, view, :spatial], values, rim[1, view, 3 * spatial :]], axis=0
        )
        bias = jnp.concatenate(
            [
                jnp.broadcast_to(below_bias, (spatial,)),
                jnp.zeros((length,), jnp.float32),
                jnp.broadcast_to(above_bias, (spatial,)),
            ]
        )
        mixed, probs = attend(query, keys_all, values_all, bias)
        middle = joined[view] + product(mixed, outw[view])
        normed_two = lowered(norm_rows(middle, gain[view, 1]))
        hidden_pre = product(normed_two, upw[view])
        active = lowered(jax.nn.gelu(hidden_pre, approximate=False))
        outputs.append(middle + product(active, downw[view]))
        self_keep.append(
            (
                normed,
                query,
                keys_all,
                values_all,
                mixed,
                probs,
                middle,
                normed_two,
                hidden_pre,
                active,
            )
        )
    layer_out = jnp.concatenate(outputs, axis=0)[None]
    qkv, outw, upw, downw, gain_low = unstack(
        (
            lax.all_gather(qkv_weights, ("seq", "tm"), axis=0, tiled=True),
            lax.all_gather(out_weights, ("seq", "tm"), axis=0, tiled=True),
            lax.all_gather(up_weights, ("seq", "tm"), axis=0, tiled=True),
            lax.all_gather(down_weights, ("seq", "tm"), axis=0, tiled=True),
            lax.all_gather(gains, ("seq", "tm"), axis=0, tiled=True),
        )
    )
    grad_qkv = [[None, None, None] for index in range(5)]
    grad_out = [None] * 5
    grad_up = [None] * 3
    grad_down = [None] * 3
    grad_gain = [[None, None] for index in range(5)]
    halves = []
    for view in range(3):
        (
            normed,
            query,
            keys_all,
            values_all,
            mixed,
            probs,
            middle,
            normed_two,
            hidden_pre,
            active,
        ) = self_keep[view]
        start, stop = bounds[view]
        dfinal = incoming[start:stop]
        dbranch = lowered(dfinal)
        grad_down[view] = product_tn(active, dbranch)
        dactive = product_nt(dbranch, downw[view])
        dpre_low = lowered(gelu_back(hidden_pre, dactive))
        grad_up[view] = product_tn(normed_two, dpre_low)
        dnormed_two = product_nt(dpre_low, upw[view])
        dmid_norm, grad_gain[view][1] = norm_back(middle, gain[view, 1], dnormed_two)
        dmiddle = dfinal + dmid_norm
        dattn = lowered(dmiddle)
        grad_out[view] = product_tn(mixed, dattn)
        dmixed = lowered(product_nt(dattn, outw[view]))
        dquery, dkeys, dvalues = attend_back(query, keys_all, values_all, probs, dmixed)
        halves.append((dmiddle, dquery, dkeys, dvalues))
    lower_part = jnp.stack(
        [jnp.stack([half[2][:spatial], half[3][:spatial]]) for half in halves], axis=1
    )
    upper_part = jnp.stack(
        [jnp.stack([half[2][-spatial:], half[3][-spatial:]]) for half in halves], axis=1
    )
    from_above = from_behind(lower_part.astype(jnp.bfloat16), "tm", -1).astype(lower_part.dtype)
    from_below = from_behind(upper_part.astype(jnp.bfloat16), "tm", 1).astype(upper_part.dtype)
    dfused = []
    for view in range(3):
        dmiddle, dquery, dkeys, dvalues = halves[view]
        normed = self_keep[view][0]
        length = dquery.shape[0]
        own_keys = dkeys[spatial : spatial + length]
        own_values = dvalues[spatial : spatial + length]
        own_keys = (
            own_keys.at[:spatial]
            .add(from_below[0, view])
            .at[length - spatial :]
            .add(from_above[0, view])
        )
        own_values = (
            own_values.at[:spatial]
            .add(from_below[1, view])
            .at[length - spatial :]
            .add(from_above[1, view])
        )
        dq_low = lowered(dquery)
        dk_low = lowered(own_keys)
        dv_low = lowered(own_values)
        grad_qkv[view] = [
            product_tn(normed, dq_low),
            product_tn(normed, dk_low),
            product_tn(normed, dv_low),
        ]
        dnormed = (
            product_nt(dq_low, qkv[view, 0])
            + product_nt(dk_low, qkv[view, 1])
            + product_nt(dv_low, qkv[view, 2])
        )
        dfused_norm, grad_gain[view][0] = norm_back(joined[view], gain[view, 0], dnormed)
        dfused.append(dmiddle + dfused_norm)
    dviews = list(dfused)
    for view in range(2):
        first, second, query, keys, values, mixed, probs = cross_keep[view]
        dbranch = lowered(dfused[view])
        grad_out[3 + view] = product_tn(mixed, dbranch)
        dmixed = lowered(product_nt(dbranch, outw[3 + view]))
        dquery, dkeys, dvalues = attend_back(query, keys, values, probs, dmixed)
        dq_low = lowered(dquery)
        dk_low = lowered(dkeys)
        dv_low = lowered(dvalues)
        grad_qkv[3 + view] = [
            product_tn(first, dq_low),
            product_tn(second, dk_low),
            product_tn(second, dv_low),
        ]
        dfirst = product_nt(dq_low, qkv[3 + view, 0])
        dsecond = product_nt(dk_low, qkv[3 + view, 1]) + product_nt(dv_low, qkv[3 + view, 2])
        dx_first, grad_gain[3 + view][0] = norm_back(views[view], gain[3 + view, 0], dfirst)
        dx_second, grad_gain[3 + view][1] = norm_back(views[view + 1], gain[3 + view, 1], dsecond)
        dviews[view] = dviews[view] + dx_first
        dviews[view + 1] = dviews[view + 1] + dx_second
    token_grad = jnp.concatenate(dviews, axis=0)[None]
    qkv_total = jnp.stack([jnp.stack(entry) for entry in grad_qkv]).reshape(15 * D, D)
    out_total = jnp.stack(grad_out).reshape(5 * D, D)
    gain_total = jnp.stack([jnp.stack(entry) for entry in grad_gain]).reshape(10 * D)
    totals = (
        qkv_total,
        out_total,
        jnp.stack(grad_up).reshape(3 * D, FF),
        jnp.stack(grad_down).reshape(3 * FF, D),
        gain_total,
    )
    shares = (
        lax.psum_scatter(totals[0], ("seq", "tm"), scatter_dimension=0, tiled=True),
        lax.psum_scatter(totals[1], ("seq", "tm"), scatter_dimension=0, tiled=True),
        lax.psum_scatter(totals[2], ("seq", "tm"), scatter_dimension=0, tiled=True),
        lax.psum_scatter(totals[3], ("seq", "tm"), scatter_dimension=0, tiled=True),
        lax.psum_scatter(totals[4], ("seq", "tm"), scatter_dimension=0, tiled=True),
    )
    return (layer_out, token_grad, shares[0], shares[1], shares[2], shares[3], shares[4])


def solution(mesh):
    placed = (
        P("seq", "tm", None),
        P("seq", "tm", None),
        P(("seq", "tm"), None),
        P(("seq", "tm"), None),
        P(("seq", "tm"), None),
        P(("seq", "tm"), None),
        P(("seq", "tm")),
    )
    return jax.shard_map(
        per_device,
        mesh=mesh,
        in_specs=placed,
        out_specs=(
            P("seq", "tm", None),
            P("seq", "tm", None),
            P(("seq", "tm"), None),
            P(("seq", "tm"), None),
            P(("seq", "tm"), None),
            P(("seq", "tm"), None),
            P(("seq", "tm")),
        ),
        check_vma=False,
    )
```

profile of v0, /device:TPU:0, one launch (start us, length us, event | category | flops | bytes accessed | tf_op | source)
XLA Modules:
  0.0 1670.4 jit_solution(15745954926317472319)
XLA Ops:
  10.9 43.1 %all-reduce = bf16[7680]{0:T(1024)(128)(2,1)S(1)} all-reduce(bf16[7680]{0:T(1024)(128)(2,1)S(1)} %dynamic-update-slice.32), channel_id=1, replica_groups=mesh['seq'=4,'tm'=8] {'seq','tm'}, use_global_device_ids=true, to_apply=%add | all-reduce | flops 7680 | bytes 30720
  60.1 74.1 %all-gather.5.cloned.1.call-done = bf16[11520,768]{1,0:T(8,128)(2,1)} async-done(((bf16[360,768]{1,0:T(8,128)(2,1)}), bf16[11520,768]{1,0:T(8,128)(2,1)}) %all-gather.5.cloned.1.call-update) | async-done | bytes 17694736 | tf_op jit(solution)/shard_map/all_gather | solution.py:127
  151.2 51.9 %all-gather.7.cloned.1.call-done = bf16[3840,768]{1,0:T(8,128)(2,1)} async-done(((bf16[120,768]{1,0:T(8,128)(2,1)}), bf16[3840,768]{1,0:T(8,128)(2,1)}) %all-gather.7.cloned.1.call-update) | async-done | bytes 5898256 | tf_op jit(solution)/shard_map/all_gather | solution.py:128
  205.7 2.4 fusion.231
  223.6 2.3 convolution_convert_fusion.14
  225.8 4.0 collective-permute-start
  229.9 2.2 convolution_convert_fusion.22
  242.9 2.6 convolution_convert_fusion.3
  253.2 3.5 fusion.235
  256.8 2.2 convolution_convert_fusion.13
  261.6 48.2 %all-gather.9.cloned.1.call-done = bf16[2304,3072]{1,0:T(8,128)(2,1)} async-done(((bf16[72,3072]{1,0:T(8,128)(2,1)}), bf16[2304,3072]{1,0:T(8,128)(2,1)}) %all-gather.9.cloned.1.call-update) | async-done | bytes 14155792 | tf_op jit(solution)/shard_map/all_gather | solution.py:129
  309.8 8.2 multiply_convert_fusion.4
  318.0 96.1 %all-gather.11.cloned.1.call-done = bf16[9216,768]{1,0:T(8,128)(2,1)} async-done(((bf16[288,768]{1,0:T(8,128)(2,1)}), bf16[9216,768]{1,0:T(8,128)(2,1)}) %all-gather.11.cloned.1.call-update) | async-done | bytes 14155792 | tf_op jit(solution)/shard_map/all_gather | solution.py:130
  414.1 5.2 add_convert_fusion.1
  419.4 5.0 multiply_reduce_fusion.15
  429.9 4.3 multiply_reduce_fusion.2
  434.2 2.9 fusion.241
  441.5 5.3 fusion.237
  446.8 3.5 convolution_convert_fusion.2
  452.7 10.6 multiply_convert_fusion.1
  463.3 4.4 add_convert_fusion
  467.7 5.1 multiply_reduce_fusion.4
  473.4 2.5 convolution_convert_fusion.1
  477.9 4.5 fusion.243
  482.4 3.5 multiply_reduce_fusion
  499.3 3.1 fusion.233
  502.4 3.9 convolution_convert_fusion.12
  508.4 3.3 fusion.16
  511.8 5.3 add_convert_fusion.2
  517.1 4.6 multiply_reduce_fusion.26
  523.7 2.4 convolution_convert_fusion.21
  527.8 4.0 fusion.239
  535.3 2.1 multiply_reduce_fusion.8
  545.0 2.4 multiply_convert_fusion.3
  562.8 3.0 collective-permute-start.2
  581.1 2.8 fusion.90
  586.2 2.7 fusion.91
  596.8 2.3 copy.152
  608.4 2.3 copy.144
  612.5 3.1 bitcast_dynamic-update-slice_fusion.2
  618.8 2.7 convolution_add_fusion.6
  621.5 2.6 multiply_reduce_fusion.16
  639.2 10.9 pad_maximum_fusion
  650.1 2.9 convolution_bitcast_fusion.1
  654.5 3.0 convolution_bitcast_fusion
  657.5 10.9 pad_maximum_fusion.1
  678.6 2.9 convolution_bitcast_fusion.14
  685.4 2.8 convolution_convert_fusion.9
  690.0 2.5 convolution_convert_fusion
  695.9 2.9 convolution_bitcast_fusion.12
  700.7 2.3 convolution_convert_fusion.8
  719.8 3.4 fusion.5
  723.2 5.3 fusion.6
  728.6 3.3 fusion.7
  731.9 3.5 fusion.8
  735.4 3.5 fusion.9
  740.3 3.5 fusion.70
  743.8 3.9 fusion.63
  747.8 4.2 fusion.81
  761.3 2.1 multiply_reduce_fusion.3
  767.7 40.5 %all-reduce.1 = f32[7680]{0:T(1024)} all-reduce(f32[7680]{0:T(1024)} %reshape.1260), channel_id=6, replica_groups=mesh['seq'=4,'tm'=8] {'seq','tm'}, use_global_device_ids=true, to_apply=%region_65.66.clone | all-reduce | flops 7680 | bytes 61440
  816.5 235.3 %reduce-scatter.9.cloned.1.call-done = f32[72,3072]{1,0:T(8,128)} async-done(((f32[2304,3072]{1,0:T(8,128)}), f32[72,3072]{1,0:T(8,128)}) %reduce-scatter.9.cloned.1.call-update) | async-done | bytes 884752 | tf_op jit(solution)/shard_map/reduce_scatter | solution.py:322
  1051.8 271.4 %reduce-scatter.11.cloned.1.call-done = f32[288,768]{1,0:T(8,128)} async-done(((f32[9216,768]{1,0:T(8,128)}), f32[288,768]{1,0:T(8,128)}) %reduce-scatter.11.cloned.1.call-update) | async-done | bytes 884752 | tf_op jit(solution)/shard_map/reduce_scatter | solution.py:323
  1323.2 340.2 %reduce-scatter.5.cloned.1.call-done = f32[360,768]{1,0:T(8,128)} async-done(((f32[11520,768]{1,0:T(8,128)}), f32[360,768]{1,0:T(8,128)}) %reduce-scatter.5.cloned.1.call-update) | async-done | bytes 1105936 | tf_op jit(solution)/shard_map/reduce_scatter | solution.py:320
  (757 shorter events, 241.2 us)
Async XLA Ops:
  7.2 51.7 %copy-start = (f32[1,448,768]{2,1,0:T(8,128)S(1)}, f32[1,448,768]{2,1,0:T(8,128)}, u32[]{:S(2)}) copy-start(f32[1,448,768]{2,1,0:T(8,128)} %param.39) | copy-start | bytes 4128772
  7.2 127.0 %all-gather.5.cloned.1.call-start = ((), (), s32[]{:S(2)}) async-start(), calls=%async_computation.4 | async-start | bytes 18247680 | tf_op jit(solution)/shard_map/all_gather | solution.py:127
  7.9 195.3 %all-gather.7.cloned.1.call-start = ((), (), s32[]{:S(2)}) async-start(), calls=%async_computation.5 | async-start | bytes 6082560 | tf_op jit(solution)/shard_map/all_gather | solution.py:128
  8.7 301.2 %all-gather.9.cloned.1.call-start = ((), (), s32[]{:S(2)}) async-start(), calls=%async_computation.6 | async-start | bytes 14598144 | tf_op jit(solution)/shard_map/all_gather | solution.py:129
  9.4 404.8 %all-gather.11.cloned.1.call-start = ((), (), s32[]{:S(2)}) async-start(), calls=%async_computation.7 | async-start | bytes 14598144 | tf_op jit(solution)/shard_map/all_gather | solution.py:130
  10.0 806.5 %reduce-scatter.7.cloned.1.call-start = ((), (), s32[]{:S(2)}) async-start(), calls=%async_computation.9 | async-start | bytes 12165120 | tf_op jit(solution)/shard_map/reduce_scatter | solution.py:321
  56.7 77.5 %copy-start.151 = (f32[768]{0:T(1024)}, f32[768]{0:T(1024)S(1)}, u32[]{:S(2)}) copy-start(f32[768]{0:T(1024)S(1)} %get-tuple-element.220) | copy-start | bytes 9220
  56.7 79.9 %copy-start.160 = (f32[768]{0:T(1024)}, f32[768]{0:T(1024)S(1)}, u32[]{:S(2)}) copy-start(f32[768]{0:T(1024)S(1)} %get-tuple-element.219) | copy-start | bytes 9220
  56.7 87.7 %copy-start.149 = (f32[768]{0:T(1024)}, f32[768]{0:T(1024)S(1)}, u32[]{:S(2)}) copy-start(f32[768]{0:T(1024)S(1)} %get-tuple-element.216) | copy-start | bytes 9220
  57.7 78.1 %copy-start.183 = (f32[64]{0:T(128)}, f32[64]{0:T(128)S(1)}, u32[]{:S(2)}) copy-start(f32[64]{0:T(128)S(1)} %broadcast_multiply_fusion.4) | copy-start | bytes 772
  59.0 85.3 %copy-start.169 = (f32[128]{0:T(128)}, f32[128]{0:T(128)S(1)}, u32[]{:S(2)}) copy-start(f32[128]{0:T(128)S(1)} %broadcast_multiply_fusion.7) | copy-start | bytes 1540
  59.3 79.1 %copy-start.178 = (f32[256]{0:T(256)}, f32[256]{0:T(256)S(1)}, u32[]{:S(2)}) copy-start(f32[256]{0:T(256)S(1)} %broadcast_multiply_fusion.2) | copy-start | bytes 3076
  59.6 78.8 %copy-start.188 = (f32[256]{0:T(256)}, f32[256]{0:T(256)S(1)}, u32[]{:S(2)}) copy-start(f32[256]{0:T(256)S(1)} %multiply_reduce_fusion.12) | copy-start | bytes 3076
  59.8 78.6 %copy-start.207 = (f32[64]{0:T(128)}, f32[64]{0:T(128)S(1)}, u32[]{:S(2)}) copy-start(f32[64]{0:T(128)S(1)} %fusion.181) | copy-start | bytes 772
  59.8 84.6 %copy-start.201 = (f32[128]{0:T(128)}, f32[128]{0:T(128)S(1)}, u32[]{:S(2)}) copy-start(f32[128]{0:T(128)S(1)} %fusion.180) | copy-start | bytes 1540
  59.8 78.6 %copy-start.191 = (f32[256]{0:T(256)}, f32[256]{0:T(256)S(1)}, u32[]{:S(2)}) copy-start(f32[256]{0:T(256)S(1)} %fusion.177) | copy-start | bytes 3076
  60.0 82.5 %copy-start.91 = (bf16[64,768]{1,0:T(8,128)(2,1)}, bf16[64,768]{1,0:T(8,128)(2,1)S(1)}, u32[]{:S(2)}) copy-start(bf16[64,768]{1,0:T(8,128)(2,1)S(1)} %get-tuple-element.243) | copy-start | bytes 294916
  60.0 169.9 %copy-start.62 = (bf16[64,768]{1,0:T(8,128)(2,1)}, bf16[64,768]{1,0:T(8,128)(2,1)S(1)}, u32[]{:S(2)}) copy-start(bf16[64,768]{1,0:T(8,128)(2,1)S(1)} %get-tuple-element.244) | copy-start | bytes 294916
  60.1 78.5 %copy-start.60 = (bf16[128,768]{1,0:T(8,128)(2,1)}, bf16[128,768]{1,0:T(8,128)(2,1)S(1)}, u32[]{:S(2)}) copy-start(bf16[128,768]{1,0:T(8,128)(2,1)S(1)} %fusion.125) | copy-start | bytes 589828
  138.6 67.0 %copy-start.69 = (bf16[256,768]{0,1:T(8,128)(2,1)}, bf16[256,768]{0,1:T(8,128)(2,1)S(1)}, u32[]{:S(2)}) copy-start(bf16[256,768]{0,1:T(8,128)(2,1)S(1)} %copy.105) | copy-start | bytes 1179652
  140.6 65.1 %copy-start.109 = (bf16[128,768]{0,1:T(8,128)(2,1)}, bf16[128,768]{0,1:T(8,128)(2,1)S(1)}, u32[]{:S(2)}) copy-start(bf16[128,768]{0,1:T(8,128)(2,1)S(1)} %copy.106) | copy-start | bytes 589828
  142.4 8.3 copy-start.133
  144.3 6.4 copy-start.50
  150.7 54.9 %copy-start.163 = (f32[12,128]{1,0:T(8,128)}, f32[12,128]{1,0:T(8,128)S(1)}, u32[]{:S(2)}) copy-start(f32[12,128]{1,0:T(8,128)S(1)} %get-tuple-element.279) | copy-start | bytes 18436
  151.2 56.9 %copy-start.95 = (bf16[12,64,128]{2,1,0:T(8,128)(2,1)}, bf16[12,64,128]{2,1,0:T(8,128)(2,1)S(1)}, u32[]{:S(2)}) copy-start(bf16[12,64,128]{2,1,0:T(8,128)(2,1)S(1)} %convolution_convert_fusion.17) | copy-start | bytes 589828
  212.7 10.9 copy-start.41
  212.8 30.1 %copy-start.17 = (bf16[256,768]{1,0:T(8,128)(2,1)}, bf16[256,768]{1,0:T(8,128)(2,1)S(1)}, u32[]{:S(2)}) copy-start(bf16[256,768]{1,0:T(8,128)(2,1)S(1)} %multiply_convert_fusion.8) | copy-start | bytes 1179652
  222.1 18.0 %copy-start.80 = (bf16[256,768]{1,0:T(8,128)(2,1)S(1)}, bf16[256,768]{1,0:T(8,128)(2,1)}, u32[]{:S(2)}) copy-start(bf16[256,768]{1,0:T(8,128)(2,1)} %copy-done.79) | copy-start | bytes 1179652
  222.1 24.6 %collective-permute-start.1 = (bf16[2,3,64,768]{3,2,0,1:T(8,128)(2,1)}, bf16[2,3,64,768]{3,2,0,1:T(8,128)(2,1)}, u32[]{:S(2)}, u32[]{:S(2)}) collective-permute-start(bf16[2,3,64,768]{3,2,0,1:T(8,128)(2,1)} %get-tuple-element.254), channel_id=1, source_target_pairs={{1,0},{2,1},{3,2},{4,3},{5,4},{6,5},{7,6},{9,8},{10,9},{11,10},{12... | collective-permute-start | bytes 1769480 | tf_op jit(solution)/shard_map/ppermute | solution.py:25
  225.8 23.7 %collective-permute-start = (bf16[2,3,64,768]{3,2,0,1:T(8,128)(2,1)}, bf16[2,3,64,768]{3,2,0,1:T(8,128)(2,1)}, u32[]{:S(2)}, u32[]{:S(2)}) collective-permute-start(bf16[2,3,64,768]{3,2,0,1:T(8,128)(2,1)} %get-tuple-element.253), channel_id=1, source_target_pairs={{0,1},{1,2},{2,3},{3,4},{4,5},{5,6},{6,7},{8,9},{9,10},{10,11},{11... | collective-permute-start | bytes 1769480 | tf_op jit(solution)/shard_map/ppermute | solution.py:23
  232.1 8.9 copy-start.157
  242.9 10.3 copy-start.99
  246.7 194.8 %copy-start.67 = (bf16[256,768]{0,1:T(8,128)(2,1)}, bf16[256,768]{0,1:T(8,128)(2,1)S(1)}, u32[]{:S(2)}) copy-start(bf16[256,768]{0,1:T(8,128)(2,1)S(1)} %copy.114) | copy-start | bytes 1179652
  252.4 6.6 copy-start.137
  261.4 163.0 %copy-start.15 = (f32[128,768]{1,0:T(8,128)}, f32[128,768]{1,0:T(8,128)S(1)}, u32[]{:S(2)}) copy-start(f32[128,768]{1,0:T(8,128)S(1)} %get-tuple-element.294) | copy-start | bytes 1179652
  261.4 157.9 %copy-start.196 = (f32[128]{0:T(128)}, f32[128]{0:T(128)S(1)}, u32[]{:S(2)}) copy-start(f32[128]{0:T(128)S(1)} %broadcast_multiply_fusion.5) | copy-start | bytes 1540
  261.6 56.4 %copy-start.230 = (f32[128]{0:T(128)}, f32[128]{0:T(128)S(1)}, u32[]{:S(2)}) copy-start(f32[128]{0:T(128)S(1)} %multiply_reduce_fusion.22) | copy-start | bytes 1540
  261.6 157.7 %copy-start.210 = (f32[128]{0:T(128)}, f32[128]{0:T(128)S(1)}, u32[]{:S(2)}) copy-start(f32[128]{0:T(128)S(1)} %fusion.183) | copy-start | bytes 1540
  434.2 7.3 copy-start.125
  452.4 20.4 %copy-start.1 = (f32[256,768]{1,0:T(8,128)}, f32[256,768]{1,0:T(8,128)S(1)}, u32[]{:S(2)}) copy-start(f32[256,768]{1,0:T(8,128)S(1)} %get-tuple-element.299) | copy-start | bytes 2359300
  452.4 20.4 %copy-start.167 = (f32[256]{0:T(256)}, f32[256]{0:T(256)S(1)}, u32[]{:S(2)}) copy-start(f32[256]{0:T(256)S(1)} %broadcast_multiply_fusion) | copy-start | bytes 3076
  452.7 20.2 %copy-start.181 = (f32[256]{0:T(256)}, f32[256]{0:T(256)S(1)}, u32[]{:S(2)}) copy-start(f32[256]{0:T(256)S(1)} %fusion.179) | copy-start | bytes 3076
  452.7 10.6 copy-start.32
  477.9 8.0 slice-start.5
  490.6 8.7 copy-start.101
  508.2 13.6 copy-start.186
  508.4 13.4 copy-start.205
  562.8 52.8 %collective-permute-start.2 = (bf16[2,3,64,768]{3,2,1,0:T(8,128)(2,1)}, bf16[2,3,64,768]{3,2,1,0:T(8,128)(2,1)}, u32[]{:S(2)}, u32[]{:S(2)}) collective-permute-start(bf16[2,3,64,768]{3,2,1,0:T(8,128)(2,1)} %pad_maximum_fusion.5), channel_id=1, source_target_pairs={{0,1},{1,2},{2,3},{3,4},{4,5},{5,6},{6,7},{8,9},{9,10},{10,11},{11... | collective-permute-start | bytes 1769480 | tf_op jit(solution)/shard_map/ppermute | solution.py:35
  575.9 8.0 copy-start.21
  575.9 8.0 copy-start.98
  579.8 37.2 %collective-permute-start.3 = (bf16[2,3,64,768]{3,2,1,0:T(8,128)(2,1)}, bf16[2,3,64,768]{3,2,1,0:T(8,128)(2,1)}, u32[]{:S(2)}, u32[]{:S(2)}) collective-permute-start(bf16[2,3,64,768]{3,2,1,0:T(8,128)(2,1)} %pad_maximum_fusion.6), channel_id=1, source_target_pairs={{1,0},{2,1},{3,2},{4,3},{5,4},{6,5},{7,6},{9,8},{10,9},{11,10},{12... | collective-permute-start | bytes 1769480 | tf_op jit(solution)/shard_map/ppermute | solution.py:35
  618.8 7.5 copy-start.13
  633.5 418.3 %reduce-scatter.9.cloned.1.call-start = ((), (), s32[]{:S(2)}) async-start(), calls=%async_computation.10 | async-start | bytes 29196288 | tf_op jit(solution)/shard_map/reduce_scatter | solution.py:322
  650.1 673.1 %reduce-scatter.11.cloned.1.call-start = ((), (), s32[]{:S(2)}) async-start(), calls=%async_computation.11 | async-start | bytes 29196288 | tf_op jit(solution)/shard_map/reduce_scatter | solution.py:323
  668.4 995.0 %reduce-scatter.5.cloned.1.call-start = ((), (), s32[]{:S(2)}) async-start(), calls=%async_computation.8 | async-start | bytes 36495360 | tf_op jit(solution)/shard_map/reduce_scatter | solution.py:320
  743.8 10.3 slice-start
  743.8 10.3 slice-start.1
  747.7 6.7 slice-start.4
  763.3 51.5 %copy-start.25 = (f32[128,768]{1,0:T(8,128)S(1)}, f32[128,768]{1,0:T(8,128)}, u32[]{:S(2)}) copy-start(f32[128,768]{1,0:T(8,128)} %copy-done.23) | copy-start | bytes 1179652
  808.3 6.4 copy-start.221
  808.3 6.6 copy-start.172
  808.3 6.6 copy-start.204
  808.3 6.6 copy-start.217
  808.3 6.6 copy-start.227
  (187 other events, 534.2 us)
Sparse Core Ops, SparseCore 0:
  11.0 123.1 all-gather.4
  137.2 65.9 all-gather.6
  206.2 103.5 all-gather.8
  312.7 101.4 all-gather.10
  633.6 147.4 reduce-scatter.6
  789.1 262.6 reduce-scatter.8
  1059.9 263.2 reduce-scatter.10
  1331.3 331.9 reduce-scatter.4
where the time goes:
time: 1680 us; the launch traced here: 1670 us
  waiting for transfers between devices  1120 us (67%)
  matrix products  237 us (14%)
  local copies, waits for them, and re-layouts  120 us (7%)
  blocking collectives  83.6 us (5%)
  other arithmetic  81.4 us (5%)
  between operations  17.7 us (1%)
    reduce_scatter x1, waiting for transfers between devices, per_device(): lax.psum_scatter(totals[0], ('seq', 'tm'), scatter_dimension=0, tiled=True)  340 us
    reduce_scatter x1, waiting for transfers between devices, per_device(): lax.psum_scatter(totals[3], ('seq', 'tm'), scatter_dimension=0, tiled=True)  271 us
    reduce_scatter x1, waiting for transfers between devices, per_device(): lax.psum_scatter(totals[2], ('seq', 'tm'), scatter_dimension=0, tiled=True)  235 us
    all_gather x1, waiting for transfers between devices, per_device(): lax.all_gather(down_weights, ('seq', 'tm'), axis=0, tiled=True)  96.1 us
    unnamed x2, blocking collectives  83.6 us
    all_gather x1, waiting for transfers between devices, per_device(): lax.all_gather(qkv_weights, ('seq', 'tm'), axis=0, tiled=True)  74.1 us
    dot_general x26, matrix products, product(): return jnp.dot(left, right, preferred_element_type=jnp.float32)  70.8 us
    dot_general x26, matrix products, product_nt(): lax.dot_general(left, right, (((1,), (1,)), ((), ())), preferred_element_...  62.8 us
  transfers between devices with their start and end apart: 12, of which 7 were waited for; matrix products, arithmetic and copies ran while one was open for 16% of the time, Pallas kernels for 0%

commit v1 on v0

--- a/solution.py
+++ b/solution.py
@@ -1,15 +1,26 @@
+import functools
+
 import jax
 import jax.numpy as jnp
 from jax import lax
+from jax.experimental import pallas as pl
+from jax.experimental.pallas import tpu as pltpu
 from jax.sharding import PartitionSpec as P
 
 D = 768
 HEADS = 12
 FF = 3072
 
-
 EPS = 1e-06
 FAR = -1e30
+MESH = pl.DeviceIdType.MESH
+BF = jnp.bfloat16
+F32 = jnp.float32
+BLOCK = D // 2
+ROWS = 48
+LAG = 0.5
+SLOTS = 36
+COPIES = 480
 
 
 def extended(cells, sides, width):
@@ -117,7 +128,567 @@
     return (dquery.reshape(rows, width), dkeys.reshape(-1, width), dvalues.reshape(-1, width))
 
 
-def per_device(tokens, cotangent, qkv_weights, out_weights, up_weights, down_weights, gains):
+class Place:
+    def __init__(self, dims):
+        self.dims = dims
+        s = lax.axis_index("seq")
+        t = lax.axis_index("tm")
+        self.at = (s // dims[1], s % dims[1], t // 2)
+        self.core = t % 2
+
+    def device(self, at, core):
+        return (at[0] * self.dims[1] + at[1], at[2] * 2 + core)
+
+    def along(self, dim, value):
+        at = list(self.at)
+        at[dim] = value
+        return self.device(at, self.core)
+
+    def sibling(self):
+        return self.device(self.at, 1 - self.core)
+
+
+def meet(place):
+    barrier = pltpu.get_barrier_semaphore()
+    count = 1
+    pl.semaphore_signal(barrier, inc=1, device_id=place.sibling(), device_id_type=MESH)
+    for dim, n in enumerate(place.dims):
+        me = place.at[dim]
+        for step in (1, -1):
+            ok = (me + step >= 0) & (me + step < n)
+
+            @pl.when(ok)
+            def _():
+                pl.semaphore_signal(barrier, inc=1, device_id=place.along(dim, me + step), device_id_type=MESH)
+
+            count = count + jnp.where(ok, 1, 0)
+    pl.semaphore_wait(barrier, count)
+
+
+class Copies:
+    def __init__(self, send, recv):
+        self.send, self.recv = send, recv
+        self.used = 0
+        self.sent = []
+
+    def start(self, src, dst, device, ok=None):
+        copy = pltpu.make_async_remote_copy(
+            src_ref=src,
+            dst_ref=dst,
+            send_sem=self.send.at[self.used],
+            recv_sem=self.recv.at[self.used],
+            device_id=device,
+            device_id_type=MESH,
+        )
+        self.used += 1
+        when(ok, copy.start)
+        self.sent.append((copy, ok))
+        return copy
+
+    def drain(self):
+        for copy, ok in self.sent:
+            when(ok, copy.wait_send)
+        self.sent = []
+
+
+def when(ok, action):
+    if ok is None:
+        action()
+    else:
+
+        @pl.when(ok)
+        def _():
+            action()
+
+
+def gather_line(copies, place, dim, pick):
+    n = place.dims[dim]
+    me = place.at[dim]
+    if n == 2:
+        part = pick(me)
+        copy = copies.start(part, part, place.along(dim, 1 - me))
+        yield
+        copy.wait_recv()
+        return
+    before = {}
+    for hop in range(1, n):
+        for step in (1, -1):
+            origin = me - step * (hop - 1)
+            held = (origin >= 0) & (origin < n)
+            if hop > 1:
+                when(held, before[step].wait_recv)
+            ok = held & (me + step >= 0) & (me + step < n)
+            part = pick(jnp.clip(origin, 0, n - 1))
+            before[step] = copies.start(part, part, place.along(dim, jnp.clip(me + step, 0, n - 1)), ok)
+        yield
+    for step in (1, -1):
+        origin = me - step * (n - 1)
+        when((origin >= 0) & (origin < n), before[step].wait_recv)
+
+
+def gather_piece(copies, place, full, rows, cols, order, pair):
+    done = set()
+    for dim in order:
+
+        def pick(value):
+            index = [slice(None) if d in done else place.at[d] for d in range(3)]
+            index[dim] = value
+            return full.at[(*index, pl.ds(*rows), cols)]
+
+        yield from gather_line(copies, place, dim, pick)
+        done.add(dim)
+    if pair is not None:
+        part = full.at[:, :, :, pl.ds(*rows), cols]
+        pair.append(copies.start(part, part, place.sibling()))
+
+
+ZXY, ZYX, XZY, YZX = (2, 1, 0), (2, 0, 1), (1, 2, 0), (0, 2, 1)
+CYCLE = (XZY, YZX, ZXY, XZY, YZX, ZYX)
+
+
+def pieces_of(slabs, arrays):
+    flat = []
+    for array in arrays:
+        rows, width = slabs[array]
+        for block in range(width // 2 // BLOCK):
+            for row in range(0, rows, ROWS):
+                flat.append((array, row, block, CYCLE[len(flat) % 6]))
+    return [flat[i : i + 3] for i in range(0, len(flat), 3)]
+
+
+def march(sets, begin, extra=(), between=None):
+    waiting = list(sets)
+    active = list(extra)
+    step = 0
+    while active or waiting:
+        while waiting and step >= LAG * (len(sets) - len(waiting)):
+            for piece in waiting.pop(0):
+                active.append(begin(piece))
+        still = []
+        for one in active:
+            try:
+                next(one)
+                still.append(one)
+            except StopIteration:
+                pass
+        active = still
+        if between is not None:
+            between(step)
+        step += 1
+
+
+def gather_kernel(dims, qkv, out, up, down, gain, fqkv, fout, fup, fdown, fgain, *scratch):
+    place = Place(dims)
+    shards = (qkv, out, up, down)
+    fulls = (fqkv, fout, fup, fdown)
+    theirs = scratch[:4]
+    merged = scratch[4:8]
+    gain_pair, send, recv, local = scratch[8:]
+    copies = Copies(send, recv)
+    core = place.core
+    meet(place)
+    width = [s.shape[1] // 2 for s in shards]
+    mine = [pl.ds(pl.multiple_of(core * w, 128), w) for w in width]
+    other = [pl.ds(pl.multiple_of((1 - core) * w, 128), w) for w in width]
+    swaps = []
+    for a in range(4):
+        swaps.append(copies.start(shards[a].at[:, other[a]], theirs[a], place.sibling()))
+    gain_pair[core] = gain[...]
+    part = gain_pair.at[core]
+    swap_gain = copies.start(part, part, place.sibling())
+    at = place.at
+
+    def prepare(a):
+        swaps[a].wait_recv()
+        w = width[a]
+        own = jnp.where(core == 0, shards[a][:, :w].astype(F32), shards[a][:, w:].astype(F32))
+        got = theirs[a][...].astype(F32)
+        upper = jnp.where(core == 0, own, got)
+        lower = jnp.where(core == 0, got, own)
+        merged[a][...] = jnp.concatenate([upper, lower], axis=0).astype(BF)
+        copy = pltpu.make_async_copy(merged[a], fulls[a].at[at[0], at[1], at[2], :, mine[a]], local.at[a])
+        copy.start()
+        copy.wait()
+
+    pair = []
+    ready = set()
+
+    def begin(piece):
+        a, row, block, order = piece
+        if a not in ready:
+            prepare(a)
+            ready.add(a)
+        cols = pl.ds(pl.multiple_of(core * width[a] + block * BLOCK, 128), BLOCK)
+        return gather_piece(copies, place, fulls[a], (row, ROWS), cols, order, pair)
+
+    def gains():
+        swap_gain.wait_recv()
+        copy = pltpu.make_async_copy(gain_pair, fgain.at[at[0], at[1], at[2]], local.at[4])
+        copy.start()
+        copy.wait()
+        done = set()
+        for dim in ZXY:
+
+            def pick(value):
+                index = [slice(None) if d in done else at[d] for d in range(3)]
+                index[dim] = value
+                return fgain.at[tuple(index)]
+
+            yield from gather_line(copies, place, dim, pick)
+            done.add(dim)
+
+    march(pieces_of([m.shape[:1] + (2 * m.shape[1],) for m in merged], range(4)), begin, (gains(),))
+    for copy in pair:
+        copy.wait_recv()
+    copies.drain()
+
+
+def gather_all(dims, qkv, out, up, down, gain):
+    shards = (qkv, out, up, down)
+    slabs = [(2 * s.shape[0], s.shape[1]) for s in shards]
+    anywhere = pl.BlockSpec(memory_space=pl.ANY)
+    vmem = pl.BlockSpec(memory_space=pltpu.VMEM)
+    return pl.pallas_call(
+        functools.partial(gather_kernel, dims),
+        out_shape=[jax.ShapeDtypeStruct((*dims, *s), BF) for s in slabs]
+        + [jax.ShapeDtypeStruct((*dims, 2, 8, 128), F32)],
+        in_specs=[vmem] * 5,
+        out_specs=[anywhere] * 5,
+        scratch_shapes=[pltpu.VMEM((r // 2, w // 2), BF) for r, w in slabs]
+        + [pltpu.VMEM((r, w // 2), BF) for r, w in slabs]
+        + [
+            pltpu.VMEM((2, 8, 128), F32),
+            pltpu.SemaphoreType.DMA((COPIES,)),
+            pltpu.SemaphoreType.DMA((COPIES,)),
+            pltpu.SemaphoreType.DMA((5,)),
+        ],
+        compiler_params=pltpu.CompilerParams(
+            collective_id=0, has_side_effects=True, vmem_limit_bytes=48 << 20
+        ),
+    )(qkv, out, up, down, gain)
+
+
+def add_to(total, term):
+    total[...] = (total[...].astype(F32) + term[...].astype(F32)).astype(total.dtype)
+
+
+def reduce_line(copies, place, pick, slots):
+    n = place.dims[2]
+    z = place.at[2]
+    before = {}
+    for turn in range(n):
+        for step in (1, -1):
+            far = z if step == 1 else n - 1 - z
+            goal = far + n - 1 - turn
+            goal = jnp.minimum(goal if step == 1 else n - 1 - goal, n - 1)
+            goal = jnp.maximum(goal, 0)
+            if turn > 0:
+
+                def take(step=step, turn=turn, goal=goal):
+                    before[step].wait_recv()
+                    add_to(pick(goal), slots(turn - 1, step))
+
+                when((far >= 1) & (far <= turn), take)
+            if turn < n - 1:
+                before[step] = copies.start(
+                    pick(goal), slots(turn, step), place.along(2, jnp.clip(z + step, 0, n - 1)), far <= turn
+                )
+        if turn < n - 1:
+            yield
+
+
+def reduce_piece(copies, place, source, order, acc, first, turns, last, local, finish):
+    lead = order[0]
+    rest = 1 - lead
+    me, mine = place.at[lead], place.at[rest]
+    z = place.at[2]
+    copy = copies.start(source(lead, 1 - me), first, place.along(lead, 1 - me))
+    load = pltpu.make_async_copy(source(lead, me), acc, local)
+    load.start()
+    yield
+    load.wait()
+    copy.wait_recv()
+    add_to(acc, first)
+    slots = lambda turn, step: turns.at[turn, (1 - step) // 2]
+    if order[1] == 2:
+        yield from reduce_line(copies, place, lambda v: acc.at[:, v], slots)
+        copy = copies.start(acc.at[1 - mine, z], last, place.along(rest, 1 - mine))
+        yield
+        copy.wait_recv()
+        finish(acc[mine, z].astype(F32) + last[...].astype(F32))
+    else:
+        copy = copies.start(acc.at[1 - mine], last, place.along(rest, 1 - mine))
+        yield
+        copy.wait_recv()
+        add_to(acc.at[mine], last)
+        yield from reduce_line(copies, place, lambda v: acc.at[mine, v], slots)
+        finish(acc[mine, z].astype(F32))
+
+
+LEFTS = ("active", "normed_two", "mixed", "normed", "first", "second", "cross_mixed")
+RIGHTS = ("d_out", "d_pre", "d_attn", "dq", "dk", "dv", "d_cross", "cq", "ck", "cv")
+
+
+def jobs_of(spatial):
+    rows = {0: (0, 4 * spatial), 1: (4 * spatial, 2 * spatial), 2: (6 * spatial, spatial)}
+    late = {0: (0, 2 * spatial), 1: (2 * spatial, spatial)}
+    jobs = {a: [] for a in range(4)}
+    for view in range(3):
+        for block in range(FF // D):
+            jobs[3].append((view * FF + block * D, 0, "active", block, rows[view], "d_out", 0, rows[view]))
+        for block in range(FF // 2 // BLOCK):
+            jobs[2].append((view * D, block, "normed_two", 0, rows[view], "d_pre", block, rows[view]))
+        jobs[1].append((view * D, 0, "mixed", 0, rows[view], "d_attn", 0, rows[view]))
+        for j, name in enumerate(("dq", "dk", "dv")):
+            jobs[0].append(((3 * view + j) * D, 0, "normed", 0, rows[view], name, 0, rows[view]))
+    for view in range(2):
+        jobs[1].append(((3 + view) * D, 0, "cross_mixed", 0, rows[view], "d_cross", 0, rows[view]))
+        jobs[0].append(((9 + 3 * view) * D, 0, "first", 0, rows[view], "cq", 0, rows[view]))
+        for j, name in enumerate(("ck", "cv")):
+            jobs[0].append(((10 + 3 * view + j) * D, 0, "second", 0, late[view], name, 0, late[view]))
+    return jobs
+
+
+def reduce_kernel(dims, slabs, sets, count, spatial, *refs):
+    refs = list(refs)
+    take = lambda n: [refs.pop(0) for _ in range(n)]
+    lefts, rights = dict(zip(LEFTS, take(7))), dict(zip(RIGHTS, take(10)))
+    (gain,) = take(1)
+    results = take(4)
+    (gain_out,) = take(1)
+    parts = take(4)
+    far_lefts, far_rights = dict(zip(LEFTS, take(7))), dict(zip(RIGHTS, take(10)))
+    acc, first, turns_a, turns_b, last_a, last_b = take(6)
+    finals = take(4)
+    xs, ys, made = take(3)
+    g_far, g_acc, g_first, g_turns, g_last = take(5)
+    send, recv, local, load_sem, store_sem, final_sem = take(6)
+    place = Place(dims)
+    core = place.core
+    copies = Copies(send, recv)
+    meet(place)
+    half_of = lambda ref, c: pl.ds(pl.multiple_of(c * (ref.shape[1] // 2), 128), ref.shape[1] // 2)
+    coming = {}
+    for name in ("active", "d_out", "normed_two", "d_pre", "mixed", "d_attn", "normed", "dq", "dk", "dv", "cross_mixed", "d_cross", "first", "cq", "second", "ck", "cv"):
+        if name in lefts:
+            coming[name] = copies.start(lefts[name], far_lefts[name], place.sibling())
+        else:
+            ref = rights[name]
+            coming[name] = copies.start(ref.at[:, half_of(ref, 1 - core)], far_rights[name], place.sibling())
+    swap_gain = copies.start(gain, g_far, place.sibling())
+
+    arrived = set()
+
+    def arrive(name):
+        if name not in arrived:
+            coming[name].wait_recv()
+            arrived.add(name)
+
+    order = [(a, job) for a in (3, 2, 1, 0) for job in jobs_of(spatial)[a]]
+
+    def load(i):
+        a, (row, block, left, lcol, lrows, right, rcol, rrows) = order[i]
+        slot = i % 2
+        arrive(left)
+        arrive(right)
+        n = lrows[1]
+        ref = rights[right]
+        own = pl.ds(pl.multiple_of(core * (ref.shape[1] // 2) + rcol * BLOCK, 128), BLOCK)
+        pairs = [
+            (lefts[left].at[pl.ds(*lrows), pl.ds(lcol * D, D)], xs.at[slot, pl.ds(0, n)]),
+            (far_lefts[left].at[pl.ds(*lrows), pl.ds(lcol * D, D)], xs.at[slot, pl.ds(n, n)]),
+            (ref.at[pl.ds(*rrows), own], ys.at[slot, pl.ds(0, n)]),
+            (far_rights[right].at[pl.ds(*rrows), pl.ds(rcol * BLOCK, BLOCK)], ys.at[slot, pl.ds(n, n)]),
+        ]
+        loads = [pltpu.make_async_copy(s, d, load_sem.at[slot, j]) for j, (s, d) in enumerate(pairs)]
+        for one in loads:
+            one.start()
+        return loads
+
+    loading = {0: load(0)}
+    storing = {}
+    done = {"jobs": 0}
+
+    def store(i):
+        a, job = order[i]
+        row, block = job[0], job[1]
+        slab = slabs[a][0]
+        slot = i % 2
+        stores = []
+        at, end = row, row + D
+        while at < end:
+            chip, off = at // slab, at % slab
+            n = min(end - at, slab - off)
+            p, q, z = chip // (dims[1] * dims[2]), chip // dims[2] % dims[1], chip % dims[2]
+            stores.append(
+                pltpu.make_async_copy(
+                    made.at[slot, pl.ds(at - row, n)],
+                    parts[a].at[p, q, z, pl.ds(off, n), pl.ds(block * BLOCK, BLOCK)],
+                    store_sem.at[slot, len(stores)],
+                )
+            )
+            at += n
+        for one in stores:
+            one.start()
+        return stores
+
+    def finish_stores(i):
+        for one in storing.pop(i, ()):
+            one.wait()
+
+    def multiply(upto):
+        while done["jobs"] < upto:
+            i = done["jobs"]
+            for one in loading.pop(i):
+                one.wait()
+            if i + 1 < len(order):
+                loading[i + 1] = load(i + 1)
+            finish_stores(i - 2)
+            n = 2 * order[i][1][4][1]
+            slot = i % 2
+            made[slot] = lax.dot_general(
+                xs[slot, :n], ys[slot, :n], (((0,), (0,)), ((), ())), preferred_element_type=F32
+            ).astype(BF)
+            storing[i] = store(i)
+            done["jobs"] += 1
+
+    upto = {}
+    for a in (3, 2, 1, 0):
+        upto[a] = max(i for i, one in enumerate(order) if one[0] == a) + 1
+
+    used = {"n": 0, 0: 0, 1: 0}
+    owners = []
+    left_in = {a: sum(1 for s in sets for piece in s if piece[0] == a) for a in range(4)}
+    ending = []
+
+    def begin(piece):
+        a, row, block, order_ = piece
+        multiply(upto[a])
+        for i in list(storing):
+            finish_stores(i)
+        i = used["n"]
+        used["n"] += 1
+        kind = 0 if order_[1] == 0 or order_[1] == 2 else 1
+        way = order_[::-1]
+        kind = 0 if way[1] == 2 else 1
+        k = used[kind]
+        used[kind] += 1
+        slot = i % SLOTS
+        if i >= SLOTS:
+            owners[i - SLOTS].drain()
+        mine = Copies(send, recv)
+        mine.used = copies.used
+        copies.used += 9
+        owners.append(mine)
+        cols = pl.ds(block * BLOCK, BLOCK)
+
+        def source(dim, value):
+            index = [slice(None)] * 3
+            index[dim] = value
+            return parts[a].at[(*index, pl.ds(row, ROWS), cols)]
+
+        def finish(value):
+            finals[a][pl.ds(row, ROWS), cols] = value
+            left_in[a] -= 1
+            if left_in[a] == 0:
+                deliver(a)
+
+        turns, last = ((turns_a, last_a), (turns_b, last_b))[kind]
+        return reduce_piece(
+            mine, place, source, way, acc.at[slot], first.at[i], turns.at[k], last.at[k], local.at[slot], finish
+        )
+
+    def deliver(a):
+        rows, width = slabs[a][0] // 2, slabs[a][1] // 2
+        cols = pl.ds(pl.multiple_of(core * width, 128), width)
+        ending.append(
+            copies.start(
+                finals[a].at[pl.ds(pl.multiple_of((1 - core) * rows, 8), rows)], results[a].at[:, cols], place.sibling()
+            )
+        )
+        keep = pltpu.make_async_copy(
+            finals[a].at[pl.ds(pl.multiple_of(core * rows, 8), rows)], results[a].at[:, cols], final_sem.at[a]
+        )
+        keep.start()
+        keep.wait()
+
+    def gains():
+        swap_gain.wait_recv()
+        add_to(g_far, gain)
+        source = lambda dim, value: g_far.at[(*[value if d == dim else slice(None) for d in range(3)], core)]
+
+        def finish(value):
+            gain_out[...] = value
+
+        yield from reduce_piece(copies, place, source, (0, 1, 2), g_acc, g_first, g_turns, g_last, local.at[SLOTS], finish)
+
+    def between(step):
+        multiply(min(len(order), done["jobs"] + 6))
+
+    march(sets, begin, (gains(),), between)
+    for one in ending:
+        one.wait_recv()
+    copies.drain()
+    for one in owners:
+        one.drain()
+
+
+def reduce_all(dims, slabs, lefts, rights, gain):
+    anywhere = pl.BlockSpec(memory_space=pl.ANY)
+    vmem = pl.BlockSpec(memory_space=pltpu.VMEM)
+    sets = pieces_of(slabs, (3, 2, 1, 0))
+    flat = [piece for group in sets for piece in group]
+    count = len(flat)
+    bundled = sum(1 for piece in flat if piece[3][1] == 2)
+    single = count - bundled
+    z = dims[2]
+    spatial = lefts[0].shape[0] // 7
+    longest = 2 * 4 * spatial
+    tile = (ROWS, BLOCK)
+    segments = max(D // slab[0] + 2 for slab in slabs)
+    halves = lambda ref: jax.ShapeDtypeStruct((ref.shape[0], ref.shape[1] // 2), BF)
+    outs = pl.pallas_call(
+        functools.partial(reduce_kernel, dims, slabs, sets, count, spatial),
+        out_shape=[jax.ShapeDtypeStruct((s[0] // 2, s[1]), F32) for s in slabs]
+        + [jax.ShapeDtypeStruct((8, 128), F32)]
+        + [jax.ShapeDtypeStruct((*dims, s[0], s[1] // 2), BF) for s in slabs]
+        + [jax.ShapeDtypeStruct(x.shape, BF) for x in lefts]
+        + [halves(y) for y in rights],
+        in_specs=[anywhere] * 17 + [vmem],
+        out_specs=[vmem] * 5 + [anywhere] * 21,
+        scratch_shapes=[
+            pltpu.VMEM((SLOTS, 2, z, *tile), BF),
+            pltpu.VMEM((count, 2, z, *tile), BF),
+            pltpu.VMEM((bundled, z - 1, 2, 2, *tile), BF),
+            pltpu.VMEM((single, z - 1, 2, *tile), BF),
+            pltpu.VMEM((bundled, *tile), BF),
+            pltpu.VMEM((single, z, *tile), BF),
+        ]
+        + [pltpu.VMEM((s[0], s[1] // 2), F32) for s in slabs]
+        + [
+            pltpu.VMEM((2, longest, D), BF),
+            pltpu.VMEM((2, longest, BLOCK), BF),
+            pltpu.VMEM((2, D, BLOCK), BF),
+            pltpu.VMEM((*dims, 2, 8, 128), F32),
+            pltpu.VMEM((2, z, 8, 128), F32),
+            pltpu.VMEM((2, z, 8, 128), F32),
+            pltpu.VMEM((z - 1, 2, 8, 128), F32),
+            pltpu.VMEM((z, 8, 128), F32),
+            pltpu.SemaphoreType.DMA((COPIES,)),
+            pltpu.SemaphoreType.DMA((COPIES,)),
+            pltpu.SemaphoreType.DMA((SLOTS + 1,)),
+            pltpu.SemaphoreType.DMA((2, 4)),
+            pltpu.SemaphoreType.DMA((2, segments)),
+            pltpu.SemaphoreType.DMA((4,)),
+        ],
+        compiler_params=pltpu.CompilerParams(
+            collective_id=1, has_side_effects=True, vmem_limit_bytes=60 << 20
+        ),
+    )(*lefts, *rights, gain)
+    return outs[:5]
+
+
+def plain_device(tokens, cotangent, qkv_weights, out_weights, up_weights, down_weights, gains):
     rows = tokens[0]
     incoming = cotangent[0]
     spatial = rows.shape[0] // 7
@@ -326,7 +897,156 @@
     return (layer_out, token_grad, shares[0], shares[1], shares[2], shares[3], shares[4])
 
 
+def per_device(dims, tokens, cotangent, qkv_weights, out_weights, up_weights, down_weights, gains):
+    rows = tokens[0]
+    incoming = cotangent[0]
+    spatial = rows.shape[0] // 7
+    bounds = ((0, 4 * spatial), (4 * spatial, 6 * spatial), (6 * spatial, 7 * spatial))
+    own_gains = gains.shape[0]
+    tile = jnp.pad(gains.astype(F32), (0, 1024 - own_gains)).reshape(8, 128)
+    shards = (qkv_weights, out_weights, up_weights, down_weights)
+    slabs = tuple((2 * w.shape[0], w.shape[1]) for w in shards)
+    wholes = gather_all(dims, *shards, tile)
+    gain = wholes[4].reshape(-1, 1024)[:, :own_gains].reshape(5, 2, D)
+    qkv = wholes[0].reshape(5, 3, D, D)
+    outw = wholes[1].reshape(5, D, D)
+    upw = wholes[2].reshape(3, D, FF)
+    downw = wholes[3].reshape(3, FF, D)
+    place = lax.axis_index("tm")
+    count = lax.axis_size("tm")
+    below_bias = jnp.where(place > 0, 0.0, FAR).astype(jnp.float32)
+    above_bias = jnp.where(place < count - 1, 0.0, FAR).astype(jnp.float32)
+    views = [rows[start:stop] for start, stop in bounds]
+    cross_keep = []
+    joined = []
+    for view in range(2):
+        first = lowered(norm_rows(views[view], gain[3 + view, 0]))
+        second = lowered(norm_rows(views[view + 1], gain[3 + view, 1]))
+        query = lowered(product(first, qkv[3 + view, 0]))
+        keys = lowered(product(second, qkv[3 + view, 1]))
+        values = lowered(product(second, qkv[3 + view, 2]))
+        mixed, probs = attend(query, keys, values, 0.0)
+        joined.append(views[view] + product(mixed, outw[3 + view]))
+        cross_keep.append((first, second, query, keys, values, mixed, probs))
+    joined.append(views[2])
+    local_keep = []
+    edges = []
+    for view in range(3):
+        normed = lowered(norm_rows(joined[view], gain[view, 0]))
+        query = lowered(product(normed, qkv[view, 0]))
+        keys = lowered(product(normed, qkv[view, 1]))
+        values = lowered(product(normed, qkv[view, 2]))
+        local_keep.append((normed, query, keys, values))
+        paired = jnp.stack([keys, values])
+        edges.append(jnp.concatenate([paired[:, :spatial], paired[:, -spatial:]], axis=1))
+    rim = extended(jnp.stack(edges, axis=1), (("tm", 2),), spatial)
+    self_keep = []
+    outputs = []
+    for view in range(3):
+        normed, query, keys, values = local_keep[view]
+        length = keys.shape[0]
+        keys_all = jnp.concatenate([rim[0, view, :spatial], keys, rim[0, view, 3 * spatial :]], axis=0)
+        values_all = jnp.concatenate([rim[1, view, :spatial], values, rim[1, view, 3 * spatial :]], axis=0)
+        bias = jnp.concatenate(
+            [
+                jnp.broadcast_to(below_bias, (spatial,)),
+                jnp.zeros((length,), jnp.float32),
+                jnp.broadcast_to(above_bias, (spatial,)),
+            ]
+        )
+        mixed, probs = attend(query, keys_all, values_all, bias)
+        middle = joined[view] + product(mixed, outw[view])
+        normed_two = lowered(norm_rows(middle, gain[view, 1]))
+        hidden_pre = product(normed_two, upw[view])
+        active = lowered(jax.nn.gelu(hidden_pre, approximate=False))
+        outputs.append(middle + product(active, downw[view]))
+        self_keep.append((normed, query, keys_all, values_all, mixed, probs, middle, normed_two, hidden_pre, active))
+    layer_out = jnp.concatenate(outputs, axis=0)[None]
+    grad_gain = [[None, None] for index in range(5)]
+    halves = []
+    d_pre, d_attn = [], []
+    d_out = lowered(incoming)
+    for view in range(3):
+        normed, query, keys_all, values_all, mixed, probs, middle, normed_two, hidden_pre, active = self_keep[view]
+        start, stop = bounds[view]
+        dfinal = incoming[start:stop]
+        dactive = product_nt(d_out[start:stop], downw[view])
+        d_pre.append(lowered(gelu_back(hidden_pre, dactive)))
+        dnormed_two = product_nt(d_pre[view], upw[view])
+        dmid_norm, grad_gain[view][1] = norm_back(middle, gain[view, 1], dnormed_two)
+        dmiddle = dfinal + dmid_norm
+        d_attn.append(lowered(dmiddle))
+        dmixed = lowered(product_nt(d_attn[view], outw[view]))
+        dquery, dkeys, dvalues = attend_back(query, keys_all, values_all, probs, dmixed)
+        halves.append((dmiddle, dquery, dkeys, dvalues))
+    lower_part = jnp.stack([jnp.stack([half[2][:spatial], half[3][:spatial]]) for half in halves], axis=1)
+    upper_part = jnp.stack([jnp.stack([half[2][-spatial:], half[3][-spatial:]]) for half in halves], axis=1)
+    from_above = from_behind(lower_part.astype(jnp.bfloat16), "tm", -1).astype(lower_part.dtype)
+    from_below = from_behind(upper_part.astype(jnp.bfloat16), "tm", 1).astype(upper_part.dtype)
+    dfused = []
+    d_self = [[], [], []]
+    for view in range(3):
+        dmiddle, dquery, dkeys, dvalues = halves[view]
+        length = dquery.shape[0]
+        own = [dquery]
+        for index, whole in ((0, dkeys), (1, dvalues)):
+            part = whole[spatial : spatial + length]
+            part = part.at[:spatial].add(from_below[index, view]).at[length - spatial :].add(from_above[index, view])
+            own.append(part)
+        own = [lowered(part) for part in own]
+        for index in range(3):
+            d_self[index].append(own[index])
+        dnormed = (
+            product_nt(own[0], qkv[view, 0]) + product_nt(own[1], qkv[view, 1]) + product_nt(own[2], qkv[view, 2])
+        )
+        dfused_norm, grad_gain[view][0] = norm_back(joined[view], gain[view, 0], dnormed)
+        dfused.append(dmiddle + dfused_norm)
+    dviews = list(dfused)
+    d_cross = []
+    d_join = [[], [], []]
+    for view in range(2):
+        first, second, query, keys, values, mixed, probs = cross_keep[view]
+        d_cross.append(lowered(dfused[view]))
+        dmixed = lowered(product_nt(d_cross[view], outw[3 + view]))
+        own = [lowered(part) for part in attend_back(query, keys, values, probs, dmixed)]
+        for index in range(3):
+            d_join[index].append(own[index])
+        dfirst = product_nt(own[0], qkv[3 + view, 0])
+        dsecond = product_nt(own[1], qkv[3 + view, 1]) + product_nt(own[2], qkv[3 + view, 2])
+        dx_first, grad_gain[3 + view][0] = norm_back(views[view], gain[3 + view, 0], dfirst)
+        dx_second, grad_gain[3 + view][1] = norm_back(views[view + 1], gain[3 + view, 1], dsecond)
+        dviews[view] = dviews[view] + dx_first
+        dviews[view + 1] = dviews[view + 1] + dx_second
+    token_grad = jnp.concatenate(dviews, axis=0)[None]
+    gain_total = jnp.stack([jnp.stack(entry) for entry in grad_gain]).reshape(-1, own_gains)
+    gain_total = jnp.pad(gain_total, ((0, 0), (0, 1024 - own_gains))).reshape(*dims, 2, 8, 128)
+    tall = lambda parts: jnp.concatenate(parts, axis=0)
+    kept = lambda index: tall([entry[index] for entry in self_keep])
+    lefts = (
+        kept(9),
+        kept(7),
+        kept(4),
+        kept(0),
+        tall([entry[0] for entry in cross_keep]),
+        tall([entry[1] for entry in cross_keep]),
+        tall([entry[5] for entry in cross_keep]),
+    )
+    rights = (d_out, tall(d_pre), tall(d_attn), *[tall(part) for part in d_self], tall(d_cross), *[tall(part) for part in d_join])
+    shares = reduce_all(dims, slabs, lefts, rights, gain_total)
+    gain_share = shares[4].reshape(-1)[:own_gains]
+    return (layer_out, token_grad, shares[0], shares[1], shares[2], shares[3], gain_share)
+
+
+def fits(mesh, dims):
+    chips = dims[0] * dims[1] * dims[2]
+    rows = (15 * D, 5 * D, 3 * D, 3 * FF)
+    return dims[:2] == (2, 2) and all(r % (chips * ROWS) == 0 for r in rows) and 10 * D // (2 * chips) <= 1024
+
+
 def solution(mesh):
+    seq, tm = mesh.shape["seq"], mesh.shape["tm"]
+    dims = (2, seq // 2, tm // 2)
+    body = functools.partial(per_device, dims) if fits(mesh, dims) else plain_device
     placed = (
         P("seq", "tm", None),
         P("seq", "tm", None),
@@ -336,18 +1056,4 @@
         P(("seq", "tm"), None),
         P(("seq", "tm")),
     )
-    return jax.shard_map(
-        per_device,
-        mesh=mesh,
-        in_specs=placed,
-        out_specs=(
-            P("seq", "tm", None),
-            P("seq", "tm", None),
-            P(("seq", "tm"), None),
-            P(("seq", "tm"), None),
-            P(("seq", "tm"), None),
-            P(("seq", "tm"), None),
-            P(("seq", "tm")),
-        ),
-        check_vma=False,
-    )
+    return jax.shard_map(body, mesh=mesh, in_specs=placed, out_specs=placed, check_vma=False)

time: 1680 us -> 933 us (0.56)
  waiting for transfers between devices: 1120 us -> 0.01 us
  Pallas kernels: 0 us -> 477 us
  blocking collectives: 83.6 us -> 0 us
  local copies, waits for them, and re-layouts: 120 us -> 152 us
  matrix products: 237 us -> 207 us
    reduce_scatter x4 -> x0, waiting for transfers between devices: 847 us -> none  [the longest x1 340 us: per_device(): lax.psum_scatter(totals[0], ('seq', 'tm'), scatter_dimension=0, tiled=True)]
    pallas_call x0 -> x2, Pallas kernels: none -> 477 us  [the longest x1 255 us: reduce_all(): pl.pallas_call(functools.partial(reduce_kernel, dims, slabs, sets, count,...]
    all_gather x4 -> x0, waiting for transfers between devices: 270 us -> none  [the longest x1 96.1 us: per_device(): lax.all_gather(down_weights, ('seq', 'tm'), axis=0, tiled=True)]
    unnamed x2 -> x0, blocking collectives: 83.6 us -> none
    dot_general x26 -> x0, matrix products: 43.1 us -> none  [product_tn(): lax.dot_general(left, right, (((0,), (0,)), ((), ())), preferred_element_...]
    another operation x4 -> x1, other arithmetic: 25.8 us -> 0.6 us  [per_device(): jnp.stack([jnp.stack(entry) for entry in grad_gain]).reshape(-1, own_gains)]
    concatenate x0 -> x16, other arithmetic: none -> 21.4 us  [per_device(): tall = lambda parts: jnp.concatenate(parts, axis=0)]
  transfers between devices with their start and end apart: 12 -> 4, of which waited for: 7 -> 0; matrix products, arithmetic and copies ran while one was open for 16% -> 11% of each run, Pallas kernels for 0% -> 0%
where the time goes in v1:
time: 933 us; the launch traced here: 918 us
  Pallas kernels  477 us (51%)
  matrix products  207 us (22%)
  local copies, waits for them, and re-layouts  152 us (16%)
  other arithmetic  67.5 us (7%)
  starting transfers between devices  10 us (1%)
    pallas_call x1, Pallas kernels, reduce_all(): pl.pallas_call(functools.partial(reduce_kernel, dims, slabs, sets, count,...  255 us
    pallas_call x1, Pallas kernels, gather_all(): pl.pallas_call(functools.partial(gather_kernel, dims), out_shape=[jax.Sha...  223 us
    dot_general x26, matrix products, product(): return jnp.dot(left, right, preferred_element_type=jnp.float32)  75.7 us
    dot_general x26, matrix products, product_nt(): lax.dot_general(left, right, (((1,), (1,)), ((), ())), preferred_element_...  71.4 us
    convert_element_type x28, local copies, waits for them, and re-layouts, lowered(): return value.astype(jnp.bfloat16)  28.8 us
    slice x14, local copies, waits for them, and re-layouts, per_device(): part = whole[spatial:spatial + length]  22.8 us
    unnamed x509, local copies, waits for them, and re-layouts  21.6 us
    concatenate x16, other arithmetic, per_device(): tall = lambda parts: jnp.concatenate(parts, axis=0)  21.4 us
  transfers between devices with their start and end apart: 4, of which 0 were waited for; matrix products, arithmetic and copies ran while one was open for 11% of the time, Pallas kernels for 0%

profile of v1, /device:TPU:0, one launch (start us, length us, event | category | flops | bytes accessed | tf_op | source)
XLA Modules:
  0.0 917.7 jit_solution(3819684295821593247)
XLA Ops:
  7.7 222.6 %shard_map.146 = (bf16[2,2,4,720,768]{4,3,2,1,0:T(8,128)(2,1)}, bf16[2,2,4,240,768]{4,3,2,1,0:T(8,128)(2,1)}, bf16[2,2,4,144,3072]{4,3,2,1,0:T(8,128)(2,1)}, bf1...) custom-call(bf16[360,768]{1,0:T(8,128)(2,1)S(1)} %copy-done, bf16[120,768]{1,0:T(8,128)(2,1)S(1)} %copy-done.3, ...), custom_call_target="tpu_custom_call" | custom-call | tf_op jit(solution)/shard_map/pallas_call | solution.py:351
  243.8 2.4 convolution_convert_fusion.16
  246.1 2.3 convolution_convert_fusion.15
  249.4 2.2 convolution_convert_fusion.7
  267.5 3.6 collective-permute-start
  272.3 2.5 convolution_convert_fusion.3
  277.7 2.4 convolution_convert_fusion.14
  283.4 2.3 convolution_convert_fusion.22
  288.8 2.4 convert_element_type.440
  296.8 2.3 convert_bitcast_fusion.refs_7_
  299.1 2.0 fusion.184
  302.8 1.9 fusion.185
  309.9 5.3 fusion.198
  315.2 3.5 convolution_convert_fusion.2
  318.8 2.0 fusion.199
  321.3 11.0 %multiply_convert_fusion.1 = (bf16[256,3072]{1,0:T(8,128)(2,1)}, f32[256,3072]{1,0:T(8,128)S(1)}, f32[256,3072]{1,0:T(8,128)S(1)}) fusion(bf16[256,768]{1,0:T(8,128)(2,1)S(1)} %multiply_convert_fusion.8, bf16[3,768,3072]{2,1,0:T(8,128)(2,1)} %bitcast.781), kind=kOutput, calls=%fused_computation.34 | convolution fusion | flops 1259077632 | bytes 12976128 | tf_op jit(solution)/shard_map/dot_general | solution.py:71
  332.3 2.3 add_convert_fusion
  334.6 5.1 multiply_reduce_fusion.4
  342.9 2.5 convolution_convert_fusion.1
  347.3 4.5 multiply_reduce_fusion
  365.2 3.7 fusion.196
  368.9 2.3 convolution_convert_fusion.13
  374.0 7.3 multiply_convert_fusion.4
  381.4 2.8 add_convert_fusion.1
  384.3 5.0 multiply_reduce_fusion.15
  392.0 2.5 convolution_convert_fusion.11
  396.3 2.7 multiply_reduce_fusion.2
  410.9 2.5 fusion.194
  413.4 3.9 convolution_convert_fusion.12
  419.5 5.5 multiply_convert_fusion.7
  425.0 4.9 add_convert_fusion.2
  430.0 4.6 multiply_reduce_fusion.26
  437.2 2.4 convolution_convert_fusion.21
  441.4 4.0 fusion.200
  445.4 2.1 multiply_reduce_fusion.8
  450.7 2.9 fusion.66
  455.5 2.7 fusion.67
  459.9 2.1 pad_maximum_fusion.6.refs_9_
  462.0 3.1 pad_maximum_fusion.1.refs_8_
  465.1 1.9 copy.168
  470.5 2.2 pad_maximum_fusion.3.refs_1_
  496.4 3.9 collective-permute-start.2
  517.3 5.2 fusion.45
  522.4 4.0 fusion.50
  526.4 4.0 fusion.59
  542.8 2.3 copy.151
  546.9 1.9 copy.155
  550.6 1.9 copy.157
  567.3 2.7 maximum_bitcast_fusion
  577.8 1.9 convolution_add_fusion.1
  579.8 2.6 multiply_reduce_fusion.5
  583.8 2.7 convolution_convert_fusion
  587.7 2.0 multiply_reduce_fusion.1
  596.5 2.0 multiply_reduce_fusion.16
  599.4 2.0 convolution_convert_fusion.9
  605.0 2.5 fusion.61
  608.4 2.5 fusion.62
  611.7 3.4 multiply_reduce_fusion.3
  620.7 2.0 fusion.64
  622.8 2.7 fusion.65
  628.2 1.9 multiply_reduce_fusion.29
  633.2 2.1 multiply_reduce_fusion.19
  643.4 2.1 pad_maximum_fusion.9.refs_12_
  653.9 254.9 %shard_map.147 = (f32[360,768]{1,0:T(8,128)}, f32[120,768]{1,0:T(8,128)}, f32[72,3072]{1,0:T(8,128)}, f32[288,768]{1,0:T(8,128)}, f32[8,128]{1,0:T(8,128)}, /*in...) custom-call(bf16[448,3072]{1,0:T(8,128)(2,1)} %pad_maximum_fusion.re, ...), custom_call_target="tpu_custom_call" | custom-call | tf_op jit(solution)/shard_map/pallas_call | solution.py:650
  (770 shorter events, 244.2 us)
Async XLA Ops:
  7.7 222.9 %copy-start.4 = (f32[1,448,768]{2,1,0:T(8,128)S(1)}, f32[1,448,768]{2,1,0:T(8,128)}, u32[]{:S(2)}) copy-start(f32[1,448,768]{2,1,0:T(8,128)} %param.39) | copy-start | bytes 4128772
  230.5 5.6 copy-start.153
  230.5 7.5 copy-start.147
  230.5 13.1 %copy-start.155 = (f32[768]{0:T(1024)}, f32[768]{0:T(1024)S(1)}, u32[]{:S(2)}) copy-start(f32[768]{0:T(1024)S(1)} %get-tuple-element.235) | copy-start | bytes 9220
  230.5 18.4 %copy-start.166 = (f32[768]{0:T(1024)}, f32[768]{0:T(1024)S(1)}, u32[]{:S(2)}) copy-start(f32[768]{0:T(1024)S(1)} %get-tuple-element.239) | copy-start | bytes 9220
  230.5 27.2 %copy-start.157 = (f32[768]{0:T(1024)}, f32[768]{0:T(1024)S(1)}, u32[]{:S(2)}) copy-start(f32[768]{0:T(1024)S(1)} %get-tuple-element.238) | copy-start | bytes 9220
  230.5 52.9 %copy-start.151 = (f32[768]{0:T(1024)}, f32[768]{0:T(1024)S(1)}, u32[]{:S(2)}) copy-start(f32[768]{0:T(1024)S(1)} %get-tuple-element.234) | copy-start | bytes 9220
  230.6 7.4 copy-start.194
  230.8 7.2 copy-start.227
  243.4 5.0 copy-start.197
  243.6 4.8 copy-start.235
  258.2 14.1 %copy-start.63 = (bf16[256,768]{1,0:T(8,128)(2,1)}, bf16[256,768]{1,0:T(8,128)(2,1)S(1)}, u32[]{:S(2)}) copy-start(bf16[256,768]{1,0:T(8,128)(2,1)S(1)} %multiply_convert_fusion.9) | copy-start | bytes 1179652
  260.2 6.0 copy-start.68
  267.5 31.7 %collective-permute-start = (bf16[2,3,64,768]{3,2,0,1:T(8,128)(2,1)}, bf16[2,3,64,768]{3,2,0,1:T(8,128)(2,1)}, u32[]{:S(2)}, u32[]{:S(2)}) collective-permute-start(bf16[2,3,64,768]{3,2,0,1:T(8,128)(2,1)} %get-tuple-element.281), channel_id=1, source_target_pairs={{0,1},{1,2},{2,3},{3,4},{4,5},{5,6},{6,7},{8,9},{9,10},{10,11},{11... | collective-permute-start | bytes 1769480 | tf_op jit(solution)/shard_map/ppermute | solution.py:34
  271.0 31.8 %collective-permute-start.1 = (bf16[2,3,64,768]{3,2,0,1:T(8,128)(2,1)}, bf16[2,3,64,768]{3,2,0,1:T(8,128)(2,1)}, u32[]{:S(2)}, u32[]{:S(2)}) collective-permute-start(bf16[2,3,64,768]{3,2,0,1:T(8,128)(2,1)} %get-tuple-element.282), channel_id=1, source_target_pairs={{1,0},{2,1},{3,2},{4,3},{5,4},{6,5},{7,6},{9,8},{10,9},{11,10},{12... | collective-permute-start | bytes 1769480 | tf_op jit(solution)/shard_map/ppermute | solution.py:36
  288.8 21.1 %copy-start.47 = (bf16[256,768]{0,1:T(8,128)(2,1)}, bf16[256,768]{0,1:T(8,128)(2,1)S(1)}, u32[]{:S(2)}) copy-start(bf16[256,768]{0,1:T(8,128)(2,1)S(1)} %copy.112) | copy-start | bytes 1179652
  293.1 120.3 %copy-start.82 = (bf16[64,768]{0,1:T(8,128)(2,1)}, bf16[64,768]{0,1:T(8,128)(2,1)S(1)}, u32[]{:S(2)}) copy-start(bf16[64,768]{0,1:T(8,128)(2,1)S(1)} %copy.223) | copy-start | bytes 294916
  299.1 10.8 %copy-start.116 = (bf16[256,768]{0,1:T(8,128)(2,1)S(1)}, bf16[256,768]{0,1:T(8,128)(2,1)}, u32[]{:S(2)}) copy-start(bf16[256,768]{0,1:T(8,128)(2,1)} %copy.113) | copy-start | bytes 1179652
  299.1 10.8 %copy-start.224 = (f32[384]{0:T(512)S(1)}, f32[384]{0:T(512)}, u32[]{:S(2)}) copy-start(f32[384]{0:T(512)} %pad_maximum_fusion.35) | copy-start | bytes 4612
  320.8 11.5 %slice-start.2 = ((s8[14155776]{0:T(1024)(128)(4,1)}), s8[4194304]{0:T(1024)(128)(4,1)S(1)}, s32[]{:S(2)}) async-start(s8[14155776]{0:T(1024)(128)(4,1)} %bitcast.775), calls=%async_computation.2 | async-start | bytes 8388608
  321.2 11.0 %copy-start.66 = (bf16[256,768]{1,0:T(8,128)(2,1)}, bf16[256,768]{1,0:T(8,128)(2,1)S(1)}, u32[]{:S(2)}) copy-start(bf16[256,768]{1,0:T(8,128)(2,1)S(1)} %multiply_convert_fusion.8) | copy-start | bytes 1179652
  321.2 11.0 %copy-start.115 = (bf16[1,448,768]{2,1,0:T(8,128)(2,1)S(1)}, bf16[1,448,768]{2,1,0:T(8,128)(2,1)}, u32[]{:S(2)}) copy-start(bf16[1,448,768]{2,1,0:T(8,128)(2,1)} %convert_element_type.440) | copy-start | bytes 2064388
  321.2 11.0 %slice-start.3 = ((s8[14155776]{0:T(1024)(128)(4,1)}), s8[4194304]{0:T(1024)(128)(4,1)S(1)}, s32[]{:S(2)}) async-start(s8[14155776]{0:T(1024)(128)(4,1)} %bitcast.775), calls=%async_computation.3 | async-start | bytes 8388608
  321.3 11.0 %slice-start.4 = ((s8[14155776]{0:T(1024)(128)(4,1)}), s8[4194304]{0:T(1024)(128)(4,1)S(1)}, s32[]{:S(2)}) async-start(s8[14155776]{0:T(1024)(128)(4,1)} %bitcast.775), calls=%async_computation.4 | async-start | bytes 8388608
  321.3 11.0 %slice-start.5 = ((s8[14155776]{0:T(1024)(128)(4,1)}), s8[1572864]{0:T(1024)(128)(4,1)S(1)}, s32[]{:S(2)}) async-start(s8[14155776]{0:T(1024)(128)(4,1)} %bitcast.775), calls=%async_computation.5 | async-start | bytes 3145728
  334.6 5.1 copy-start.61
  356.5 8.7 copy-start.234
  368.9 12.4 %slice-start.6 = ((s8[14155776]{0:T(1024)(128)(4,1)}), s8[4194304]{0:T(1024)(128)(4,1)S(1)}, s32[]{:S(2)}) async-start(s8[14155776]{0:T(1024)(128)(4,1)} %bitcast.778), calls=%async_computation.6 | async-start | bytes 8388608
  373.6 15.6 %copy-start.11 = (f32[128,768]{1,0:T(8,128)}, f32[128,768]{1,0:T(8,128)S(1)}, u32[]{:S(2)}) copy-start(f32[128,768]{1,0:T(8,128)S(1)} %get-tuple-element.324) | copy-start | bytes 1179652
  374.0 7.4 copy-start.102
  374.0 7.4 slice-start.7
  374.0 7.4 slice-start.8
  374.0 7.4 slice-start.9
  384.3 5.0 copy-start.106
  389.5 6.8 copy-start.189
  402.9 8.0 copy-start.233
  419.5 5.6 copy-start.125
  434.9 10.5 %copy-start.216 = (f32[64]{0:T(128)}, f32[64]{0:T(128)S(1)}, u32[]{:S(2)}) copy-start(f32[64]{0:T(128)S(1)} %negate_multiply_fusion.11) | copy-start | bytes 772
  496.4 75.5 %collective-permute-start.2 = (bf16[2,3,64,768]{3,2,1,0:T(8,128)(2,1)}, bf16[2,3,64,768]{3,2,1,0:T(8,128)(2,1)}, u32[]{:S(2)}, u32[]{:S(2)}) collective-permute-start(bf16[2,3,64,768]{3,2,1,0:T(8,128)(2,1)} %pad_maximum_fusion.12), channel_id=1, source_target_pairs={{0,1},{1,2},{2,3},{3,4},{4,5},{5,6},{6,7},{8,9},{9,10},{10,11},{11... | collective-permute-start | bytes 1769480 | tf_op jit(solution)/shard_map/ppermute | solution.py:46
  514.3 59.0 %collective-permute-start.3 = (bf16[2,3,64,768]{3,2,1,0:T(8,128)(2,1)}, bf16[2,3,64,768]{3,2,1,0:T(8,128)(2,1)}, u32[]{:S(2)}, u32[]{:S(2)}) collective-permute-start(bf16[2,3,64,768]{3,2,1,0:T(8,128)(2,1)} %pad_maximum_fusion.13), channel_id=1, source_target_pairs={{1,0},{2,1},{3,2},{4,3},{5,4},{6,5},{7,6},{9,8},{10,9},{11,10},{12... | collective-permute-start | bytes 1769480 | tf_op jit(solution)/shard_map/ppermute | solution.py:46
  517.3 5.2 copy-start.12
  517.3 5.2 copy-start.104
  526.4 5.0 copy-start.56
  526.4 5.0 copy-start.99
  526.4 5.0 copy-start.124
  552.6 9.3 %copy-start.208 = (f32[768]{0:T(1024)S(1)}, f32[768]{0:T(1024)}, u32[]{:S(2)}) copy-start(f32[768]{0:T(1024)} %get-tuple-element.215) | copy-start | bytes 9220
  552.6 9.9 %copy-start.209 = (f32[768]{0:T(1024)S(1)}, f32[768]{0:T(1024)}, u32[]{:S(2)}) copy-start(f32[768]{0:T(1024)} %get-tuple-element.227) | copy-start | bytes 9220
  556.3 10.4 %copy-start.210 = (f32[768]{0:T(1024)S(1)}, f32[768]{0:T(1024)}, u32[]{:S(2)}) copy-start(f32[768]{0:T(1024)} %get-tuple-element.229) | copy-start | bytes 9220
  622.7 5.3 copy-start.81
  622.8 5.3 copy-start.152
  622.8 5.3 copy-start.154
  628.2 4.9 copy-start.148
  628.2 4.9 copy-start.150
  630.1 5.1 copy-start.38
  630.2 5.1 copy-start.199
  630.2 5.0 copy-start.218
  633.1 5.2 copy-start.175
  633.1 5.2 copy-start.179
  635.2 10.2 %copy-start.21 = (f32[128,768]{1,0:T(8,128)}, f32[128,768]{1,0:T(8,128)S(1)}, u32[]{:S(2)}) copy-start(f32[128,768]{1,0:T(8,128)S(1)} %get-tuple-element.359) | copy-start | bytes 1179652
  635.3 10.1 %copy-start.16 = (bf16[256,768]{1,0:T(8,128)(2,1)S(1)}, bf16[256,768]{1,0:T(8,128)(2,1)}, u32[]{:S(2)}) copy-start(bf16[256,768]{1,0:T(8,128)(2,1)} %copy-done.15) | copy-start | bytes 1179652
  653.8 256.2 %copy-start.238 = (f32[128]{0:T(128)S(1)}, f32[128]{0:T(128)}, u32[]{:S(2)}) copy-start(f32[128]{0:T(128)} %get-tuple-element.206) | copy-start | bytes 1540
  653.9 256.2 %copy-start.237 = (f32[128]{0:T(128)S(1)}, f32[128]{0:T(128)}, u32[]{:S(2)}) copy-start(f32[128]{0:T(128)} %get-tuple-element.217) | copy-start | bytes 1540
  653.9 256.2 %copy-start.8 = (f32[256,768]{1,0:T(8,128)S(1)}, f32[256,768]{1,0:T(8,128)}, u32[]{:S(2)}) copy-start(f32[256,768]{1,0:T(8,128)} %copy-done.7) | copy-start | bytes 2359300
  653.9 256.2 %copy-start.181 = (f32[256]{0:T(256)S(1)}, f32[256]{0:T(256)}, u32[]{:S(2)}) copy-start(f32[256]{0:T(256)} %copy-done.180) | copy-start | bytes 3076
  (191 other events, 505.8 us)

commit v2 on v1

--- a/solution.py
+++ b/solution.py
@@ -135,6 +135,7 @@
         t = lax.axis_index("tm")
         self.at = (s // dims[1], s % dims[1], t // 2)
         self.core = t % 2
+        self.slab = t
 
     def device(self, at, core):
         return (at[0] * self.dims[1] + at[1], at[2] * 2 + core)
@@ -162,6 +163,15 @@
                 pl.semaphore_signal(barrier, inc=1, device_id=place.along(dim, me + step), device_id_type=MESH)
 
             count = count + jnp.where(ok, 1, 0)
+    step = 2 * place.core - 1
+    ok = (place.at[2] + step >= 0) & (place.at[2] + step < place.dims[2])
+
+    @pl.when(ok)
+    def _():
+        beside = (place.at[0], place.at[1], place.at[2] + step)
+        pl.semaphore_signal(barrier, inc=1, device_id=place.device(beside, 1 - place.core), device_id_type=MESH)
+
+    count = count + jnp.where(ok, 1, 0)
     pl.semaphore_wait(barrier, count)
 
 
@@ -256,7 +266,7 @@
     return [flat[i : i + 3] for i in range(0, len(flat), 3)]
 
 
-def march(sets, begin, extra=(), between=None):
+def march(sets, begin, extra=()):
     waiting = list(sets)
     active = list(extra)
     step = 0
@@ -267,25 +277,328 @@
         still = []
         for one in active:
             try:
-                next(one)
+                yield next(one)
                 still.append(one)
             except StopIteration:
                 pass
         active = still
-        if between is not None:
-            between(step)
         step += 1
 
 
-def gather_kernel(dims, qkv, out, up, down, gain, fqkv, fout, fup, fdown, fgain, *scratch):
+def weave(comm, work, each):
+    live = [True, True]
+    gate = [None, None]
+    sources = (comm, work)
+
+    def advance(k):
+        if not live[k]:
+            return None
+        if gate[k] is not None:
+            if not gate[k]():
+                return None
+            gate[k] = None
+        try:
+            item = next(sources[k])
+        except StopIteration:
+            live[k] = False
+            return None
+        if callable(item):
+            gate[k] = item
+            return 0.0
+        return item or 0.0
+
+    credit = 0.0
+    while live[0] or live[1]:
+        moved = advance(0)
+        if moved is not None:
+            credit = min(credit + each, 4.0)
+        stuck = moved is None
+        while live[1] and (credit > 0 or stuck):
+            cost = advance(1)
+            if cost is None:
+                break
+            credit = max(credit - cost, -8.0)
+            if stuck and live[0] and (gate[0] is None or gate[0]()):
+                break
+
+
+def matmul(left, right):
+    return jnp.dot(left, right, preferred_element_type=F32)
+
+
+def matmul_nt(left, right):
+    return lax.dot_general(left, right, (((1,), (1,)), ((), ())), preferred_element_type=F32)
+
+
+def matmul_tn(left, right):
+    return lax.dot_general(left, right, (((0,), (0,)), ((), ())), preferred_element_type=F32)
+
+
+def halves_of(pair):
+    low = lax.broadcasted_iota(jnp.int32, pair.shape, 1) < pair.shape[1] // 2
+    zero = jnp.zeros_like(pair)
+    return jnp.where(low, pair, zero), jnp.where(low, zero, pair)
+
+
+def softmax_rows(scores):
+    expo = jnp.exp(scores - jnp.max(scores, axis=-1, keepdims=True))
+    return expo * (1.0 / jnp.sum(expo, axis=-1, keepdims=True))
+
+
+def attend_pair(query, keys, values, bias):
+    outs = []
+    for part in halves_of(query):
+        scores = matmul_nt(part, keys) * 0.125
+        if bias is not None:
+            scores = scores + bias
+        outs.append(matmul(softmax_rows(scores).astype(BF), values))
+    low = lax.broadcasted_iota(jnp.int32, outs[0].shape, 1) < outs[0].shape[1] // 2
+    return jnp.where(low, outs[0], outs[1]).astype(BF)
+
+
+def gain_table(tiles, own):
+    rows = tiles.shape[0]
+    filled = own // 48
+    r = lax.broadcasted_iota(jnp.int32, (rows, D), 0)
+    c = lax.broadcasted_iota(jnp.int32, (rows, D), 1)
+    spread = (lax.broadcasted_iota(jnp.int32, (128, D), 0) == lax.broadcasted_iota(jnp.int32, (128, D), 1) % 48)
+    wide = matmul(tiles.astype(BF), spread.astype(BF))
+    flat = (r // 8) * filled + r % 8
+    wide = jnp.where((r % 8 < filled) & (c // 48 == flat % 16), wide, 0.0).astype(BF)
+    rr = lax.broadcasted_iota(jnp.int32, (16, rows), 1)
+    vv = lax.broadcasted_iota(jnp.int32, (16, rows), 0)
+    pick = (rr % 8 < filled) & (((rr // 8) * filled + rr % 8) // 16 == vv)
+    return matmul(pick.astype(BF), wide)
+
+
+class Weights:
+    def __init__(self, dims, slabs, wholes, ring, sems, blocks):
+        self.dims, self.slabs, self.wholes, self.ring, self.sems, self.blocks = dims, slabs, wholes, ring, sems, blocks
+        self.depth = ring.shape[0]
+        self.loading = {}
+        self.next_load = 0
+        self.next_use = 0
+        self.ready = set()
+
+    def fetch(self):
+        while self.next_load < min(len(self.blocks), self.next_use + self.depth):
+            i = self.next_load
+            a, row, block = self.blocks[i]
+            if a not in self.ready:
+                return
+            slot = i % self.depth
+            copies = []
+            at, end = row, row + D
+            slab = self.slabs[a][0]
+            while at < end:
+                chip, off = at // slab, at % slab
+                n = min(end - at, slab - off)
+                p, q, z = chip // (self.dims[1] * self.dims[2]), chip // self.dims[2] % self.dims[1], chip % self.dims[2]
+                copies.append(
+                    pltpu.make_async_copy(
+                        self.wholes[a].at[p, q, z, pl.ds(off, n), pl.ds(block * D, D)],
+                        self.ring.at[slot, pl.ds(at - row, n)],
+                        self.sems.at[slot, len(copies)],
+                    )
+                )
+                at += n
+            for one in copies:
+                one.start()
+            self.loading[i] = copies
+            self.next_load += 1
+
+    def take(self, expected):
+        i = self.next_use
+        assert self.blocks[i] == expected, (self.blocks[i], expected)
+        self.fetch()
+        for one in self.loading.pop(i):
+            one.wait()
+        return self.ring.at[i % self.depth]
+
+    def give_back(self):
+        self.next_use += 1
+        self.fetch()
+
+
+def forward_blocks():
+    blocks = [(0, (9 + i) * D, 0) for i in range(6)]
+    blocks += [(1, 3 * D, 0), (1, 4 * D, 0)]
+    blocks += [(0, i * D, 0) for i in range(9)]
+    blocks += [(1, i * D, 0) for i in range(3)]
+    blocks += [(2, v * D, j) for v in range(3) for j in range(FF // D)]
+    blocks += [(3, v * FF + j * D, 0) for v in range(3) for j in range(FF // D)]
+    return blocks
+
+
+KEPT = ("first", "second", "cq", "ck", "cv", "cmixed", "joined", "normed", "q", "kx", "vx", "mixed", "middle", "normed_two", "hidden", "active")
+
+
+def forward_shapes(rows):
+    u = rows // 7
+    sizes = dict(
+        first=(6 * u, D), second=(3 * u, D), cq=(6 * u, D), ck=(3 * u, D), cv=(3 * u, D), cmixed=(6 * u, D),
+        joined=(rows, D), normed=(rows, D), q=(rows, D), kx=(rows + 6 * u, D), vx=(rows + 6 * u, D),
+        mixed=(rows, D), middle=(rows, D), normed_two=(rows, D), hidden=(rows, FF), active=(rows, FF),
+    )
+    return {k: (sizes[k], F32 if k in ("joined", "middle", "hidden") else BF) for k in KEPT}
+
+
+def halo_device(place, count, step):
+    t = jnp.clip(place.slab + step, 0, count - 1)
+    return (place.at[0] * place.dims[1] + place.at[1], t)
+
+
+def slab_bias(place, count, width, spatial):
+    col = lax.broadcasted_iota(jnp.int32, (1, width), 1)
+    below = (col < spatial) & (place.slab == 0)
+    above = (col >= width - spatial) & (place.slab == count - 1)
+    return jnp.where(below | above, FAR, 0.0).astype(F32)
+
+
+def forward_work(place, copies, weights, need, gain, x, layer, v, save):
+    u = x.shape[0] // 7
+    count = 2 * place.dims[2]
+    spans = ((0, 4 * u), (4 * u, 2 * u), (6 * u, u))
+    bases = (0, 6 * u, 10 * u)
+    yield need("gain")
+    for c in range(2):
+        r0, n = spans[c]
+        k0, m = spans[c + 1]
+        rows, keys = pl.ds(r0, n), pl.ds(k0 - 4 * u, m)
+        g = lambda j: gain[pl.ds(2 * (3 + c) + j, 1), :]
+        v["first"][rows] = norm_rows(x[rows], g(0)).astype(BF)
+        v["second"][keys] = norm_rows(x[pl.ds(k0, m)], g(1)).astype(BF)
+        yield 0.5
+    save("first")
+    save("second")
+    yield need(0)
+    for c in range(2):
+        r0, n = spans[c]
+        k0, m = spans[c + 1]
+        rows, keys = pl.ds(r0, n), pl.ds(k0 - 4 * u, m)
+        for j, (src, dst, part) in enumerate((("first", "cq", rows), ("second", "ck", keys), ("second", "cv", keys))):
+            w = weights.take((0, (9 + 3 * c + j) * D, 0))
+            v[dst][part] = matmul(v[src][part], w[...]).astype(BF)
+            weights.give_back()
+            yield 0.8
+        for h in range(HEADS // 2):
+            cols = pl.ds(h * 128, 128)
+            v["cmixed"][rows, cols] = attend_pair(v["cq"][rows, cols], v["ck"][keys, cols], v["cv"][keys, cols], None)
+            yield 0.8 if c == 0 else 0.3
+    for name in ("cq", "ck", "cv", "cmixed"):
+        save(name)
+    yield need(1)
+    for c in range(2):
+        rows = pl.ds(*spans[c])
+        w = weights.take((1, (3 + c) * D, 0))
+        v["joined"][rows] = x[rows] + matmul(v["cmixed"][rows], w[...])
+        weights.give_back()
+        yield 0.8
+    v["joined"][pl.ds(*spans[2])] = x[pl.ds(*spans[2])]
+    save("joined")
+    for name in ("kx", "vx"):
+        for view in range(3):
+            base, n = bases[view], spans[view][1]
+
+            @pl.when(place.slab == 0)
+            def _():
+                v[name][pl.ds(base, u)] = jnp.zeros((u, D), BF)
+
+            @pl.when(place.slab == count - 1)
+            def _():
+                v[name][pl.ds(base + u + n, u)] = jnp.zeros((u, D), BF)
+
+    halo = {0: [], 1: [], 2: []}
+    for view in range(3):
+        r0, n = spans[view]
+        rows = pl.ds(r0, n)
+        base = bases[view]
+        v["normed"][rows] = norm_rows(v["joined"][rows], gain[pl.ds(2 * view, 1), :]).astype(BF)
+        for j, (dst, part) in enumerate((("q", rows), ("kx", pl.ds(base + u, n)), ("vx", pl.ds(base + u, n)))):
+            w = weights.take((0, (3 * view + j) * D, 0))
+            v[dst][part] = matmul(v["normed"][rows], w[...]).astype(BF)
+            weights.give_back()
+            if j > 0:
+                ref = v[dst]
+                up, down = place.slab < count - 1, place.slab > 0
+                halo[view].append(
+                    (copies.start(ref.at[pl.ds(base + n, u)], ref.at[pl.ds(base, u)], halo_device(place, count, 1), up), down)
+                )
+                halo[view].append(
+                    (
+                        copies.start(
+                            ref.at[pl.ds(base + u, u)], ref.at[pl.ds(base + u + n, u)], halo_device(place, count, -1), down
+                        ),
+                        up,
+                    )
+                )
+            yield 0.8
+    save("normed")
+    save("q")
+    for view in range(3):
+        r0, n = spans[view]
+        rows, keys = pl.ds(r0, n), pl.ds(bases[view], n + 2 * u)
+        for one, ok in halo[view]:
+            when(ok, one.wait_recv)
+        bias = slab_bias(place, count, n + 2 * u, u)
+        for h in range(HEADS // 2):
+            cols = pl.ds(h * 128, 128)
+            v["mixed"][rows, cols] = attend_pair(v["q"][rows, cols], v["kx"][keys, cols], v["vx"][keys, cols], bias)
+            yield (1.4, 0.6, 0.3)[view]
+        w = weights_later = None
+    save("kx")
+    save("vx")
+    save("mixed")
+    for view in range(3):
+        rows = pl.ds(*spans[view])
+        w = weights.take((1, view * D, 0))
+        v["middle"][rows] = v["joined"][rows] + matmul(v["mixed"][rows], w[...])
+        weights.give_back()
+        v["normed_two"][rows] = norm_rows(v["middle"][rows], gain[pl.ds(2 * view + 1, 1), :]).astype(BF)
+        yield 1.0
+    save("middle")
+    save("normed_two")
+    yield need(2)
+    for view in range(3):
+        rows = pl.ds(*spans[view])
+        for j in range(FF // D):
+            cols = pl.ds(j * D, D)
+            w = weights.take((2, view * D, j))
+            pre = matmul(v["normed_two"][rows], w[...])
+            weights.give_back()
+            v["hidden"][rows, cols] = pre
+            v["active"][rows, cols] = (0.5 * pre * (1.0 + lax.erf(pre * (0.5**0.5)))).astype(BF)
+            yield 1.2
+    save("hidden")
+    save("active")
+    yield need(3)
+    for view in range(3):
+        rows = pl.ds(*spans[view])
+        for j in range(FF // D):
+            w = weights.take((3, view * FF + j * D, 0))
+            term = matmul(v["active"][rows, pl.ds(j * D, D)], w[...])
+            weights.give_back()
+            layer[rows] = (v["middle"][rows] if j == 0 else layer[rows]) + term
+            yield 0.8
+    save("layer")
+
+
+def gather_kernel(dims, own_gains, *refs):
+    refs = list(refs)
+    take = lambda n: [refs.pop(0) for _ in range(n)]
+    shards = take(4)
+    gain_tile, x = take(2)
+    fulls = take(4)
+    gain_out, layer_out = take(2)
+    kept_out = dict(zip(KEPT, take(len(KEPT))))
+    theirs, merged = take(4), take(4)
+    gain_all, gain, layer = take(3)
+    v = dict(zip(KEPT, take(len(KEPT))))
+    ring, send, recv, local, ring_sem, save_sem = take(6)
     place = Place(dims)
-    shards = (qkv, out, up, down)
-    fulls = (fqkv, fout, fup, fdown)
-    theirs = scratch[:4]
-    merged = scratch[4:8]
-    gain_pair, send, recv, local = scratch[8:]
     copies = Copies(send, recv)
     core = place.core
+    at = place.at
     meet(place)
     width = [s.shape[1] // 2 for s in shards]
     mine = [pl.ds(pl.multiple_of(core * w, 128), w) for w in width]
@@ -293,10 +606,15 @@
     swaps = []
     for a in range(4):
         swaps.append(copies.start(shards[a].at[:, other[a]], theirs[a], place.sibling()))
-    gain_pair[core] = gain[...]
-    part = gain_pair.at[core]
-    swap_gain = copies.start(part, part, place.sibling())
-    at = place.at
+    own_tile = gain_all.at[at[0], at[1], at[2], core]
+    own_tile[...] = gain_tile[...]
+    swap_gain = copies.start(own_tile, own_tile, place.sibling())
+    slabs = [(m.shape[0], 2 * m.shape[1]) for m in merged]
+    sets = pieces_of(slabs, range(4))
+    left = {a: sum(1 for s in sets for piece in s if piece[0] == a) for a in range(4)}
+    pair = {a: [] for a in range(4)}
+    ready = set()
+    state = {"gain": False}
 
     def prepare(a):
         swaps[a].wait_recv()
@@ -310,62 +628,93 @@
         copy.start()
         copy.wait()
 
-    pair = []
-    ready = set()
-
     def begin(piece):
         a, row, block, order = piece
         if a not in ready:
             prepare(a)
             ready.add(a)
         cols = pl.ds(pl.multiple_of(core * width[a] + block * BLOCK, 128), BLOCK)
-        return gather_piece(copies, place, fulls[a], (row, ROWS), cols, order, pair)
+        yield from gather_piece(copies, place, fulls[a], (row, ROWS), cols, order, pair[a])
+        left[a] -= 1
 
     def gains():
         swap_gain.wait_recv()
-        copy = pltpu.make_async_copy(gain_pair, fgain.at[at[0], at[1], at[2]], local.at[4])
-        copy.start()
-        copy.wait()
         done = set()
         for dim in ZXY:
 
             def pick(value):
                 index = [slice(None) if d in done else at[d] for d in range(3)]
                 index[dim] = value
-                return fgain.at[tuple(index)]
+                return gain_all.at[tuple(index)]
 
             yield from gather_line(copies, place, dim, pick)
             done.add(dim)
-
-    march(pieces_of([m.shape[:1] + (2 * m.shape[1],) for m in merged], range(4)), begin, (gains(),))
-    for copy in pair:
-        copy.wait_recv()
+        gain[...] = gain_table(gain_all[...].reshape(-1, 128), own_gains)
+        copy = pltpu.make_async_copy(gain, gain_out, local.at[4])
+        copy.start()
+        copy.wait()
+        state["gain"] = True
+
+    weights = Weights(dims, slabs, fulls, ring, ring_sem, forward_blocks())
+
+    def need(what):
+        def gate():
+            if what == "gain":
+                return state["gain"]
+            if left[what]:
+                return False
+            if what not in weights.ready:
+                for copy in pair[what]:
+                    copy.wait_recv()
+                weights.ready.add(what)
+                weights.fetch()
+            return True
+
+        return gate
+
+    saves = []
+
+    def save(name):
+        src, dst = (layer, layer_out) if name == "layer" else (v[name], kept_out[name])
+        copy = pltpu.make_async_copy(src, dst, save_sem.at[len(saves)])
+        copy.start()
+        saves.append(copy)
+
+    work = forward_work(place, copies, weights, need, gain, x, layer, v, save)
+    weave(march(sets, begin, (gains(),)), work, 0.8)
+    for copy in saves:
+        copy.wait()
     copies.drain()
 
 
-def gather_all(dims, qkv, out, up, down, gain):
-    shards = (qkv, out, up, down)
+def gather_all(dims, own_gains, shards, tile, x):
     slabs = [(2 * s.shape[0], s.shape[1]) for s in shards]
     anywhere = pl.BlockSpec(memory_space=pl.ANY)
     vmem = pl.BlockSpec(memory_space=pltpu.VMEM)
-    return pl.pallas_call(
-        functools.partial(gather_kernel, dims),
+    kept = forward_shapes(x.shape[0])
+    segments = max(D // s[0] + 2 for s in slabs)
+    outs = pl.pallas_call(
+        functools.partial(gather_kernel, dims, own_gains),
         out_shape=[jax.ShapeDtypeStruct((*dims, *s), BF) for s in slabs]
-        + [jax.ShapeDtypeStruct((*dims, 2, 8, 128), F32)],
-        in_specs=[vmem] * 5,
-        out_specs=[anywhere] * 5,
+        + [jax.ShapeDtypeStruct((16, D), F32), jax.ShapeDtypeStruct(x.shape, F32)]
+        + [jax.ShapeDtypeStruct(*kept[k]) for k in KEPT],
+        in_specs=[vmem] * 6,
+        out_specs=[anywhere] * (6 + len(KEPT)),
         scratch_shapes=[pltpu.VMEM((r // 2, w // 2), BF) for r, w in slabs]
         + [pltpu.VMEM((r, w // 2), BF) for r, w in slabs]
+        + [pltpu.VMEM((*dims, 2, 8, 128), F32), pltpu.VMEM((16, D), F32), pltpu.VMEM(x.shape, F32)]
+        + [pltpu.VMEM(*kept[k]) for k in KEPT]
         + [
-            pltpu.VMEM((2, 8, 128), F32),
+            pltpu.VMEM((4, D, D), BF),
             pltpu.SemaphoreType.DMA((COPIES,)),
             pltpu.SemaphoreType.DMA((COPIES,)),
             pltpu.SemaphoreType.DMA((5,)),
+            pltpu.SemaphoreType.DMA((4, segments)),
+            pltpu.SemaphoreType.DMA((1 + len(KEPT),)),
         ],
-        compiler_params=pltpu.CompilerParams(
-            collective_id=0, has_side_effects=True, vmem_limit_bytes=48 << 20
-        ),
-    )(qkv, out, up, down, gain)
+        compiler_params=pltpu.CompilerParams(collective_id=0, has_side_effects=True, vmem_limit_bytes=60 << 20),
+    )(*shards, tile, x)
+    return outs[:4], outs[4], outs[5], dict(zip(KEPT, outs[6:]))
 
 
 def add_to(total, term):
@@ -622,10 +971,9 @@
 
         yield from reduce_piece(copies, place, source, (0, 1, 2), g_acc, g_first, g_turns, g_last, local.at[SLOTS], finish)
 
-    def between(step):
-        multiply(min(len(order), done["jobs"] + 6))
-
-    march(sets, begin, (gains(),), between)
+    for step, _ in enumerate(march(sets, begin, (gains(),))):
+        if step % 8 == 7:
+            multiply(min(len(order), done["jobs"] + 2))
     for one in ending:
         one.wait_recv()
     copies.drain()
@@ -903,11 +1251,12 @@
     spatial = rows.shape[0] // 7
     bounds = ((0, 4 * spatial), (4 * spatial, 6 * spatial), (6 * spatial, 7 * spatial))
     own_gains = gains.shape[0]
-    tile = jnp.pad(gains.astype(F32), (0, 1024 - own_gains)).reshape(8, 128)
+    tile = jnp.pad(gains.astype(F32).reshape(-1, 48), ((0, 8 - own_gains // 48), (0, 80)))
     shards = (qkv_weights, out_weights, up_weights, down_weights)
     slabs = tuple((2 * w.shape[0], w.shape[1]) for w in shards)
-    wholes = gather_all(dims, *shards, tile)
-    gain = wholes[4].reshape(-1, 1024)[:, :own_gains].reshape(5, 2, D)
+    wholes, gain_rows, layer_out, kept = gather_all(dims, own_gains, shards, tile, rows)
+    layer_out = layer_out[None]
+    gain = gain_rows[:10].reshape(5, 2, D)
     qkv = wholes[0].reshape(5, 3, D, D)
     outw = wholes[1].reshape(5, D, D)
     upw = wholes[2].reshape(3, D, FF)
@@ -917,36 +1266,21 @@
     below_bias = jnp.where(place > 0, 0.0, FAR).astype(jnp.float32)
     above_bias = jnp.where(place < count - 1, 0.0, FAR).astype(jnp.float32)
     views = [rows[start:stop] for start, stop in bounds]
+    starts = (0, 6 * spatial, 10 * spatial, 13 * spatial)
     cross_keep = []
-    joined = []
     for view in range(2):
-        first = lowered(norm_rows(views[view], gain[3 + view, 0]))
-        second = lowered(norm_rows(views[view + 1], gain[3 + view, 1]))
-        query = lowered(product(first, qkv[3 + view, 0]))
-        keys = lowered(product(second, qkv[3 + view, 1]))
-        values = lowered(product(second, qkv[3 + view, 2]))
-        mixed, probs = attend(query, keys, values, 0.0)
-        joined.append(views[view] + product(mixed, outw[3 + view]))
-        cross_keep.append((first, second, query, keys, values, mixed, probs))
-    joined.append(views[2])
-    local_keep = []
-    edges = []
+        qs = slice(*bounds[view])
+        ks = slice(bounds[view + 1][0] - 4 * spatial, bounds[view + 1][1] - 4 * spatial)
+        query, keys, values = kept["cq"][qs], kept["ck"][ks], kept["cv"][ks]
+        probs = attend(query, keys, values, 0.0)[1]
+        cross_keep.append((None, None, query, keys, values, None, probs))
+    joined = [kept["joined"][start:stop] for start, stop in bounds]
+    self_keep = []
     for view in range(3):
-        normed = lowered(norm_rows(joined[view], gain[view, 0]))
-        query = lowered(product(normed, qkv[view, 0]))
-        keys = lowered(product(normed, qkv[view, 1]))
-        values = lowered(product(normed, qkv[view, 2]))
-        local_keep.append((normed, query, keys, values))
-        paired = jnp.stack([keys, values])
-        edges.append(jnp.concatenate([paired[:, :spatial], paired[:, -spatial:]], axis=1))
-    rim = extended(jnp.stack(edges, axis=1), (("tm", 2),), spatial)
-    self_keep = []
-    outputs = []
-    for view in range(3):
-        normed, query, keys, values = local_keep[view]
-        length = keys.shape[0]
-        keys_all = jnp.concatenate([rim[0, view, :spatial], keys, rim[0, view, 3 * spatial :]], axis=0)
-        values_all = jnp.concatenate([rim[1, view, :spatial], values, rim[1, view, 3 * spatial :]], axis=0)
+        rs = slice(*bounds[view])
+        ks = slice(starts[view], starts[view + 1])
+        length = bounds[view][1] - bounds[view][0]
+        query, keys_all, values_all = kept["q"][rs], kept["kx"][ks], kept["vx"][ks]
         bias = jnp.concatenate(
             [
                 jnp.broadcast_to(below_bias, (spatial,)),
@@ -954,14 +1288,8 @@
                 jnp.broadcast_to(above_bias, (spatial,)),
             ]
         )
-        mixed, probs = attend(query, keys_all, values_all, bias)
-        middle = joined[view] + product(mixed, outw[view])
-        normed_two = lowered(norm_rows(middle, gain[view, 1]))
-        hidden_pre = product(normed_two, upw[view])
-        active = lowered(jax.nn.gelu(hidden_pre, approximate=False))
-        outputs.append(middle + product(active, downw[view]))
-        self_keep.append((normed, query, keys_all, values_all, mixed, probs, middle, normed_two, hidden_pre, active))
-    layer_out = jnp.concatenate(outputs, axis=0)[None]
+        probs = attend(query, keys_all, values_all, bias)[1]
+        self_keep.append((None, query, keys_all, values_all, None, probs, kept["middle"][rs], None, kept["hidden"][rs], None))
     grad_gain = [[None, None] for index in range(5)]
     halves = []
     d_pre, d_attn = [], []
@@ -1021,16 +1349,7 @@
     gain_total = jnp.stack([jnp.stack(entry) for entry in grad_gain]).reshape(-1, own_gains)
     gain_total = jnp.pad(gain_total, ((0, 0), (0, 1024 - own_gains))).reshape(*dims, 2, 8, 128)
     tall = lambda parts: jnp.concatenate(parts, axis=0)
-    kept = lambda index: tall([entry[index] for entry in self_keep])
-    lefts = (
-        kept(9),
-        kept(7),
-        kept(4),
-        kept(0),
-        tall([entry[0] for entry in cross_keep]),
-        tall([entry[1] for entry in cross_keep]),
-        tall([entry[5] for entry in cross_keep]),
-    )
+    lefts = tuple(kept[name] for name in ("active", "normed_two", "mixed", "normed", "first", "second", "cmixed"))
     rights = (d_out, tall(d_pre), tall(d_attn), *[tall(part) for part in d_self], tall(d_cross), *[tall(part) for part in d_join])
     shares = reduce_all(dims, slabs, lefts, rights, gain_total)
     gain_share = shares[4].reshape(-1)[:own_gains]
@@ -1040,7 +1359,7 @@
 def fits(mesh, dims):
     chips = dims[0] * dims[1] * dims[2]
     rows = (15 * D, 5 * D, 3 * D, 3 * FF)
-    return dims[:2] == (2, 2) and all(r % (chips * ROWS) == 0 for r in rows) and 10 * D // (2 * chips) <= 1024
+    return dims[:2] == (2, 2) and all(r % (chips * ROWS) == 0 for r in rows) and (10 * D) % (2 * chips * 48) == 0 and 10 * D // (2 * chips) <= 384
 
 
 def solution(mesh):

time: 933 us -> 863 us (0.925)
  matrix products: 207 us -> 133 us
  Pallas kernels: 477 us -> 500 us
  local copies, waits for them, and re-layouts: 152 us -> 139 us
    dot_general x31 -> x0, matrix products: 87.6 us -> none  [the longest x26 75.7 us: product(): return jnp.dot(left, right, preferred_element_type=jnp.float32)]
    pallas_call x1, Pallas kernels: 223 us -> 250 us  [gather_all(): pl.pallas_call(functools.partial(gather_kernel, dims, own_gains), out_sha...]
    slice x5 -> x28, local copies, waits for them, and re-layouts: 5.1 us -> 30.4 us  [the longest x10 11.3 us: per_device(): query, keys, values = (kept['cq'][qs], kept['ck'][ks], kept['cv'][ks])]
    concatenate x14 -> x0, local copies, waits for them, and re-layouts: 23 us -> none  [the longest x7 11.9 us: per_device(): jnp.concatenate([rim[0, view, :spatial], keys, rim[0, view, 3 * spatial:]...]
    dot_general x26, matrix products: 71.4 us -> 82.2 us  [product_nt(): lax.dot_general(left, right, (((1,), (1,)), ((), ())), preferred_element_...]
    concatenate x16 -> x9, other arithmetic: 21.4 us -> 13.1 us  [per_device(): tall = lambda parts: jnp.concatenate(parts, axis=0)]
    convert_element_type x28 -> x13, local copies, waits for them, and re-layouts: 28.8 us -> 22.3 us  [lowered(): return value.astype(jnp.bfloat16)]
    unnamed x509 -> x409, local copies, waits for them, and re-layouts: 21.6 us -> 19.3 us
  transfers between devices with their start and end apart: 4 -> 2, of which waited for: 0 -> 0; matrix products, arithmetic and copies ran while one was open for 11% -> 12% of each run, Pallas kernels for 0% -> 0%
where the time goes in v2:
time: 863 us; the launch traced here: 851 us
  Pallas kernels  500 us (58%)
  local copies, waits for them, and re-layouts  139 us (16%)
  matrix products  133 us (15%)
  other arithmetic  69.9 us (8%)
    pallas_call x1, Pallas kernels, gather_all(): pl.pallas_call(functools.partial(gather_kernel, dims, own_gains), out_sha...  250 us
    pallas_call x1, Pallas kernels, reduce_all(): pl.pallas_call(functools.partial(reduce_kernel, dims, slabs, sets, count,...  249 us
    dot_general x26, matrix products, product_nt(): lax.dot_general(left, right, (((1,), (1,)), ((), ())), preferred_element_...  82.2 us
    slice x14, local copies, waits for them, and re-layouts, per_device(): part = whole[spatial:spatial + length]  23.6 us
    convert_element_type x13, local copies, waits for them, and re-layouts, lowered(): return value.astype(jnp.bfloat16)  22.3 us
    unnamed x409, local copies, waits for them, and re-layouts  19.3 us
  transfers between devices with their start and end apart: 2, of which 0 were waited for; matrix products, arithmetic and copies ran while one was open for 12% of the time, Pallas kernels for 0%

profile of v2, /device:TPU:0, one launch (start us, length us, event | category | flops | bytes accessed | tf_op | source)
XLA Modules:
  0.0 850.6 jit_solution(10020880408107063558)
XLA Ops:
  2.0 250.0 %shard_map.146 = (bf16[2,2,4,720,768]{4,3,2,1,0:T(8,128)(2,1)}, bf16[2,2,4,240,768]{4,3,2,1,0:T(8,128)(2,1)}, bf16[2,2,4,144,3072]{4,3,2,1,0:T(8,128)(2,1)}, bf1...) custom-call(bf16[360,768]{1,0:T(8,128)(2,1)} %refs_0_.1, ...), custom_call_target="tpu_custom_call" | custom-call | tf_op jit(solution)/shard_map/pallas_call | solution.py:696
  263.6 6.2 fusion.88
  271.9 5.5 fusion.37
  277.4 9.2 %fusion.19 = bf16[256,3072]{1,0:T(8,128)(2,1)} fusion(f32[448,3072]{1,0:T(8,128)S(1)} %bitcast.584, bf16[1,448,768]{2,1,0:T(8,128)(2,1)S(1)} %convert_element_type.214, bf16[3,3072,768]{2,1,0:T(8,128)(2,1)S(1)} %bitcast.577), kind=kOutput, calls=%fused_computation.30 | convolution fusion | flops 1264582656 | bytes 9830400 | tf_op jit(solution)/shard_map/dot_general | solution.py:81
  293.3 2.0 multiply_reduce_fusion.9
  300.5 2.1 copy.100
  302.6 4.6 multiply_reduce_fusion.26
  308.8 2.4 fusion.83
  312.9 2.1 copy.85
  315.0 1.9 copy.93
  316.9 2.1 copy.88
  319.1 1.9 copy.95
  321.0 5.0 multiply_reduce_fusion.4
  327.7 4.7 multiply_reduce_fusion.15
  333.5 1.9 fusion.73
  337.6 2.7 convolution_convert_fusion.1
  340.2 2.0 copy.87
  343.5 2.2 fusion.167
  347.3 1.8 multiply_reduce_fusion.10
  352.2 2.7 fusion.165
  354.9 2.9 fusion.169
  359.4 2.7 multiply_reduce_fusion.2
  366.6 4.7 fusion.171
  371.3 4.2 fusion.172
  377.0 3.3 multiply_reduce_fusion
  388.9 5.1 collective-permute-start
  425.6 2.7 fusion.68
  428.3 1.9 copy.136
  430.2 2.9 fusion.72
  446.7 1.9 copy.116
  455.8 1.9 slice.787
  457.7 1.8 copy.165
  461.4 1.9 slice.783
  463.3 1.8 copy.164
  466.9 1.8 copy.162
  468.8 1.9 copy.123
  472.5 1.9 copy.121
  474.4 2.3 copy.114
  478.5 2.3 copy.106
  480.8 1.8 copy.147
  482.6 2.7 fusion.174
  485.3 3.5 fusion.175
  488.8 2.1 pad_maximum_fusion.2.refs_10_
  492.1 3.2 pad_maximum_fusion.refs_8_
  500.4 2.2 convolution_add_fusion.4
  502.7 2.6 multiply_reduce_fusion.16
  507.1 2.5 fusion.74
  511.3 2.3 convolution_convert_fusion.2
  518.6 2.6 fusion.60
  522.9 2.8 fusion.65
  527.0 1.9 convolution_add_fusion.1
  529.0 2.7 multiply_reduce_fusion.5
  532.9 2.6 convolution_convert_fusion
  536.3 1.9 copy.117
  538.2 2.7 convolution_convert_fusion.3
  546.2 2.7 fusion.67
  549.0 2.0 fusion.62
  551.0 2.0 fusion.63
  553.0 1.9 multiply_reduce_fusion.27
  560.3 2.1 multiply_reduce_fusion.25
  569.3 1.9 copy.140
  571.2 2.0 multiply_reduce_fusion.3
  575.1 1.9 multiply_reduce_fusion.19
  589.2 249.5 %shard_map.147 = (f32[360,768]{1,0:T(8,128)}, f32[120,768]{1,0:T(8,128)}, f32[72,3072]{1,0:T(8,128)}, f32[288,768]{1,0:T(8,128)}, f32[8,128]{1,0:T(8,128)}, /*in...) custom-call(bf16[448,3072]{1,0:T(8,128)(2,1)} %get-tuple-element.225, ...), custom_call_target="tpu_custom_call" | custom-call | tf_op jit(solution)/shard_map/pallas_call | solution.py:998
  (619 shorter events, 178.8 us)
Async XLA Ops:
  252.0 5.9 copy-start.4
  252.0 6.0 copy-start.95
  263.4 6.4 slice-start.2
  263.4 6.4 slice-start.6
  263.5 6.3 slice-start.3
  263.5 7.6 slice-start.4
  263.5 8.0 slice-start.5
  263.5 8.3 slice-start.7
  286.6 9.2 %copy-start.112 = (f32[16,768]{1,0:T(8,128)S(1)}, f32[16,768]{1,0:T(8,128)}, u32[]{:S(2)}) copy-start(f32[16,768]{1,0:T(8,128)} %get-tuple-element.214) | copy-start | bytes 147460
  288.6 7.2 copy-start.170
  288.6 7.2 copy-start.168
  288.6 7.2 copy-start.165
  288.6 7.1 copy-start.137
  288.6 7.1 copy-start.133
  290.4 5.3 copy-start.184
  295.2 7.3 copy-start.7
  300.5 43.1 %copy-start.28 = (bf16[192,768]{0,1:T(8,128)(2,1)}, bf16[192,768]{0,1:T(8,128)(2,1)S(1)}, u32[]{:S(2)}) copy-start(bf16[192,768]{0,1:T(8,128)(2,1)S(1)} %copy.98) | copy-start | bytes 884740
  302.5 4.6 copy-start.190
  302.5 4.6 copy-start.124
  302.5 4.6 copy-start.171
  302.5 4.6 copy-start.188
  307.4 7.6 copy-start.41
  321.0 5.0 copy-start.144
  327.7 4.7 copy-start.185
  337.5 4.6 copy-start.50
  337.6 4.6 copy-start.157
  349.4 5.5 copy-start.30
  354.9 4.4 copy-start.98
  354.9 4.4 copy-start.111
  371.3 4.2 copy-start.117
  371.3 5.7 copy-start.97
  371.3 5.7 copy-start.99
  383.6 10.4 %copy-start.81 = (bf16[64,12,64]{0,2,1:T(8,128)(2,1)S(1)}, bf16[64,12,64]{0,2,1:T(8,128)(2,1)}, u32[]{:S(2)}) copy-start(bf16[64,12,64]{0,2,1:T(8,128)(2,1)} %get-tuple-element.314) | copy-start | bytes 294916
  384.3 10.4 %copy-start.82 = (bf16[64,12,64]{0,2,1:T(8,128)(2,1)S(1)}, bf16[64,12,64]{0,2,1:T(8,128)(2,1)}, u32[]{:S(2)}) copy-start(bf16[64,12,64]{0,2,1:T(8,128)(2,1)} %get-tuple-element.312) | copy-start | bytes 294916
  384.3 11.2 %copy-start.83 = (bf16[64,12,64]{0,2,1:T(8,128)(2,1)S(1)}, bf16[64,12,64]{0,2,1:T(8,128)(2,1)}, u32[]{:S(2)}) copy-start(bf16[64,12,64]{0,2,1:T(8,128)(2,1)} %get-tuple-element.310) | copy-start | bytes 294916
  388.9 106.5 %collective-permute-start = (bf16[2,3,64,768]{3,2,1,0:T(8,128)(2,1)}, bf16[2,3,64,768]{3,2,1,0:T(8,128)(2,1)}, u32[]{:S(2)}, u32[]{:S(2)}) collective-permute-start(bf16[2,3,64,768]{3,2,1,0:T(8,128)(2,1)} %pad_maximum_fusion.5), channel_id=1, source_target_pairs={{0,1},{1,2},{2,3},{3,4},{4,5},{5,6},{6,7},{8,9},{9,10},{10,11},{11... | collective-permute-start | bytes 1769480 | tf_op jit(solution)/shard_map/ppermute | solution.py:46
  396.2 10.3 %copy-start = (f32[1,448,768]{2,1,0:T(8,128)S(1)}, f32[1,448,768]{2,1,0:T(8,128)}, u32[]{:S(2)}) copy-start(f32[1,448,768]{2,1,0:T(8,128)} %param.39) | copy-start | bytes 4128772
  405.2 91.5 %collective-permute-start.1 = (bf16[2,3,64,768]{3,2,1,0:T(8,128)(2,1)}, bf16[2,3,64,768]{3,2,1,0:T(8,128)(2,1)}, u32[]{:S(2)}, u32[]{:S(2)}) collective-permute-start(bf16[2,3,64,768]{3,2,1,0:T(8,128)(2,1)} %pad_maximum_fusion.6), channel_id=1, source_target_pairs={{1,0},{2,1},{3,2},{4,3},{5,4},{6,5},{7,6},{9,8},{10,9},{11,10},{12... | collective-permute-start | bytes 1769480 | tf_op jit(solution)/shard_map/ppermute | solution.py:46
  409.4 4.2 copy-start.87
  409.4 4.2 copy-start.102
  433.1 5.4 copy-start.177
  433.1 6.0 copy-start.139
  499.7 5.5 copy-start.89
  500.4 4.8 copy-start.44
  546.2 4.8 copy-start.94
  553.0 5.0 copy-start.161
  560.2 4.9 copy-start.23
  560.2 4.9 copy-start.45
  560.2 4.9 copy-start.105
  560.2 5.8 copy-start.61
  560.2 5.8 copy-start.90
  560.3 5.8 copy-start.104
  566.0 5.1 copy-start.119
  575.1 4.5 copy-start.127
  575.1 4.5 copy-start.129
  575.1 5.0 copy-start.125
  575.1 5.0 copy-start.128
  577.1 4.3 copy-start.150
  577.1 4.3 copy-start.152
  577.1 4.2 copy-start.174
  583.4 4.9 copy-start.56
  583.4 4.9 copy-start.77
  589.2 250.7 %copy-start.132 = (f32[256]{0:T(256)S(1)}, f32[256]{0:T(256)}, u32[]{:S(2)}) copy-start(f32[256]{0:T(256)} %copy-done.131) | copy-start | bytes 3076
  589.2 250.8 %copy-start.158 = (f32[256]{0:T(256)S(1)}, f32[256]{0:T(256)}, u32[]{:S(2)}) copy-start(f32[256]{0:T(256)} %negate_multiply_fusion.3) | copy-start | bytes 3076
  (139 other events, 331.1 us)

commit v3 on v2

--- a/solution.py
+++ b/solution.py
@@ -19,7 +19,8 @@
 BLOCK = D // 2
 ROWS = 48
 LAG = 0.5
-SLOTS = 36
+SLOTS = 18
+EACH = 1.2
 COPIES = 480
 
 
@@ -717,11 +718,63 @@
     return outs[:4], outs[4], outs[5], dict(zip(KEPT, outs[6:]))
 
 
+class Stream:
+    def __init__(self, depth, sems, makers):
+        self.depth, self.sems, self.makers = depth, sems, makers
+        self.loading = {}
+        self.next_load = 0
+        self.next_use = 0
+        self.fetch()
+
+    def fetch(self):
+        while self.next_load < min(len(self.makers), self.next_use + self.depth):
+            slot = self.next_load % self.depth
+            copies = [
+                pltpu.make_async_copy(src, dst, self.sems.at[slot, j])
+                for j, (src, dst) in enumerate(self.makers[self.next_load](slot))
+            ]
+            for one in copies:
+                one.start()
+            self.loading[self.next_load] = copies
+            self.next_load += 1
+
+    def take(self):
+        for one in self.loading.pop(self.next_use):
+            one.wait()
+        return self.next_use % self.depth
+
+    def give_back(self):
+        self.next_use += 1
+        self.fetch()
+
+
+def row_runs(dims, slab, row, count):
+    at, end = row, row + count
+    while at < end:
+        chip, off = at // slab, at % slab
+        n = min(end - at, slab - off)
+        yield chip // (dims[1] * dims[2]), chip // dims[2] % dims[1], chip % dims[2], off, n, at - row
+        at += n
+
+
 def add_to(total, term):
     total[...] = (total[...].astype(F32) + term[...].astype(F32)).astype(total.dtype)
 
 
-def reduce_line(copies, place, pick, slots):
+class Credits:
+    def __init__(self, sems, waits, gives):
+        self.sems, self.waits, self.gives = sems, waits, gives
+
+    def wait(self, index, ok=None):
+        if self.waits:
+            when(ok, lambda: pl.semaphore_wait(self.sems.at[index], 1))
+
+    def give(self, index, device):
+        if self.gives:
+            pl.semaphore_signal(self.sems.at[index], inc=1, device_id=device, device_id_type=MESH)
+
+
+def reduce_line(copies, place, pick, slots, credits):
     n = place.dims[2]
     z = place.at[2]
     before = {}
@@ -736,9 +789,11 @@
                 def take(step=step, turn=turn, goal=goal):
                     before[step].wait_recv()
                     add_to(pick(goal), slots(turn - 1, step))
+                    credits.give(2 + 2 * (turn - 1) + (1 - step) // 2, place.along(2, jnp.clip(z - step, 0, n - 1)))
 
                 when((far >= 1) & (far <= turn), take)
             if turn < n - 1:
+                credits.wait(2 + 2 * turn + (1 - step) // 2, far <= turn)
                 before[step] = copies.start(
                     pick(goal), slots(turn, step), place.along(2, jnp.clip(z + step, 0, n - 1)), far <= turn
                 )
@@ -746,85 +801,203 @@
             yield
 
 
-def reduce_piece(copies, place, source, order, acc, first, turns, last, local, finish):
+def reduce_piece(copies, place, source, order, acc, first, turns, last, local, credits, finish):
     lead = order[0]
     rest = 1 - lead
     me, mine = place.at[lead], place.at[rest]
     z = place.at[2]
-    copy = copies.start(source(lead, 1 - me), first, place.along(lead, 1 - me))
+    beside, across = place.along(lead, 1 - me), place.along(rest, 1 - mine)
+    credits.wait(0)
+    copy = copies.start(source(lead, 1 - me), first, beside)
     load = pltpu.make_async_copy(source(lead, me), acc, local)
     load.start()
     yield
     load.wait()
     copy.wait_recv()
     add_to(acc, first)
+    credits.give(0, beside)
     slots = lambda turn, step: turns.at[turn, (1 - step) // 2]
     if order[1] == 2:
-        yield from reduce_line(copies, place, lambda v: acc.at[:, v], slots)
-        copy = copies.start(acc.at[1 - mine, z], last, place.along(rest, 1 - mine))
+        yield from reduce_line(copies, place, lambda v: acc.at[:, v], slots, credits)
+        credits.wait(1)
+        copy = copies.start(acc.at[1 - mine, z], last, across)
         yield
         copy.wait_recv()
         finish(acc[mine, z].astype(F32) + last[...].astype(F32))
+        credits.give(1, across)
     else:
-        copy = copies.start(acc.at[1 - mine], last, place.along(rest, 1 - mine))
+        credits.wait(1)
+        copy = copies.start(acc.at[1 - mine], last, across)
         yield
         copy.wait_recv()
         add_to(acc.at[mine], last)
-        yield from reduce_line(copies, place, lambda v: acc.at[mine, v], slots)
+        credits.give(1, across)
+        yield from reduce_line(copies, place, lambda v: acc.at[mine, v], slots, credits)
         finish(acc[mine, z].astype(F32))
 
 
-LEFTS = ("active", "normed_two", "mixed", "normed", "first", "second", "cross_mixed")
-RIGHTS = ("d_out", "d_pre", "d_attn", "dq", "dk", "dv", "d_cross", "cq", "ck", "cv")
-
-
-def jobs_of(spatial):
-    rows = {0: (0, 4 * spatial), 1: (4 * spatial, 2 * spatial), 2: (6 * spatial, spatial)}
-    late = {0: (0, 2 * spatial), 1: (2 * spatial, spatial)}
-    jobs = {a: [] for a in range(4)}
+def march_ready(sets, begin, ready, limit):
+    waiting = list(sets)
+    active = []
+    step = 0
+    started = 0
+    while active or waiting:
+        while (
+            waiting
+            and step >= LAG * started
+            and len(active) + len(waiting[0]) <= limit
+            and ready(waiting[0])
+        ):
+            for piece in waiting.pop(0):
+                active.append(begin(piece))
+            started += 1
+        if not active:
+            if step < LAG * started:
+                step += 1
+            else:
+                yield lambda: ready(waiting[0])
+            continue
+        still = []
+        for one in active:
+            try:
+                yield next(one)
+                still.append(one)
+            except StopIteration:
+                pass
+        active = still
+        step += 1
+
+
+LEFTS = ("active", "normed_two", "mixed", "normed", "first", "second", "cmixed")
+RIGHTS = ("d_out", "d_pre", "d_attn", "dq", "dk", "dv", "d_cross", "dcq", "dck", "dcv")
+HELD = ("q", "kx", "vx", "cq", "ck", "cv")
+
+
+def right_shapes(rows):
+    u = rows // 7
+    tall = dict(d_cross=6 * u, dcq=6 * u, dck=3 * u, dcv=3 * u)
+    return [(tall.get(k, rows), FF if k == "d_pre" else D) for k in RIGHTS]
+
+
+def job_batches(u):
+    rows = ((0, 4 * u), (4 * u, 2 * u), (6 * u, u))
+    late = ((0, 2 * u), (2 * u, u))
+    batches = {"down": [], "up": [], "out": [], "qkv": [], "cout": [], "cqkv": []}
     for view in range(3):
         for block in range(FF // D):
-            jobs[3].append((view * FF + block * D, 0, "active", block, rows[view], "d_out", 0, rows[view]))
+            batches["down"].append((3, view * FF + block * D, 0, "active", block, rows[view], "d_out", rows[view]))
         for block in range(FF // 2 // BLOCK):
-            jobs[2].append((view * D, block, "normed_two", 0, rows[view], "d_pre", block, rows[view]))
-        jobs[1].append((view * D, 0, "mixed", 0, rows[view], "d_attn", 0, rows[view]))
+            batches["up"].append((2, view * D, block, "normed_two", 0, rows[view], "d_pre", rows[view]))
+        batches["out"].append((1, view * D, 0, "mixed", 0, rows[view], "d_attn", rows[view]))
         for j, name in enumerate(("dq", "dk", "dv")):
-            jobs[0].append(((3 * view + j) * D, 0, "normed", 0, rows[view], name, 0, rows[view]))
-    for view in range(2):
-        jobs[1].append(((3 + view) * D, 0, "cross_mixed", 0, rows[view], "d_cross", 0, rows[view]))
-        jobs[0].append(((9 + 3 * view) * D, 0, "first", 0, rows[view], "cq", 0, rows[view]))
-        for j, name in enumerate(("ck", "cv")):
-            jobs[0].append(((10 + 3 * view + j) * D, 0, "second", 0, late[view], name, 0, late[view]))
-    return jobs
-
-
-def reduce_kernel(dims, slabs, sets, count, spatial, *refs):
+            batches["qkv"].append((0, (3 * view + j) * D, 0, "normed", 0, rows[view], name, rows[view]))
+    for c in range(2):
+        batches["cout"].append((1, (3 + c) * D, 0, "cmixed", 0, rows[c], "d_cross", rows[c]))
+        batches["cqkv"].append((0, (9 + 3 * c) * D, 0, "first", 0, rows[c], "dcq", rows[c]))
+        for j, name in enumerate(("dck", "dcv")):
+            batches["cqkv"].append((0, (10 + 3 * c + j) * D, 0, "second", 0, late[c], name, late[c]))
+    return batches
+
+
+def backward_blocks():
+    blocks = []
+    for view in range(3):
+        for j in range(FF // D):
+            blocks += [(3, view * FF + j * D, 0), (2, view * D, j)]
+    blocks += [(1, view * D, 0) for view in range(3)]
+    blocks += [(0, i * D, 0) for i in range(9)]
+    for c in range(2):
+        blocks += [(1, (3 + c) * D, 0)] + [(0, (9 + 3 * c + j) * D, 0) for j in range(3)]
+    return blocks
+
+
+def norm_pull(x, gain, grad):
+    centered = x - jnp.mean(x, axis=-1, keepdims=True)
+    scale = lax.rsqrt(jnp.mean(centered * centered, axis=-1, keepdims=True) + EPS)
+    unit = centered * scale
+    inner = grad * gain
+    pulled = scale * (
+        inner - jnp.mean(inner, axis=-1, keepdims=True) - unit * jnp.mean(inner * unit, axis=-1, keepdims=True)
+    )
+    return pulled, jnp.sum(grad * unit, axis=0, keepdims=True)
+
+
+def gelu_slope(pre):
+    return 0.5 * (1.0 + lax.erf(pre * (0.5**0.5))) + pre * jnp.exp(-0.5 * pre * pre) * 0.3989422804014327
+
+
+def attend_pair_back(query, keys, values, grad, bias):
+    dq, dk, dv = [], None, None
+    for part, g in zip(halves_of(query), halves_of(grad)):
+        scores = matmul_nt(part, keys) * 0.125
+        if bias is not None:
+            scores = scores + bias
+        probs = softmax_rows(scores)
+        dprobs = matmul_nt(g, values)
+        inner = jnp.sum(dprobs * probs, axis=-1, keepdims=True)
+        dscores = (probs * (dprobs - inner) * 0.125).astype(BF)
+        dq.append(matmul(dscores, keys))
+        k_term = matmul_tn(dscores, part)
+        v_term = matmul_tn(probs.astype(BF), g)
+        dk = k_term if dk is None else dk + k_term
+        dv = v_term if dv is None else dv + v_term
+    low = lax.broadcasted_iota(jnp.int32, dq[0].shape, 1) < dq[0].shape[1] // 2
+    return jnp.where(low, dq[0], dq[1]), dk, dv
+
+
+def gain_tiles(table, rows, own):
+    filled = own // 48
+    r = lax.broadcasted_iota(jnp.int32, (rows, D), 0)
+    c = lax.broadcasted_iota(jnp.int32, (rows, D), 1)
+    flat = (r // 8) * filled + r % 8
+    rr = lax.broadcasted_iota(jnp.int32, (rows, 16), 0)
+    vv = lax.broadcasted_iota(jnp.int32, (rows, 16), 1)
+    pick = (rr % 8 < filled) & (((rr // 8) * filled + rr % 8) // 16 == vv)
+    wide = jnp.dot(pick.astype(F32), table, precision=lax.Precision.HIGHEST, preferred_element_type=F32)
+    wide = jnp.where((r % 8 < filled) & (c // 48 == flat % 16), wide, 0.0)
+    j = lax.broadcasted_iota(jnp.int32, (D, 128), 1)
+    fold = (j < 48) & (j == lax.broadcasted_iota(jnp.int32, (D, 128), 0) % 48)
+    return jnp.dot(wide, fold.astype(F32), precision=lax.Precision.HIGHEST, preferred_element_type=F32)
+
+
+def reduce_kernel(dims, slabs, sets, own_gains, *refs):
     refs = list(refs)
     take = lambda n: [refs.pop(0) for _ in range(n)]
-    lefts, rights = dict(zip(LEFTS, take(7))), dict(zip(RIGHTS, take(10)))
-    (gain,) = take(1)
+    wholes = take(4)
+    (cot, gain, x, joined, middle, hidden) = take(6)
+    lefts = dict(zip(LEFTS, take(7)))
+    held_in = dict(zip(HELD, take(6)))
+    token_out = take(1)[0]
     results = take(4)
     (gain_out,) = take(1)
     parts = take(4)
     far_lefts, far_rights = dict(zip(LEFTS, take(7))), dict(zip(RIGHTS, take(10)))
+    rights = dict(zip(RIGHTS, take(10)))
+    held = dict(zip(HELD, take(6)))
     acc, first, turns_a, turns_b, last_a, last_b = take(6)
     finals = take(4)
     xs, ys, made = take(3)
-    g_far, g_acc, g_first, g_turns, g_last = take(5)
-    send, recv, local, load_sem, store_sem, final_sem = take(6)
+    g_far, g_own, g_acc, g_first, g_turns, g_last, g_sum = take(7)
+    ring, rowring, preing, flow, total, dmixed, dkf, dvf, halo_out, halo_in = take(10)
+    send, recv, local, load_sem, store_sem, final_sem, ring_sem, row_sem, pre_sem, held_sem, credit = take(11)
     place = Place(dims)
     core = place.core
     copies = Copies(send, recv)
     meet(place)
+    rows_all = cot.shape[0]
+    u = rows_all // 7
+    spans = ((0, 4 * u), (4 * u, 2 * u), (6 * u, u))
+    bases = (0, 6 * u, 10 * u)
+    count = 2 * dims[2]
     half_of = lambda ref, c: pl.ds(pl.multiple_of(c * (ref.shape[1] // 2), 128), ref.shape[1] // 2)
     coming = {}
-    for name in ("active", "d_out", "normed_two", "d_pre", "mixed", "d_attn", "normed", "dq", "dk", "dv", "cross_mixed", "d_cross", "first", "cq", "second", "ck", "cv"):
+
+    def swap(name):
         if name in lefts:
             coming[name] = copies.start(lefts[name], far_lefts[name], place.sibling())
         else:
             ref = rights[name]
             coming[name] = copies.start(ref.at[:, half_of(ref, 1 - core)], far_rights[name], place.sibling())
-    swap_gain = copies.start(gain, g_far, place.sibling())
 
     arrived = set()
 
@@ -833,103 +1006,279 @@
             coming[name].wait_recv()
             arrived.add(name)
 
-    order = [(a, job) for a in (3, 2, 1, 0) for job in jobs_of(spatial)[a]]
-
-    def load(i):
-        a, (row, block, left, lcol, lrows, right, rcol, rrows) = order[i]
-        slot = i % 2
+    def weight_maker(block):
+        a, row, col = block
+        return lambda slot: [
+            (wholes[a].at[p, q, z, pl.ds(off, n), pl.ds(col * D, D)], ring.at[slot, pl.ds(at, n)])
+            for p, q, z, off, n, at in row_runs(dims, slabs[a][0], row, D)
+        ]
+
+    def row_maker(ref, r0, n):
+        return lambda slot: [(ref.at[pl.ds(r0, n)], rowring.at[slot, pl.ds(0, n)])]
+
+    def pre_maker(view, j):
+        r0, n = spans[view]
+        return lambda slot: [(hidden.at[pl.ds(r0, n), pl.ds(j * D, D)], preing.at[slot, pl.ds(0, n)])]
+
+    swap("active")
+    rights["d_out"][...] = cot[...].astype(BF)
+    swap("d_out")
+    blocks = backward_blocks()
+    weights = Stream(ring.shape[0], ring_sem, [weight_maker(b) for b in blocks])
+    pres = Stream(2, pre_sem, [pre_maker(view, j) for view in range(3) for j in range(FF // D)])
+    row_list = [(middle, *spans[view]) for view in range(3)] + [(joined, *spans[view]) for view in range(3)]
+    for c in range(2):
+        row_list += [(x, *spans[c]), (x, *spans[c + 1])]
+    rowed = Stream(2, row_sem, [row_maker(*one) for one in row_list])
+    used_blocks = []
+
+    def weight(expected):
+        assert blocks[len(used_blocks)] == expected
+        used_blocks.append(expected)
+        return ring.at[weights.take()][...]
+
+    holding = {}
+    for i, name in enumerate(HELD):
+        holding[name] = pltpu.make_async_copy(held_in[name], held[name], held_sem.at[i])
+        holding[name].start()
+    for name in LEFTS[1:]:
+        swap(name)
+
+    state = {"jobs": 0, "gain": False}
+    ready = set()
+    storing = {}
+
+    def finish_stores(i):
+        for one in storing.pop(i, ()):
+            one.wait()
+
+    def load(job, i):
+        a, row, block, left, lcol, lrows, right, rrows = job
         arrive(left)
         arrive(right)
+        slot = i % 2
         n = lrows[1]
         ref = rights[right]
-        own = pl.ds(pl.multiple_of(core * (ref.shape[1] // 2) + rcol * BLOCK, 128), BLOCK)
+        own = pl.ds(pl.multiple_of(core * (ref.shape[1] // 2) + block * BLOCK, 128), BLOCK)
         pairs = [
             (lefts[left].at[pl.ds(*lrows), pl.ds(lcol * D, D)], xs.at[slot, pl.ds(0, n)]),
             (far_lefts[left].at[pl.ds(*lrows), pl.ds(lcol * D, D)], xs.at[slot, pl.ds(n, n)]),
             (ref.at[pl.ds(*rrows), own], ys.at[slot, pl.ds(0, n)]),
-            (far_rights[right].at[pl.ds(*rrows), pl.ds(rcol * BLOCK, BLOCK)], ys.at[slot, pl.ds(n, n)]),
+            (far_rights[right].at[pl.ds(*rrows), pl.ds(block * BLOCK, BLOCK)], ys.at[slot, pl.ds(n, n)]),
         ]
         loads = [pltpu.make_async_copy(s, d, load_sem.at[slot, j]) for j, (s, d) in enumerate(pairs)]
         for one in loads:
             one.start()
         return loads
 
-    loading = {0: load(0)}
-    storing = {}
-    done = {"jobs": 0}
-
-    def store(i):
-        a, job = order[i]
-        row, block = job[0], job[1]
-        slab = slabs[a][0]
-        slot = i % 2
-        stores = []
-        at, end = row, row + D
-        while at < end:
-            chip, off = at // slab, at % slab
-            n = min(end - at, slab - off)
-            p, q, z = chip // (dims[1] * dims[2]), chip // dims[2] % dims[1], chip % dims[2]
-            stores.append(
+    batches = job_batches(u)
+
+    def multiply(name, cost):
+        batch = batches[name]
+        loading = load(batch[0], state["jobs"])
+        for index, job in enumerate(batch):
+            i = state["jobs"]
+            slot = i % 2
+            for one in loading:
+                one.wait()
+            if index + 1 < len(batch):
+                loading = load(batch[index + 1], i + 1)
+            finish_stores(i - 2)
+            n = 2 * job[5][1]
+            made[slot] = matmul_tn(xs[slot, :n], ys[slot, :n]).astype(BF)
+            a, row, block = job[:3]
+            storing[i] = [
                 pltpu.make_async_copy(
-                    made.at[slot, pl.ds(at - row, n)],
+                    made.at[slot, pl.ds(at, n)],
                     parts[a].at[p, q, z, pl.ds(off, n), pl.ds(block * BLOCK, BLOCK)],
-                    store_sem.at[slot, len(stores)],
+                    store_sem.at[slot, k],
                 )
-            )
-            at += n
-        for one in stores:
-            one.start()
-        return stores
-
-    def finish_stores(i):
-        for one in storing.pop(i, ()):
-            one.wait()
-
-    def multiply(upto):
-        while done["jobs"] < upto:
-            i = done["jobs"]
-            for one in loading.pop(i):
-                one.wait()
-            if i + 1 < len(order):
-                loading[i + 1] = load(i + 1)
-            finish_stores(i - 2)
-            n = 2 * order[i][1][4][1]
-            slot = i % 2
-            made[slot] = lax.dot_general(
-                xs[slot, :n], ys[slot, :n], (((0,), (0,)), ((), ())), preferred_element_type=F32
-            ).astype(BF)
-            storing[i] = store(i)
-            done["jobs"] += 1
-
-    upto = {}
-    for a in (3, 2, 1, 0):
-        upto[a] = max(i for i, one in enumerate(order) if one[0] == a) + 1
-
-    used = {"n": 0, 0: 0, 1: 0}
-    owners = []
-    left_in = {a: sum(1 for s in sets for piece in s if piece[0] == a) for a in range(4)}
-    ending = []
-
-    def begin(piece):
-        a, row, block, order_ = piece
-        multiply(upto[a])
+                for k, (p, q, z, off, n, at) in enumerate(row_runs(dims, slabs[a][0], row, D))
+            ]
+            for one in storing[i]:
+                one.start()
+            state["jobs"] += 1
+            yield cost
         for i in list(storing):
             finish_stores(i)
-        i = used["n"]
-        used["n"] += 1
-        kind = 0 if order_[1] == 0 or order_[1] == 2 else 1
-        way = order_[::-1]
-        kind = 0 if way[1] == 2 else 1
-        k = used[kind]
-        used[kind] += 1
+
+    g = lambda e, j: gain[pl.ds(2 * e + j, 1), :]
+
+    def work():
+        for view in range(3):
+            r0, n = spans[view]
+            rows = pl.ds(r0, n)
+            cost = (2.0, 1.2, 0.9)[view]
+            for j in range(FF // D):
+                cols = pl.ds(j * D, D)
+                dactive = matmul_nt(rights["d_out"][rows], weight((3, view * FF + j * D, 0)))
+                weights.give_back()
+                slot = pres.take()
+                rights["d_pre"][rows, cols] = (dactive * gelu_slope(preing[slot, :n])).astype(BF)
+                pres.give_back()
+                term = matmul_nt(rights["d_pre"][rows, cols], weight((2, view * D, j)))
+                weights.give_back()
+                total[:n] = term if j == 0 else total[:n] + term
+                yield cost
+            slot = rowed.take()
+            pulled, g_sum[pl.ds(2 * view + 1, 1), :] = norm_pull(rowring[slot, :n], g(view, 1), total[:n])
+            rowed.give_back()
+            flow[rows] = cot[rows] + pulled
+            rights["d_attn"][rows] = flow[rows].astype(BF)
+            yield 0.8
+            if view == 0:
+                yield from multiply("down", 0.8)
+                ready.add(3)
+        swap("d_pre")
+        swap("d_attn")
+        for view in range(3):
+            rows = pl.ds(*spans[view])
+            dmixed[rows] = matmul_nt(rights["d_attn"][rows], weight((1, view * D, 0))).astype(BF)
+            weights.give_back()
+            yield 0.7
+        yield from multiply("up", 0.8)
+        ready.add(2)
+        for name in ("q", "kx", "vx"):
+            holding[name].wait()
+        halo = {}
+        up, down = place.slab < count - 1, place.slab > 0
+        for view in range(3):
+            r0, n = spans[view]
+            rows, keys = pl.ds(r0, n), pl.ds(bases[view], n + 2 * u)
+            bias = slab_bias(place, count, n + 2 * u, u)
+            for h in range(HEADS // 2):
+                cols = pl.ds(h * 128, 128)
+                dq, dk, dv = attend_pair_back(
+                    held["q"][rows, cols], held["kx"][keys, cols], held["vx"][keys, cols], dmixed[rows, cols], bias
+                )
+                rights["dq"][rows, cols] = dq.astype(BF)
+                for k, (whole, own) in enumerate(((dk, dkf), (dv, dvf))):
+                    halo_out[k, view, 0, :, cols] = whole[:u].astype(BF)
+                    own[rows, cols] = whole[u : u + n]
+                    halo_out[k, view, 1, :, cols] = whole[u + n :].astype(BF)
+                yield (3.0, 1.3, 0.7)[view]
+            for k in range(2):
+                for side, step, ok in ((0, -1, down), (1, 1, up)):
+                    halo[k, view, side] = copies.start(
+                        halo_out.at[k, view, side], halo_in.at[k, view, side], halo_device(place, count, step), ok
+                    )
+        swap("dq")
+        yield from multiply("out", 0.8)
+        for view in range(3):
+            r0, n = spans[view]
+            rows = pl.ds(r0, n)
+            for k, (own, name) in enumerate(((dkf, "dk"), (dvf, "dv"))):
+                for side, edge, ok in ((0, r0 + n - u, up), (1, r0, down)):
+
+                    def join(k=k, side=side, edge=edge, own=own):
+                        halo[k, view, side].wait_recv()
+                        own[pl.ds(edge, u)] = own[pl.ds(edge, u)] + halo_in[k, view, side].astype(F32)
+
+                    when(ok, join)
+                rights[name][rows] = own[rows].astype(BF)
+            for j, name in enumerate(("dq", "dk", "dv")):
+                term = matmul_nt(rights[name][rows], weight((0, (3 * view + j) * D, 0)))
+                weights.give_back()
+                total[:n] = term if j == 0 else total[:n] + term
+                yield 0.7
+            slot = rowed.take()
+            pulled, g_sum[pl.ds(2 * view, 1), :] = norm_pull(rowring[slot, :n], g(view, 0), total[:n])
+            rowed.give_back()
+            flow[rows] = flow[rows] + pulled
+            yield 0.6
+        swap("dk")
+        swap("dv")
+        rights["d_cross"][...] = flow[pl.ds(0, 6 * u)].astype(BF)
+        swap("d_cross")
+        for name in ("cq", "ck", "cv"):
+            holding[name].wait()
+        yield from multiply("qkv", 0.8)
+        for c in range(2):
+            r0, n = spans[c]
+            k0, m = spans[c + 1]
+            rows, keys = pl.ds(r0, n), pl.ds(k0 - 4 * u, m)
+            dmixed[rows] = matmul_nt(rights["d_cross"][rows], weight((1, (3 + c) * D, 0))).astype(BF)
+            weights.give_back()
+            yield 0.7
+            for h in range(HEADS // 2):
+                cols = pl.ds(h * 128, 128)
+                dq, dk, dv = attend_pair_back(
+                    held["cq"][rows, cols], held["ck"][keys, cols], held["cv"][keys, cols], dmixed[rows, cols], None
+                )
+                rights["dcq"][rows, cols] = dq.astype(BF)
+                rights["dck"][keys, cols] = dk.astype(BF)
+                rights["dcv"][keys, cols] = dv.astype(BF)
+                yield (1.5, 0.6)[c]
+            term = matmul_nt(rights["dcq"][rows], weight((0, (9 + 3 * c) * D, 0)))
+            weights.give_back()
+            slot = rowed.take()
+            pulled, g_sum[pl.ds(2 * (3 + c), 1), :] = norm_pull(rowring[slot, :n], g(3 + c, 0), term)
+            rowed.give_back()
+            flow[rows] = flow[rows] + pulled
+            yield 1.0
+            term = matmul_nt(rights["dck"][keys], weight((0, (10 + 3 * c) * D, 0)))
+            weights.give_back()
+            term = term + matmul_nt(rights["dcv"][keys], weight((0, (11 + 3 * c) * D, 0)))
+            weights.give_back()
+            slot = rowed.take()
+            pulled, g_sum[pl.ds(2 * (3 + c) + 1, 1), :] = norm_pull(rowring[slot, :m], g(3 + c, 1), term)
+            rowed.give_back()
+            late = pl.ds(k0, m)
+            flow[late] = flow[late] + pulled
+            yield 1.0
+        for name in ("dcq", "dck", "dcv"):
+            swap(name)
+        yield from multiply("cout", 0.8)
+        ready.add(1)
+        token = pltpu.make_async_copy(flow, token_out, final_sem.at[4])
+        token.start()
+        g_sum[pl.ds(10, 6), :] = jnp.zeros((6, D), F32)
+        g_own[...] = gain_tiles(g_sum[...], 2 * dims[0] * dims[1] * dims[2] * 8, own_gains).reshape(g_own.shape)
+        coming["gain"] = copies.start(g_own, g_far, place.sibling())
+        yield 1.0
+        yield from multiply("cqkv", 0.8)
+        ready.add(0)
+        state["gain"] = True
+        token.wait()
+
+    flat = [piece for group in sets for piece in group if piece != "gain"]
+    owners = {}
+    kinds = [0 if piece[3][1] == 2 else 1 for piece in flat[:SLOTS]]
+    left_in = {a: sum(1 for piece in flat if piece[0] == a) for a in range(4)}
+    ending = []
+    begun = {"n": 0}
+
+    def gains():
+        coming["gain"].wait_recv()
+        add_to(g_far, g_own)
+        source = lambda dim, value: g_far.at[(*[value if d == dim else slice(None) for d in range(3)], core)]
+
+        def finish(value):
+            g_first[0, 0] = value
+            copy = pltpu.make_async_copy(g_first.at[0, 0], gain_out, final_sem.at[5])
+            copy.start()
+            copy.wait()
+
+        yield from reduce_piece(
+            copies, place, source, (0, 1, 2), g_acc, g_first, g_turns, g_last, local.at[SLOTS], Credits(None, False, False), finish
+        )
+
+    def begin(piece):
+        if piece == "gain":
+            return gains()
+        a, row, block, order = piece
+        i = begun["n"]
+        begun["n"] += 1
         slot = i % SLOTS
         if i >= SLOTS:
             owners[i - SLOTS].drain()
         mine = Copies(send, recv)
-        mine.used = copies.used
-        copies.used += 9
-        owners.append(mine)
+        mine.used = COPIES - 9 * (len(flat) - i)
+        owners[i] = mine
         cols = pl.ds(block * BLOCK, BLOCK)
+        kind = kinds[slot]
+        k = kinds[:slot].count(kind)
+        turns, last = ((turns_a, last_a), (turns_b, last_b))[kind]
 
         def source(dim, value):
             index = [slice(None)] * 3
@@ -942,9 +1291,9 @@
             if left_in[a] == 0:
                 deliver(a)
 
-        turns, last = ((turns_a, last_a), (turns_b, last_b))[kind]
+        credits = Credits(credit.at[slot], i >= SLOTS, i + SLOTS < len(flat))
         return reduce_piece(
-            mine, place, source, way, acc.at[slot], first.at[i], turns.at[k], last.at[k], local.at[slot], finish
+            mine, place, source, order[::-1], acc.at[slot], first.at[slot], turns.at[k], last.at[k], local.at[slot], credits, finish
         )
 
     def deliver(a):
@@ -961,52 +1310,49 @@
         keep.start()
         keep.wait()
 
-    def gains():
-        swap_gain.wait_recv()
-        add_to(g_far, gain)
-        source = lambda dim, value: g_far.at[(*[value if d == dim else slice(None) for d in range(3)], core)]
-
-        def finish(value):
-            gain_out[...] = value
-
-        yield from reduce_piece(copies, place, source, (0, 1, 2), g_acc, g_first, g_turns, g_last, local.at[SLOTS], finish)
-
-    for step, _ in enumerate(march(sets, begin, (gains(),))):
-        if step % 8 == 7:
-            multiply(min(len(order), done["jobs"] + 2))
+    def set_ready(group):
+        return state["gain"] if group[0] == "gain" else all(piece[0] in ready for piece in group)
+
+    weave(march_ready(sets, begin, set_ready, SLOTS), work(), EACH)
     for one in ending:
         one.wait_recv()
     copies.drain()
-    for one in owners:
+    for one in owners.values():
         one.drain()
-
-
-def reduce_all(dims, slabs, lefts, rights, gain):
+    assert copies.used <= COPIES - 9 * len(flat)
+
+
+def reduce_all(dims, slabs, own_gains, wholes, cot, gain, x, kept):
     anywhere = pl.BlockSpec(memory_space=pl.ANY)
     vmem = pl.BlockSpec(memory_space=pltpu.VMEM)
     sets = pieces_of(slabs, (3, 2, 1, 0))
     flat = [piece for group in sets for piece in group]
-    count = len(flat)
-    bundled = sum(1 for piece in flat if piece[3][1] == 2)
-    single = count - bundled
+    sets.insert(len(sets) - 3, ["gain"])
+    kinds = [0 if piece[3][1] == 2 else 1 for piece in flat[:SLOTS]]
+    bundled, single = kinds.count(0), kinds.count(1)
     z = dims[2]
-    spatial = lefts[0].shape[0] // 7
-    longest = 2 * 4 * spatial
+    rows = cot.shape[0]
+    u = rows // 7
     tile = (ROWS, BLOCK)
     segments = max(D // slab[0] + 2 for slab in slabs)
-    halves = lambda ref: jax.ShapeDtypeStruct((ref.shape[0], ref.shape[1] // 2), BF)
+    lefts = [kept[k] for k in LEFTS]
+    held = [kept[k] for k in HELD]
+    rights = right_shapes(rows)
     outs = pl.pallas_call(
-        functools.partial(reduce_kernel, dims, slabs, sets, count, spatial),
-        out_shape=[jax.ShapeDtypeStruct((s[0] // 2, s[1]), F32) for s in slabs]
+        functools.partial(reduce_kernel, dims, slabs, sets, own_gains),
+        out_shape=[jax.ShapeDtypeStruct((rows, D), F32)]
+        + [jax.ShapeDtypeStruct((s[0] // 2, s[1]), F32) for s in slabs]
         + [jax.ShapeDtypeStruct((8, 128), F32)]
         + [jax.ShapeDtypeStruct((*dims, s[0], s[1] // 2), BF) for s in slabs]
-        + [jax.ShapeDtypeStruct(x.shape, BF) for x in lefts]
-        + [halves(y) for y in rights],
-        in_specs=[anywhere] * 17 + [vmem],
-        out_specs=[vmem] * 5 + [anywhere] * 21,
-        scratch_shapes=[
+        + [jax.ShapeDtypeStruct(one.shape, BF) for one in lefts]
+        + [jax.ShapeDtypeStruct((r, w // 2), BF) for r, w in rights],
+        in_specs=[anywhere] * 4 + [vmem] * 2 + [anywhere] * 17,
+        out_specs=[anywhere] * 27,
+        scratch_shapes=[pltpu.VMEM(s, BF) for s in rights]
+        + [pltpu.VMEM(one.shape, BF) for one in held]
+        + [
             pltpu.VMEM((SLOTS, 2, z, *tile), BF),
-            pltpu.VMEM((count, 2, z, *tile), BF),
+            pltpu.VMEM((SLOTS, 2, z, *tile), BF),
             pltpu.VMEM((bundled, z - 1, 2, 2, *tile), BF),
             pltpu.VMEM((single, z - 1, 2, *tile), BF),
             pltpu.VMEM((bundled, *tile), BF),
@@ -1014,26 +1360,41 @@
         ]
         + [pltpu.VMEM((s[0], s[1] // 2), F32) for s in slabs]
         + [
-            pltpu.VMEM((2, longest, D), BF),
-            pltpu.VMEM((2, longest, BLOCK), BF),
+            pltpu.VMEM((2, 8 * u, D), BF),
+            pltpu.VMEM((2, 8 * u, BLOCK), BF),
             pltpu.VMEM((2, D, BLOCK), BF),
+            pltpu.VMEM((*dims, 2, 8, 128), F32),
             pltpu.VMEM((*dims, 2, 8, 128), F32),
             pltpu.VMEM((2, z, 8, 128), F32),
             pltpu.VMEM((2, z, 8, 128), F32),
             pltpu.VMEM((z - 1, 2, 8, 128), F32),
             pltpu.VMEM((z, 8, 128), F32),
+            pltpu.VMEM((16, D), F32),
+            pltpu.VMEM((4, D, D), BF),
+            pltpu.VMEM((2, 4 * u, D), F32),
+            pltpu.VMEM((2, 4 * u, D), F32),
+            pltpu.VMEM((rows, D), F32),
+            pltpu.VMEM((4 * u, D), F32),
+            pltpu.VMEM((rows, D), BF),
+            pltpu.VMEM((rows, D), F32),
+            pltpu.VMEM((rows, D), F32),
+            pltpu.VMEM((2, 3, 2, u, D), BF),
+            pltpu.VMEM((2, 3, 2, u, D), BF),
             pltpu.SemaphoreType.DMA((COPIES,)),
             pltpu.SemaphoreType.DMA((COPIES,)),
             pltpu.SemaphoreType.DMA((SLOTS + 1,)),
             pltpu.SemaphoreType.DMA((2, 4)),
             pltpu.SemaphoreType.DMA((2, segments)),
-            pltpu.SemaphoreType.DMA((4,)),
+            pltpu.SemaphoreType.DMA((6,)),
+            pltpu.SemaphoreType.DMA((4, segments)),
+            pltpu.SemaphoreType.DMA((2, 1)),
+            pltpu.SemaphoreType.DMA((2, 1)),
+            pltpu.SemaphoreType.DMA((6,)),
+            pltpu.SemaphoreType.REGULAR((SLOTS, 2 + 2 * (z - 1))),
         ],
-        compiler_params=pltpu.CompilerParams(
-            collective_id=1, has_side_effects=True, vmem_limit_bytes=60 << 20
-        ),
-    )(*lefts, *rights, gain)
-    return outs[:5]
+        compiler_params=pltpu.CompilerParams(collective_id=1, has_side_effects=True, vmem_limit_bytes=62 << 20),
+    )(*wholes, cot, gain, x, kept["joined"], kept["middle"], kept["hidden"], *lefts, *held)
+    return outs[:6]
 
 
 def plain_device(tokens, cotangent, qkv_weights, out_weights, up_weights, down_weights, gains):
@@ -1247,113 +1608,14 @@
 
 def per_device(dims, tokens, cotangent, qkv_weights, out_weights, up_weights, down_weights, gains):
     rows = tokens[0]
-    incoming = cotangent[0]
-    spatial = rows.shape[0] // 7
-    bounds = ((0, 4 * spatial), (4 * spatial, 6 * spatial), (6 * spatial, 7 * spatial))
     own_gains = gains.shape[0]
     tile = jnp.pad(gains.astype(F32).reshape(-1, 48), ((0, 8 - own_gains // 48), (0, 80)))
     shards = (qkv_weights, out_weights, up_weights, down_weights)
     slabs = tuple((2 * w.shape[0], w.shape[1]) for w in shards)
-    wholes, gain_rows, layer_out, kept = gather_all(dims, own_gains, shards, tile, rows)
-    layer_out = layer_out[None]
-    gain = gain_rows[:10].reshape(5, 2, D)
-    qkv = wholes[0].reshape(5, 3, D, D)
-    outw = wholes[1].reshape(5, D, D)
-    upw = wholes[2].reshape(3, D, FF)
-    downw = wholes[3].reshape(3, FF, D)
-    place = lax.axis_index("tm")
-    count = lax.axis_size("tm")
-    below_bias = jnp.where(place > 0, 0.0, FAR).astype(jnp.float32)
-    above_bias = jnp.where(place < count - 1, 0.0, FAR).astype(jnp.float32)
-    views = [rows[start:stop] for start, stop in bounds]
-    starts = (0, 6 * spatial, 10 * spatial, 13 * spatial)
-    cross_keep = []
-    for view in range(2):
-        qs = slice(*bounds[view])
-        ks = slice(bounds[view + 1][0] - 4 * spatial, bounds[view + 1][1] - 4 * spatial)
-        query, keys, values = kept["cq"][qs], kept["ck"][ks], kept["cv"][ks]
-        probs = attend(query, keys, values, 0.0)[1]
-        cross_keep.append((None, None, query, keys, values, None, probs))
-    joined = [kept["joined"][start:stop] for start, stop in bounds]
-    self_keep = []
-    for view in range(3):
-        rs = slice(*bounds[view])
-        ks = slice(starts[view], starts[view + 1])
-        length = bounds[view][1] - bounds[view][0]
-        query, keys_all, values_all = kept["q"][rs], kept["kx"][ks], kept["vx"][ks]
-        bias = jnp.concatenate(
-            [
-                jnp.broadcast_to(below_bias, (spatial,)),
-                jnp.zeros((length,), jnp.float32),
-                jnp.broadcast_to(above_bias, (spatial,)),
-            ]
-        )
-        probs = attend(query, keys_all, values_all, bias)[1]
-        self_keep.append((None, query, keys_all, values_all, None, probs, kept["middle"][rs], None, kept["hidden"][rs], None))
-    grad_gain = [[None, None] for index in range(5)]
-    halves = []
-    d_pre, d_attn = [], []
-    d_out = lowered(incoming)
-    for view in range(3):
-        normed, query, keys_all, values_all, mixed, probs, middle, normed_two, hidden_pre, active = self_keep[view]
-        start, stop = bounds[view]
-        dfinal = incoming[start:stop]
-        dactive = product_nt(d_out[start:stop], downw[view])
-        d_pre.append(lowered(gelu_back(hidden_pre, dactive)))
-        dnormed_two = product_nt(d_pre[view], upw[view])
-        dmid_norm, grad_gain[view][1] = norm_back(middle, gain[view, 1], dnormed_two)
-        dmiddle = dfinal + dmid_norm
-        d_attn.append(lowered(dmiddle))
-        dmixed = lowered(product_nt(d_attn[view], outw[view]))
-        dquery, dkeys, dvalues = attend_back(query, keys_all, values_all, probs, dmixed)
-        halves.append((dmiddle, dquery, dkeys, dvalues))
-    lower_part = jnp.stack([jnp.stack([half[2][:spatial], half[3][:spatial]]) for half in halves], axis=1)
-    upper_part = jnp.stack([jnp.stack([half[2][-spatial:], half[3][-spatial:]]) for half in halves], axis=1)
-    from_above = from_behind(lower_part.astype(jnp.bfloat16), "tm", -1).astype(lower_part.dtype)
-    from_below = from_behind(upper_part.astype(jnp.bfloat16), "tm", 1).astype(upper_part.dtype)
-    dfused = []
-    d_self = [[], [], []]
-    for view in range(3):
-        dmiddle, dquery, dkeys, dvalues = halves[view]
-        length = dquery.shape[0]
-        own = [dquery]
-        for index, whole in ((0, dkeys), (1, dvalues)):
-            part = whole[spatial : spatial + length]
-            part = part.at[:spatial].add(from_below[index, view]).at[length - spatial :].add(from_above[index, view])
-            own.append(part)
-        own = [lowered(part) for part in own]
-        for index in range(3):
-            d_self[index].append(own[index])
-        dnormed = (
-            product_nt(own[0], qkv[view, 0]) + product_nt(own[1], qkv[view, 1]) + product_nt(own[2], qkv[view, 2])
-        )
-        dfused_norm, grad_gain[view][0] = norm_back(joined[view], gain[view, 0], dnormed)
-        dfused.append(dmiddle + dfused_norm)
-    dviews = list(dfused)
-    d_cross = []
-    d_join = [[], [], []]
-    for view in range(2):
-        first, second, query, keys, values, mixed, probs = cross_keep[view]
-        d_cross.append(lowered(dfused[view]))
-        dmixed = lowered(product_nt(d_cross[view], outw[3 + view]))
-        own = [lowered(part) for part in attend_back(query, keys, values, probs, dmixed)]
-        for index in range(3):
-            d_join[index].append(own[index])
-        dfirst = product_nt(own[0], qkv[3 + view, 0])
-        dsecond = product_nt(own[1], qkv[3 + view, 1]) + product_nt(own[2], qkv[3 + view, 2])
-        dx_first, grad_gain[3 + view][0] = norm_back(views[view], gain[3 + view, 0], dfirst)
-        dx_second, grad_gain[3 + view][1] = norm_back(views[view + 1], gain[3 + view, 1], dsecond)
-        dviews[view] = dviews[view] + dx_first
-        dviews[view + 1] = dviews[view + 1] + dx_second
-    token_grad = jnp.concatenate(dviews, axis=0)[None]
-    gain_total = jnp.stack([jnp.stack(entry) for entry in grad_gain]).reshape(-1, own_gains)
-    gain_total = jnp.pad(gain_total, ((0, 0), (0, 1024 - own_gains))).reshape(*dims, 2, 8, 128)
-    tall = lambda parts: jnp.concatenate(parts, axis=0)
-    lefts = tuple(kept[name] for name in ("active", "normed_two", "mixed", "normed", "first", "second", "cmixed"))
-    rights = (d_out, tall(d_pre), tall(d_attn), *[tall(part) for part in d_self], tall(d_cross), *[tall(part) for part in d_join])
-    shares = reduce_all(dims, slabs, lefts, rights, gain_total)
-    gain_share = shares[4].reshape(-1)[:own_gains]
-    return (layer_out, token_grad, shares[0], shares[1], shares[2], shares[3], gain_share)
+    wholes, gain, layer_out, kept = gather_all(dims, own_gains, shards, tile, rows)
+    shares = reduce_all(dims, slabs, own_gains, wholes, cotangent[0], gain, rows, kept)
+    gain_share = shares[5][: own_gains // 48, :48].reshape(own_gains)
+    return (layer_out[None], shares[0][None], *shares[1:5], gain_share)
 
 
 def fits(mesh, dims):

time: 863 us -> 584 us (0.68)
  matrix products: 133 us -> 0 us
  local copies, waits for them, and re-layouts: 139 us -> 9.4 us
  other arithmetic: 69.9 us -> 0.6 us
  Pallas kernels: 500 us -> 564 us
    dot_general x46 -> x0, matrix products: 118 us -> none  [the longest x26 82.2 us: product_nt(): lax.dot_general(left, right, (((1,), (1,)), ((), ())), preferred_element_...]
    pallas_call x1, Pallas kernels: 249 us -> 314 us  [reduce_all(): pl.pallas_call(functools.partial(reduce_kernel, dims, slabs, sets, own_ga...]
    slice x49 -> x0, local copies, waits for them, and re-layouts: 59.8 us -> none  [the longest x14 23.6 us: per_device(): part = whole[spatial:spatial + length]]
    another operation x20 -> x0, local copies, waits for them, and re-layouts: 23.9 us -> none
    convert_element_type x13 -> x0, local copies, waits for them, and re-layouts: 22.3 us -> none  [lowered(): return value.astype(jnp.bfloat16)]
    reduce_sum x23 -> x0, other arithmetic: 20.7 us -> none  [the longest x9 7.83 us: norm_rows(): mean = jnp.mean(x, axis=-1, keepdims=True)]
    concatenate x12 -> x0, other arithmetic: 15 us -> none  [the longest x9 13.1 us: per_device(): tall = lambda parts: jnp.concatenate(parts, axis=0)]
    sub x5 -> x0, matrix products: 14.9 us -> none  [attend(): expo = jnp.exp(scores - top)]
  transfers between devices with their start and end apart: 2 -> 0, of which waited for: 0 -> 0; matrix products, arithmetic and copies ran while one was open for 12% -> 0% of each run, Pallas kernels for 0% -> 0%
where the time goes in v3:
time: 584 us; the launch traced here: 574 us
  Pallas kernels  564 us (97%)
  local copies, waits for them, and re-layouts  9.4 us (2%)
    pallas_call x1, Pallas kernels, reduce_all(): pl.pallas_call(functools.partial(reduce_kernel, dims, slabs, sets, own_ga...  314 us
    pallas_call x1, Pallas kernels, gather_all(): pl.pallas_call(functools.partial(gather_kernel, dims, own_gains), out_sha...  250 us

profile of v3, /device:TPU:0, one launch (start us, length us, event | category | flops | bytes accessed | tf_op | source)
XLA Modules:
  0.0 574.4 jit_solution(10431567813172361091)
XLA Ops:
  0.6 0.7 reshape.21
  1.4 0.6 pad_convert_fusion.refs_4_
  2.0 249.7 %shard_map.126 = (bf16[2,2,4,720,768]{4,3,2,1,0:T(8,128)(2,1)}, bf16[2,2,4,240,768]{4,3,2,1,0:T(8,128)(2,1)}, bf16[2,2,4,144,3072]{4,3,2,1,0:T(8,128)(2,1)}, bf1...) custom-call(bf16[360,768]{1,0:T(8,128)(2,1)} %refs_0_.1, ...), custom_call_target="tpu_custom_call" | custom-call | tf_op jit(solution)/shard_map/pallas_call | solution.py:697
  251.7 0.0 copy-start
  251.7 313.8 %shard_map.127 = (f32[448,768]{1,0:T(8,128)}, f32[360,768]{1,0:T(8,128)}, f32[120,768]{1,0:T(8,128)}, f32[72,3072]{1,0:T(8,128)}, f32[288,768]{1,0:T(8,128)}, /*...) custom-call(bf16[2,2,4,720,768]{4,3,2,1,0:T(8,128)(2,1)} %get-tuple-, ...), custom_call_target="tpu_custom_call" | custom-call | tf_op jit(solution)/shard_map/pallas_call | solution.py:1341
  565.5 1.3 reshape.22
  566.9 0.0 copy-done
  566.9 0.0 copy-start.1
  566.9 1.1 copy.20
  567.9 0.8 copy-done.1
  568.7 0.0 copy-start.2
  568.7 1.1 copy.21
  569.8 0.7 copy-done.2
  570.4 0.0 copy-start.5
  570.4 0.0 copy-start.4
  570.4 1.0 copy.22
  571.4 0.2 copy-done.5
  571.6 0.0 copy-start.3
  571.6 0.7 copy.23
  572.4 0.0 copy-done.4
  572.4 0.9 copy.24
  573.3 0.0 copy-done.3
  573.3 0.9 copy.25
Async XLA Ops:
  251.7 315.2 %copy-start = (f32[448,768]{1,0:T(8,128)S(1)}, f32[448,768]{1,0:T(8,128)}, u32[]{:S(2)}) copy-start(f32[448,768]{1,0:T(8,128)} %get-tuple-element.35) | copy-start | bytes 4128772
  566.9 1.8 copy-start.1
  568.7 1.7 copy-start.2
  570.4 1.2 copy-start.5
  570.4 1.9 copy-start.4
  571.6 1.7 copy-start.3

commit v4 on v3

--- a/solution.py
+++ b/solution.py
@@ -20,7 +20,8 @@
 ROWS = 48
 LAG = 0.5
 SLOTS = 18
-EACH = 1.2
+EACH = 1.0
+EACH_FORWARD = 0.5
 COPIES = 480
 
 
@@ -370,6 +371,15 @@
     vv = lax.broadcasted_iota(jnp.int32, (16, rows), 0)
     pick = (rr % 8 < filled) & (((rr // 8) * filled + rr % 8) // 16 == vv)
     return matmul(pick.astype(BF), wide)
+
+
+def row_runs(dims, slab, row, count):
+    at, end = row, row + count
+    while at < end:
+        chip, off = at // slab, at % slab
+        n = min(end - at, slab - off)
+        yield chip // (dims[1] * dims[2]), chip // dims[2] % dims[1], chip % dims[2], off, n, at - row
+        at += n
 
 
 class Weights:
@@ -427,11 +437,10 @@
     blocks += [(0, i * D, 0) for i in range(9)]
     blocks += [(1, i * D, 0) for i in range(3)]
     blocks += [(2, v * D, j) for v in range(3) for j in range(FF // D)]
-    blocks += [(3, v * FF + j * D, 0) for v in range(3) for j in range(FF // D)]
     return blocks
 
 
-KEPT = ("first", "second", "cq", "ck", "cv", "cmixed", "joined", "normed", "q", "kx", "vx", "mixed", "middle", "normed_two", "hidden", "active")
+KEPT = ("first", "second", "cq", "ck", "cv", "cmixed", "joined", "normed", "q", "kx", "vx", "mixed", "middle", "normed_two", "slope", "active")
 
 
 def forward_shapes(rows):
@@ -439,9 +448,9 @@
     sizes = dict(
         first=(6 * u, D), second=(3 * u, D), cq=(6 * u, D), ck=(3 * u, D), cv=(3 * u, D), cmixed=(6 * u, D),
         joined=(rows, D), normed=(rows, D), q=(rows, D), kx=(rows + 6 * u, D), vx=(rows + 6 * u, D),
-        mixed=(rows, D), middle=(rows, D), normed_two=(rows, D), hidden=(rows, FF), active=(rows, FF),
+        mixed=(rows, D), middle=(rows, D), normed_two=(rows, D), slope=(rows, FF), active=(rows, FF),
     )
-    return {k: (sizes[k], F32 if k in ("joined", "middle", "hidden") else BF) for k in KEPT}
+    return {k: (sizes[k], F32 if k in ("joined", "middle", "slope") else BF) for k in KEPT}
 
 
 def halo_device(place, count, step):
@@ -456,7 +465,7 @@
     return jnp.where(below | above, FAR, 0.0).astype(F32)
 
 
-def forward_work(place, copies, weights, need, gain, x, layer, v, save):
+def forward_work(place, copies, weights, need, gain, x, v, save, swap, products):
     u = x.shape[0] // 7
     count = 2 * place.dims[2]
     spans = ((0, 4 * u), (4 * u, 2 * u), (6 * u, u))
@@ -546,7 +555,6 @@
             cols = pl.ds(h * 128, 128)
             v["mixed"][rows, cols] = attend_pair(v["q"][rows, cols], v["kx"][keys, cols], v["vx"][keys, cols], bias)
             yield (1.4, 0.6, 0.3)[view]
-        w = weights_later = None
     save("kx")
     save("vx")
     save("mixed")
@@ -567,35 +575,28 @@
             w = weights.take((2, view * D, j))
             pre = matmul(v["normed_two"][rows], w[...])
             weights.give_back()
-            v["hidden"][rows, cols] = pre
-            v["active"][rows, cols] = (0.5 * pre * (1.0 + lax.erf(pre * (0.5**0.5)))).astype(BF)
-            yield 1.2
-    save("hidden")
+            area = 0.5 * (1.0 + lax.erf(pre * (0.5**0.5)))
+            v["active"][rows, cols] = (pre * area).astype(BF)
+            v["slope"][rows, cols] = area + pre * jnp.exp(-0.5 * pre * pre) * 0.3989422804014327
+            yield 1.4
+        swap(view)
+    save("slope")
     save("active")
-    yield need(3)
-    for view in range(3):
-        rows = pl.ds(*spans[view])
-        for j in range(FF // D):
-            w = weights.take((3, view * FF + j * D, 0))
-            term = matmul(v["active"][rows, pl.ds(j * D, D)], w[...])
-            weights.give_back()
-            layer[rows] = (v["middle"][rows] if j == 0 else layer[rows]) + term
-            yield 0.8
-    save("layer")
+    yield from products()
 
 
 def gather_kernel(dims, own_gains, *refs):
     refs = list(refs)
     take = lambda n: [refs.pop(0) for _ in range(n)]
     shards = take(4)
-    gain_tile, x = take(2)
+    gain_tile, x, cot = take(3)
     fulls = take(4)
-    gain_out, layer_out = take(2)
+    gain_out, down_part = take(2)
     kept_out = dict(zip(KEPT, take(len(KEPT))))
     theirs, merged = take(4), take(4)
-    gain_all, gain, layer = take(3)
+    gain_all, gain, d_out, far_d_out, far_active, made = take(6)
     v = dict(zip(KEPT, take(len(KEPT))))
-    ring, send, recv, local, ring_sem, save_sem = take(6)
+    ring, send, recv, local, ring_sem, save_sem, store_sem = take(7)
     place = Place(dims)
     copies = Copies(send, recv)
     core = place.core
@@ -676,19 +677,59 @@
     saves = []
 
     def save(name):
-        src, dst = (layer, layer_out) if name == "layer" else (v[name], kept_out[name])
-        copy = pltpu.make_async_copy(src, dst, save_sem.at[len(saves)])
+        copy = pltpu.make_async_copy(v[name], kept_out[name], save_sem.at[len(saves)])
         copy.start()
         saves.append(copy)
 
-    work = forward_work(place, copies, weights, need, gain, x, layer, v, save)
-    weave(march(sets, begin, (gains(),)), work, 0.8)
+    u = x.shape[0] // 7
+    spans = ((0, 4 * u), (4 * u, 2 * u), (6 * u, u))
+    d_out[...] = cot[...].astype(BF)
+    swap_out = copies.start(d_out.at[:, other[0]], far_d_out, place.sibling())
+    swapped = {}
+
+    def swap(view):
+        rows = pl.ds(*spans[view])
+        swapped[view] = copies.start(v["active"].at[rows], far_active.at[rows], place.sibling())
+
+    def products():
+        storing = {}
+        swap_out.wait_recv()
+        own_right = [jnp.where(core == 0, d_out[pl.ds(*s), :BLOCK], d_out[pl.ds(*s), BLOCK:]) for s in spans]
+        for view in range(3):
+            swapped[view].wait_recv()
+            rows = pl.ds(*spans[view])
+            right = jnp.concatenate([own_right[view], far_d_out[rows]], axis=0)
+            for j in range(FF // D):
+                i = view * (FF // D) + j
+                slot = i % 2
+                for one in storing.pop(i - 2, ()):
+                    one.wait()
+                cols = pl.ds(j * D, D)
+                left = jnp.concatenate([v["active"][rows, cols], far_active[rows, cols]], axis=0)
+                made[slot] = matmul_tn(left, right).astype(BF)
+                storing[i] = [
+                    pltpu.make_async_copy(
+                        made.at[slot, pl.ds(at_, n)], down_part.at[p, q, z, pl.ds(off, n)], store_sem.at[slot, k]
+                    )
+                    for k, (p, q, z, off, n, at_) in enumerate(row_runs(dims, slabs[3][0], view * FF + j * D, D))
+                ]
+                for one in storing[i]:
+                    one.start()
+                yield 0.8
+        for i in list(storing):
+            for one in storing.pop(i):
+                one.wait()
+
+    work = forward_work(place, copies, weights, need, gain, x, v, save, swap, products)
+    weave(march(sets, begin, (gains(),)), work, EACH_FORWARD)
+    for copy in pair[3]:
+        copy.wait_recv()
     for copy in saves:
         copy.wait()
     copies.drain()
 
 
-def gather_all(dims, own_gains, shards, tile, x):
+def gather_all(dims, own_gains, shards, tile, x, cot):
     slabs = [(2 * s.shape[0], s.shape[1]) for s in shards]
     anywhere = pl.BlockSpec(memory_space=pl.ANY)
     vmem = pl.BlockSpec(memory_space=pltpu.VMEM)
@@ -697,13 +738,19 @@
     outs = pl.pallas_call(
         functools.partial(gather_kernel, dims, own_gains),
         out_shape=[jax.ShapeDtypeStruct((*dims, *s), BF) for s in slabs]
-        + [jax.ShapeDtypeStruct((16, D), F32), jax.ShapeDtypeStruct(x.shape, F32)]
+        + [jax.ShapeDtypeStruct((16, D), F32), jax.ShapeDtypeStruct((*dims, slabs[3][0], D // 2), BF)]
         + [jax.ShapeDtypeStruct(*kept[k]) for k in KEPT],
-        in_specs=[vmem] * 6,
+        in_specs=[vmem] * 7,
         out_specs=[anywhere] * (6 + len(KEPT)),
         scratch_shapes=[pltpu.VMEM((r // 2, w // 2), BF) for r, w in slabs]
         + [pltpu.VMEM((r, w // 2), BF) for r, w in slabs]
-        + [pltpu.VMEM((*dims, 2, 8, 128), F32), pltpu.VMEM((16, D), F32), pltpu.VMEM(x.shape, F32)]
+        + [pltpu.VMEM((*dims, 2, 8, 128), F32), pltpu.VMEM((16, D), F32)]
+        + [
+            pltpu.VMEM(x.shape, BF),
+            pltpu.VMEM((x.shape[0], D // 2), BF),
+            pltpu.VMEM((x.shape[0], FF), BF),
+            pltpu.VMEM((2, D, BLOCK), BF),
+        ]
         + [pltpu.VMEM(*kept[k]) for k in KEPT]
         + [
             pltpu.VMEM((4, D, D), BF),
@@ -711,10 +758,11 @@
             pltpu.SemaphoreType.DMA((COPIES,)),
             pltpu.SemaphoreType.DMA((5,)),
             pltpu.SemaphoreType.DMA((4, segments)),
-            pltpu.SemaphoreType.DMA((1 + len(KEPT),)),
+            pltpu.SemaphoreType.DMA((len(KEPT),)),
+            pltpu.SemaphoreType.DMA((2, segments)),
         ],
         compiler_params=pltpu.CompilerParams(collective_id=0, has_side_effects=True, vmem_limit_bytes=60 << 20),
-    )(*shards, tile, x)
+    )(*shards, tile, x, cot)
     return outs[:4], outs[4], outs[5], dict(zip(KEPT, outs[6:]))
 
 
@@ -746,15 +794,6 @@
     def give_back(self):
         self.next_use += 1
         self.fetch()
-
-
-def row_runs(dims, slab, row, count):
-    at, end = row, row + count
-    while at < end:
-        chip, off = at // slab, at % slab
-        n = min(end - at, slab - off)
-        yield chip // (dims[1] * dims[2]), chip // dims[2] % dims[1], chip % dims[2], off, n, at - row
-        at += n
 
 
 def add_to(total, term):
@@ -868,7 +907,7 @@
         step += 1
 
 
-LEFTS = ("active", "normed_two", "mixed", "normed", "first", "second", "cmixed")
+LEFTS = ("normed_two", "mixed", "normed", "first", "second", "cmixed")
 RIGHTS = ("d_out", "d_pre", "d_attn", "dq", "dk", "dv", "d_cross", "dcq", "dck", "dcv")
 HELD = ("q", "kx", "vx", "cq", "ck", "cv")
 
@@ -882,10 +921,8 @@
 def job_batches(u):
     rows = ((0, 4 * u), (4 * u, 2 * u), (6 * u, u))
     late = ((0, 2 * u), (2 * u, u))
-    batches = {"down": [], "up": [], "out": [], "qkv": [], "cout": [], "cqkv": []}
+    batches = {"up": [], "out": [], "qkv": [], "cout": [], "cqkv": []}
     for view in range(3):
-        for block in range(FF // D):
-            batches["down"].append((3, view * FF + block * D, 0, "active", block, rows[view], "d_out", rows[view]))
         for block in range(FF // 2 // BLOCK):
             batches["up"].append((2, view * D, block, "normed_two", 0, rows[view], "d_pre", rows[view]))
         batches["out"].append((1, view * D, 0, "mixed", 0, rows[view], "d_attn", rows[view]))
@@ -920,10 +957,6 @@
         inner - jnp.mean(inner, axis=-1, keepdims=True) - unit * jnp.mean(inner * unit, axis=-1, keepdims=True)
     )
     return pulled, jnp.sum(grad * unit, axis=0, keepdims=True)
-
-
-def gelu_slope(pre):
-    return 0.5 * (1.0 + lax.erf(pre * (0.5**0.5))) + pre * jnp.exp(-0.5 * pre * pre) * 0.3989422804014327
 
 
 def attend_pair_back(query, keys, values, grad, bias):
@@ -964,22 +997,22 @@
     refs = list(refs)
     take = lambda n: [refs.pop(0) for _ in range(n)]
     wholes = take(4)
-    (cot, gain, x, joined, middle, hidden) = take(6)
-    lefts = dict(zip(LEFTS, take(7)))
+    (cot, gain, x, joined, middle, slope, active, down_part) = take(8)
+    lefts = dict(zip(LEFTS, take(6)))
     held_in = dict(zip(HELD, take(6)))
-    token_out = take(1)[0]
+    token_out, layer_out = take(2)
     results = take(4)
     (gain_out,) = take(1)
-    parts = take(4)
-    far_lefts, far_rights = dict(zip(LEFTS, take(7))), dict(zip(RIGHTS, take(10)))
+    parts = take(3) + [down_part]
+    far_lefts, far_rights = dict(zip(LEFTS, take(6))), dict(zip(RIGHTS, take(10)))
     rights = dict(zip(RIGHTS, take(10)))
     held = dict(zip(HELD, take(6)))
     acc, first, turns_a, turns_b, last_a, last_b = take(6)
     finals = take(4)
     xs, ys, made = take(3)
     g_far, g_own, g_acc, g_first, g_turns, g_last, g_sum = take(7)
-    ring, rowring, preing, flow, total, dmixed, dkf, dvf, halo_out, halo_in = take(10)
-    send, recv, local, load_sem, store_sem, final_sem, ring_sem, row_sem, pre_sem, held_sem, credit = take(11)
+    ring, rowring, preing, acting, layer, flow, total, dmixed, dkf, dvf, halo_out, halo_in = take(12)
+    send, recv, local, load_sem, store_sem, final_sem, ring_sem, row_sem, pre_sem, held_sem, layer_sem, credit = take(12)
     place = Place(dims)
     core = place.core
     copies = Copies(send, recv)
@@ -1018,11 +1051,13 @@
 
     def pre_maker(view, j):
         r0, n = spans[view]
-        return lambda slot: [(hidden.at[pl.ds(r0, n), pl.ds(j * D, D)], preing.at[slot, pl.ds(0, n)])]
-
-    swap("active")
+        block = (pl.ds(r0, n), pl.ds(j * D, D))
+        return lambda slot: [
+            (slope.at[block], preing.at[slot, pl.ds(0, n)]),
+            (active.at[block], acting.at[slot, pl.ds(0, n)]),
+        ]
+
     rights["d_out"][...] = cot[...].astype(BF)
-    swap("d_out")
     blocks = backward_blocks()
     weights = Stream(ring.shape[0], ring_sem, [weight_maker(b) for b in blocks])
     pres = Stream(2, pre_sem, [pre_maker(view, j) for view in range(3) for j in range(FF // D)])
@@ -1041,11 +1076,11 @@
     for i, name in enumerate(HELD):
         holding[name] = pltpu.make_async_copy(held_in[name], held[name], held_sem.at[i])
         holding[name].start()
-    for name in LEFTS[1:]:
+    for name in LEFTS:
         swap(name)
 
     state = {"jobs": 0, "gain": False}
-    ready = set()
+    ready = {3}
     storing = {}
 
     def finish_stores(i):
@@ -1111,26 +1146,30 @@
             cost = (2.0, 1.2, 0.9)[view]
             for j in range(FF // D):
                 cols = pl.ds(j * D, D)
-                dactive = matmul_nt(rights["d_out"][rows], weight((3, view * FF + j * D, 0)))
+                down_block = weight((3, view * FF + j * D, 0))
+                dactive = matmul_nt(rights["d_out"][rows], down_block)
+                slot = pres.take()
+                rights["d_pre"][rows, cols] = (dactive * preing[slot, :n]).astype(BF)
+                term = matmul(acting[slot, :n], down_block)
+                layer[rows] = term if j == 0 else layer[rows] + term
                 weights.give_back()
-                slot = pres.take()
-                rights["d_pre"][rows, cols] = (dactive * gelu_slope(preing[slot, :n])).astype(BF)
                 pres.give_back()
                 term = matmul_nt(rights["d_pre"][rows, cols], weight((2, view * D, j)))
                 weights.give_back()
                 total[:n] = term if j == 0 else total[:n] + term
                 yield cost
             slot = rowed.take()
-            pulled, g_sum[pl.ds(2 * view + 1, 1), :] = norm_pull(rowring[slot, :n], g(view, 1), total[:n])
+            mid = rowring[slot, :n]
+            layer[rows] = layer[rows] + mid
+            pulled, g_sum[pl.ds(2 * view + 1, 1), :] = norm_pull(mid, g(view, 1), total[:n])
             rowed.give_back()
             flow[rows] = cot[rows] + pulled
             rights["d_attn"][rows] = flow[rows].astype(BF)
             yield 0.8
-            if view == 0:
-                yield from multiply("down", 0.8)
-                ready.add(3)
         swap("d_pre")
         swap("d_attn")
+        layered = pltpu.make_async_copy(layer, layer_out, layer_sem)
+        layered.start()
         for view in range(3):
             rows = pl.ds(*spans[view])
             dmixed[rows] = matmul_nt(rights["d_attn"][rows], weight((1, view * D, 0))).astype(BF)
@@ -1240,6 +1279,7 @@
         ready.add(0)
         state["gain"] = True
         token.wait()
+        layered.wait()
 
     flat = [piece for group in sets for piece in group if piece != "gain"]
     owners = {}
@@ -1322,7 +1362,7 @@
     assert copies.used <= COPIES - 9 * len(flat)
 
 
-def reduce_all(dims, slabs, own_gains, wholes, cot, gain, x, kept):
+def reduce_all(dims, slabs, own_gains, wholes, down_part, cot, gain, x, kept):
     anywhere = pl.BlockSpec(memory_space=pl.ANY)
     vmem = pl.BlockSpec(memory_space=pltpu.VMEM)
     sets = pieces_of(slabs, (3, 2, 1, 0))
@@ -1340,14 +1380,14 @@
     rights = right_shapes(rows)
     outs = pl.pallas_call(
         functools.partial(reduce_kernel, dims, slabs, sets, own_gains),
-        out_shape=[jax.ShapeDtypeStruct((rows, D), F32)]
+        out_shape=[jax.ShapeDtypeStruct((rows, D), F32)] * 2
         + [jax.ShapeDtypeStruct((s[0] // 2, s[1]), F32) for s in slabs]
         + [jax.ShapeDtypeStruct((8, 128), F32)]
-        + [jax.ShapeDtypeStruct((*dims, s[0], s[1] // 2), BF) for s in slabs]
+        + [jax.ShapeDtypeStruct((*dims, s[0], s[1] // 2), BF) for s in slabs[:3]]
         + [jax.ShapeDtypeStruct(one.shape, BF) for one in lefts]
         + [jax.ShapeDtypeStruct((r, w // 2), BF) for r, w in rights],
-        in_specs=[anywhere] * 4 + [vmem] * 2 + [anywhere] * 17,
-        out_specs=[anywhere] * 27,
+        in_specs=[anywhere] * 4 + [vmem] * 2 + [anywhere] * 18,
+        out_specs=[anywhere] * 26,
         scratch_shapes=[pltpu.VMEM(s, BF) for s in rights]
         + [pltpu.VMEM(one.shape, BF) for one in held]
         + [
@@ -1373,6 +1413,8 @@
             pltpu.VMEM((4, D, D), BF),
             pltpu.VMEM((2, 4 * u, D), F32),
             pltpu.VMEM((2, 4 * u, D), F32),
+            pltpu.VMEM((2, 4 * u, D), BF),
+            pltpu.VMEM((rows, D), F32),
             pltpu.VMEM((rows, D), F32),
             pltpu.VMEM((4 * u, D), F32),
             pltpu.VMEM((rows, D), BF),
@@ -1388,13 +1430,14 @@
             pltpu.SemaphoreType.DMA((6,)),
             pltpu.SemaphoreType.DMA((4, segments)),
             pltpu.SemaphoreType.DMA((2, 1)),
-            pltpu.SemaphoreType.DMA((2, 1)),
+            pltpu.SemaphoreType.DMA((2, 2)),
             pltpu.SemaphoreType.DMA((6,)),
+            pltpu.SemaphoreType.DMA,
             pltpu.SemaphoreType.REGULAR((SLOTS, 2 + 2 * (z - 1))),
         ],
         compiler_params=pltpu.CompilerParams(collective_id=1, has_side_effects=True, vmem_limit_bytes=62 << 20),
-    )(*wholes, cot, gain, x, kept["joined"], kept["middle"], kept["hidden"], *lefts, *held)
-    return outs[:6]
+    )(*wholes, cot, gain, x, kept["joined"], kept["middle"], kept["slope"], kept["active"], down_part, *lefts, *held)
+    return outs[:7]
 
 
 def plain_device(tokens, cotangent, qkv_weights, out_weights, up_weights, down_weights, gains):
@@ -1612,10 +1655,10 @@
     tile = jnp.pad(gains.astype(F32).reshape(-1, 48), ((0, 8 - own_gains // 48), (0, 80)))
     shards = (qkv_weights, out_weights, up_weights, down_weights)
     slabs = tuple((2 * w.shape[0], w.shape[1]) for w in shards)
-    wholes, gain, layer_out, kept = gather_all(dims, own_gains, shards, tile, rows)
-    shares = reduce_all(dims, slabs, own_gains, wholes, cotangent[0], gain, rows, kept)
-    gain_share = shares[5][: own_gains // 48, :48].reshape(own_gains)
-    return (layer_out[None], shares[0][None], *shares[1:5], gain_share)
+    wholes, gain, down_part, kept = gather_all(dims, own_gains, shards, tile, rows, cotangent[0])
+    shares = reduce_all(dims, slabs, own_gains, wholes, down_part, cotangent[0], gain, rows, kept)
+    gain_share = shares[6][: own_gains // 48, :48].reshape(own_gains)
+    return (shares[1][None], shares[0][None], *shares[2:6], gain_share)
 
 
 def fits(mesh, dims):

time: 584 us -> 537 us (0.920)
  Pallas kernels: 564 us -> 517 us
    pallas_call x1, Pallas kernels: 314 us -> 271 us  [reduce_all(): pl.pallas_call(functools.partial(reduce_kernel, dims, slabs, sets, own_ga...]
where the time goes in v4:
time: 537 us; the launch traced here: 529 us
  Pallas kernels  517 us (96%)
  local copies, waits for them, and re-layouts  10.2 us (2%)
    pallas_call x1, Pallas kernels, reduce_all(): pl.pallas_call(functools.partial(reduce_kernel, dims, slabs, sets, own_ga...  271 us
    pallas_call x1, Pallas kernels, gather_all(): pl.pallas_call(functools.partial(gather_kernel, dims, own_gains), out_sha...  246 us

profile of v4, /device:TPU:0, one launch (start us, length us, event | category | flops | bytes accessed | tf_op | source)
XLA Modules:
  0.0 528.5 jit_solution(8648288015459552819)
XLA Ops:
  0.6 0.7 reshape.21
  1.4 0.6 pad_convert_fusion.refs_4_
  2.0 246.0 %shard_map.126 = (bf16[2,2,4,720,768]{4,3,2,1,0:T(8,128)(2,1)}, bf16[2,2,4,240,768]{4,3,2,1,0:T(8,128)(2,1)}, bf16[2,2,4,144,3072]{4,3,2,1,0:T(8,128)(2,1)}, bf1...) custom-call(bf16[360,768]{1,0:T(8,128)(2,1)} %refs_0_.1, ...), custom_call_target="tpu_custom_call" | custom-call | tf_op jit(solution)/shard_map/pallas_call | solution.py:738
  248.0 270.7 %shard_map.127 = (f32[448,768]{1,0:T(8,128)}, f32[448,768]{1,0:T(8,128)}, f32[360,768]{1,0:T(8,128)}, f32[120,768]{1,0:T(8,128)}, f32[72,3072]{1,0:T(8,128)}, /*...) custom-call(bf16[2,2,4,720,768]{4,3,2,1,0:T(8,128)(2,1)} %get-tuple-, ...), custom_call_target="tpu_custom_call" | custom-call | tf_op jit(solution)/shard_map/pallas_call | solution.py:1381
  518.6 1.3 reshape.22
  519.9 0.0 copy-start
  519.9 2.6 copy.20
  522.6 0.0 copy-done
  522.6 0.0 copy-start.1
  522.6 1.1 copy.21
  523.6 0.7 copy-done.1
  524.3 0.0 copy-start.4
  524.3 0.0 copy-start.3
  524.3 1.0 copy.22
  525.3 0.2 copy-done.4
  525.5 0.0 copy-start.2
  525.5 0.7 copy.23
  526.2 0.0 copy-done.3
  526.2 0.9 copy.24
  527.2 0.0 copy-done.2
  527.2 0.9 copy.25
Async XLA Ops:
  519.9 2.6 copy-start
  522.6 1.7 copy-start.1
  524.3 1.2 copy-start.4
  524.3 1.9 copy-start.3
  525.5 1.7 copy-start.2

commit v5 on v4

--- a/solution.py
+++ b/solution.py
@@ -18,10 +18,10 @@
 F32 = jnp.float32
 BLOCK = D // 2
 ROWS = 48
-LAG = 0.5
-SLOTS = 18
-EACH = 1.0
-EACH_FORWARD = 0.5
+POOLS = (0, 0, 8, 8, 4, 4)
+SLOTS = sum(POOLS)
+EACH = (6.48, 0.8, 12.38)
+EACH_FORWARD = 1.07
 COPIES = 480
 
 
@@ -254,28 +254,42 @@
         pair.append(copies.start(part, part, place.sibling()))
 
 
-ZXY, ZYX, XZY, YZX = (2, 1, 0), (2, 0, 1), (1, 2, 0), (0, 2, 1)
-CYCLE = (XZY, YZX, ZXY, XZY, YZX, ZYX)
-
-
-def pieces_of(slabs, arrays):
+XYZ, YXZ, XZY, YZX, ZXY, ZYX = (1, 0, 2), (0, 1, 2), (1, 2, 0), (0, 2, 1), (2, 1, 0), (2, 0, 1)
+ORDERS = (XYZ, YXZ, XZY, YZX, ZXY, ZYX)
+CYCLE = (2, 3, 4, 2, 3, 5)
+GATHER_PLAN = (
+    (5, 0), (5, 0), (4, 0), (5, 1), (2, 2), (5, 2), (4, 2), (5, 3), (2, 3), (1, 3), (3, 3),
+    (4, 3), (5, 3), (5, 3), (4, 3), (2, 4), (5, 4), (4, 4), (4, 4), (5, 4), (4, 5), (3, 5),
+    (2, 5), (3, 5), (3, 5), (1, 5), (2, 5), (4, 5), (3, 5), (4, 5), (0, 5), (5, 5), (2, 6),
+    (5, 6), (4, 6), (5, 6), (5, 7), (1, 7), (2, 7), (1, 7), (4, 7), (0, 7), (0, 7), (5, 7),
+)
+REDUCE_PLAN = (
+    (2, 0), (3, 0), (3, 0), (2, 0), (5, 0), (4, 0), (2, 0), (3, 0), (2, 0), (3, 1), (2, 1),
+    (3, 1), (5, 2), (2, 2), (5, 2), (4, 2), (3, 3), (4, 3), (4, 4), (5, 4), (3, 4), (2, 4),
+    (2, 4), (3, 4), (3, 5), (4, 6), (2, 6), (2, 6), (3, 6), (5, 6), (2, 6), (3, 6), (5, 7),
+    (2, 7), (4, 7), (5, 7), (2, 7), (3, 7), (3, 7), (2, 8), (5, 9), (2, 10), (4, 10), (3, 10),
+)
+
+
+def pieces_of(slabs, arrays, plan):
     flat = []
     for array in arrays:
         rows, width = slabs[array]
         for block in range(width // 2 // BLOCK):
             for row in range(0, rows, ROWS):
-                flat.append((array, row, block, CYCLE[len(flat) % 6]))
-    return [flat[i : i + 3] for i in range(0, len(flat), 3)]
-
-
-def march(sets, begin, extra=()):
-    waiting = list(sets)
+                i = len(flat)
+                order, start = plan[i] if i < len(plan) else (CYCLE[i % 6], plan[-1][1] + (i - len(plan)) // 6)
+                flat.append((array, row, block, ORDERS[order], start))
+    return flat
+
+
+def march(pieces, begin, extra=()):
+    waiting = list(pieces)
     active = list(extra)
     step = 0
     while active or waiting:
-        while waiting and step >= LAG * (len(sets) - len(waiting)):
-            for piece in waiting.pop(0):
-                active.append(begin(piece))
+        while waiting and step >= waiting[0][4]:
+            active.append(begin(waiting.pop(0)))
         still = []
         for one in active:
             try:
@@ -313,7 +327,7 @@
     while live[0] or live[1]:
         moved = advance(0)
         if moved is not None:
-            credit = min(credit + each, 4.0)
+            credit = min(credit + each(), 4.0)
         stuck = moved is None
         while live[1] and (credit > 0 or stuck):
             cost = advance(1)
@@ -458,8 +472,8 @@
     return (place.at[0] * place.dims[1] + place.at[1], t)
 
 
-def slab_bias(place, count, width, spatial):
-    col = lax.broadcasted_iota(jnp.int32, (1, width), 1)
+def slab_bias(place, count, width, spatial, axis=1):
+    col = lax.broadcasted_iota(jnp.int32, (1, width) if axis else (width, 1), axis)
     below = (col < spatial) & (place.slab == 0)
     above = (col >= width - spatial) & (place.slab == count - 1)
     return jnp.where(below | above, FAR, 0.0).astype(F32)
@@ -612,8 +626,8 @@
     own_tile[...] = gain_tile[...]
     swap_gain = copies.start(own_tile, own_tile, place.sibling())
     slabs = [(m.shape[0], 2 * m.shape[1]) for m in merged]
-    sets = pieces_of(slabs, range(4))
-    left = {a: sum(1 for s in sets for piece in s if piece[0] == a) for a in range(4)}
+    pieces = pieces_of(slabs, range(4), GATHER_PLAN)
+    left = {a: sum(1 for piece in pieces if piece[0] == a) for a in range(4)}
     pair = {a: [] for a in range(4)}
     ready = set()
     state = {"gain": False}
@@ -631,7 +645,7 @@
         copy.wait()
 
     def begin(piece):
-        a, row, block, order = piece
+        a, row, block, order, _ = piece
         if a not in ready:
             prepare(a)
             ready.add(a)
@@ -721,7 +735,7 @@
                 one.wait()
 
     work = forward_work(place, copies, weights, need, gain, x, v, save, swap, products)
-    weave(march(sets, begin, (gains(),)), work, EACH_FORWARD)
+    weave(march(pieces, begin, (gains(),)), work, lambda: EACH_FORWARD)
     for copy in pair[3]:
         copy.wait_recv()
     for copy in saves:
@@ -801,16 +815,26 @@
 
 
 class Credits:
-    def __init__(self, sems, waits, gives):
-        self.sems, self.waits, self.gives = sems, waits, gives
+    def __init__(self, sems, waits):
+        self.sems, self.waits = sems, waits
 
     def wait(self, index, ok=None):
         if self.waits:
             when(ok, lambda: pl.semaphore_wait(self.sems.at[index], 1))
 
     def give(self, index, device):
-        if self.gives:
+        if self.sems is not None:
             pl.semaphore_signal(self.sems.at[index], inc=1, device_id=device, device_id_type=MESH)
+
+    def settle(self, place):
+        self.waits = True
+        n, z = place.dims[2], place.at[2]
+        self.wait(0)
+        self.wait(1)
+        for turn in range(n - 1):
+            for step in (1, -1):
+                far = z if step == 1 else n - 1 - z
+                self.wait(2 + 2 * turn + (1 - step) // 2, far <= turn)
 
 
 def reduce_line(copies, place, pick, slots, credits):
@@ -875,23 +899,15 @@
         finish(acc[mine, z].astype(F32))
 
 
-def march_ready(sets, begin, ready, limit):
-    waiting = list(sets)
+def march_ready(pieces, begin, ready):
+    waiting = list(pieces)
     active = []
     step = 0
-    started = 0
     while active or waiting:
-        while (
-            waiting
-            and step >= LAG * started
-            and len(active) + len(waiting[0]) <= limit
-            and ready(waiting[0])
-        ):
-            for piece in waiting.pop(0):
-                active.append(begin(piece))
-            started += 1
+        while waiting and step >= waiting[0][4] and ready(waiting[0]):
+            active.append(begin(waiting.pop(0)))
         if not active:
-            if step < LAG * started:
+            if step < waiting[0][4]:
                 step += 1
             else:
                 yield lambda: ready(waiting[0])
@@ -962,16 +978,17 @@
 def attend_pair_back(query, keys, values, grad, bias):
     dq, dk, dv = [], None, None
     for part, g in zip(halves_of(query), halves_of(grad)):
-        scores = matmul_nt(part, keys) * 0.125
+        scores = matmul_nt(keys, part) * 0.125
         if bias is not None:
             scores = scores + bias
-        probs = softmax_rows(scores)
-        dprobs = matmul_nt(g, values)
-        inner = jnp.sum(dprobs * probs, axis=-1, keepdims=True)
+        expo = jnp.exp(scores - jnp.max(scores, axis=0, keepdims=True))
+        probs = expo * (1.0 / jnp.sum(expo, axis=0, keepdims=True))
+        dprobs = matmul_nt(values, g)
+        inner = jnp.sum(dprobs * probs, axis=0, keepdims=True)
         dscores = (probs * (dprobs - inner) * 0.125).astype(BF)
-        dq.append(matmul(dscores, keys))
-        k_term = matmul_tn(dscores, part)
-        v_term = matmul_tn(probs.astype(BF), g)
+        dq.append(matmul_tn(dscores, keys))
+        k_term = matmul(dscores, part)
+        v_term = matmul(probs.astype(BF), g)
         dk = k_term if dk is None else dk + k_term
         dv = v_term if dv is None else dv + v_term
     low = lax.broadcasted_iota(jnp.int32, dq[0].shape, 1) < dq[0].shape[1] // 2
@@ -993,7 +1010,7 @@
     return jnp.dot(wide, fold.astype(F32), precision=lax.Precision.HIGHEST, preferred_element_type=F32)
 
 
-def reduce_kernel(dims, slabs, sets, own_gains, *refs):
+def reduce_kernel(dims, slabs, pieces, own_gains, *refs):
     refs = list(refs)
     take = lambda n: [refs.pop(0) for _ in range(n)]
     wholes = take(4)
@@ -1011,8 +1028,8 @@
     finals = take(4)
     xs, ys, made = take(3)
     g_far, g_own, g_acc, g_first, g_turns, g_last, g_sum = take(7)
-    ring, rowring, preing, acting, layer, flow, total, dmixed, dkf, dvf, halo_out, halo_in = take(12)
-    send, recv, local, load_sem, store_sem, final_sem, ring_sem, row_sem, pre_sem, held_sem, layer_sem, credit = take(12)
+    ring, rowring, preing, acting, layer, flow, total, dvf, halo_out, halo_in = take(10)
+    send, recv, local, left_sem, right_sem, store_sem, final_sem, ring_sem, row_sem, pre_sem, held_sem, layer_sem, credit = take(13)
     place = Place(dims)
     core = place.core
     copies = Copies(send, recv)
@@ -1079,7 +1096,7 @@
     for name in LEFTS:
         swap(name)
 
-    state = {"jobs": 0, "gain": False}
+    state = {"jobs": 0, "lefts": 0, "gain": False}
     ready = {3}
     storing = {}
 
@@ -1087,53 +1104,75 @@
         for one in storing.pop(i, ()):
             one.wait()
 
-    def load(job, i):
-        a, row, block, left, lcol, lrows, right, rrows = job
+    def load_left(group, slot):
+        left, lcol, lrows = group
         arrive(left)
-        arrive(right)
-        slot = i % 2
         n = lrows[1]
-        ref = rights[right]
-        own = pl.ds(pl.multiple_of(core * (ref.shape[1] // 2) + block * BLOCK, 128), BLOCK)
-        pairs = [
-            (lefts[left].at[pl.ds(*lrows), pl.ds(lcol * D, D)], xs.at[slot, pl.ds(0, n)]),
-            (far_lefts[left].at[pl.ds(*lrows), pl.ds(lcol * D, D)], xs.at[slot, pl.ds(n, n)]),
-            (ref.at[pl.ds(*rrows), own], ys.at[slot, pl.ds(0, n)]),
-            (far_rights[right].at[pl.ds(*rrows), pl.ds(block * BLOCK, BLOCK)], ys.at[slot, pl.ds(n, n)]),
+        block = (pl.ds(*lrows), pl.ds(lcol * D, D))
+        loads = [
+            pltpu.make_async_copy(lefts[left].at[block], xs.at[slot, pl.ds(0, n)], left_sem.at[slot, 0]),
+            pltpu.make_async_copy(far_lefts[left].at[block], xs.at[slot, pl.ds(n, n)], left_sem.at[slot, 1]),
         ]
-        loads = [pltpu.make_async_copy(s, d, load_sem.at[slot, j]) for j, (s, d) in enumerate(pairs)]
         for one in loads:
             one.start()
         return loads
 
+    def load_right(job, slot):
+        block, right, rrows = job[2], job[6], job[7]
+        arrive(right)
+        n = rrows[1]
+        ref = rights[right]
+        own = pl.ds(pl.multiple_of(core * (ref.shape[1] // 2) + block * BLOCK, 128), BLOCK)
+        far = (pl.ds(*rrows), pl.ds(block * BLOCK, BLOCK))
+        loads = [
+            pltpu.make_async_copy(ref.at[pl.ds(*rrows), own], ys.at[slot, pl.ds(0, n)], right_sem.at[slot, 0]),
+            pltpu.make_async_copy(far_rights[right].at[far], ys.at[slot, pl.ds(n, n)], right_sem.at[slot, 1]),
+        ]
+        for one in loads:
+            one.start()
+        return loads
+
     batches = job_batches(u)
 
     def multiply(name, cost):
         batch = batches[name]
-        loading = load(batch[0], state["jobs"])
+        groups, member = [], []
+        for job in batch:
+            if not groups or groups[-1] != job[3:6]:
+                groups.append(job[3:6])
+            member.append(len(groups) - 1)
+        x0, i0 = state["lefts"], state["jobs"]
+        left_loads = {k: load_left(groups[k], (x0 + k) % 2) for k in range(min(2, len(groups)))}
+        right_loads = {k: load_right(batch[k], (i0 + k) % 3) for k in range(min(2, len(batch)))}
         for index, job in enumerate(batch):
-            i = state["jobs"]
-            slot = i % 2
-            for one in loading:
+            i, k = i0 + index, member[index]
+            if k in left_loads:
+                for one in left_loads.pop(k):
+                    one.wait()
+                if 0 < k < len(groups) - 1:
+                    left_loads[k + 1] = load_left(groups[k + 1], (x0 + k + 1) % 2)
+            for one in right_loads.pop(index):
                 one.wait()
-            if index + 1 < len(batch):
-                loading = load(batch[index + 1], i + 1)
+            if index + 2 < len(batch):
+                right_loads[index + 2] = load_right(batch[index + 2], (i + 2) % 3)
             finish_stores(i - 2)
             n = 2 * job[5][1]
-            made[slot] = matmul_tn(xs[slot, :n], ys[slot, :n]).astype(BF)
+            slot = i % 2
+            made[slot] = matmul_tn(xs[(x0 + k) % 2, :n], ys[i % 3, :n]).astype(BF)
             a, row, block = job[:3]
             storing[i] = [
                 pltpu.make_async_copy(
                     made.at[slot, pl.ds(at, n)],
                     parts[a].at[p, q, z, pl.ds(off, n), pl.ds(block * BLOCK, BLOCK)],
-                    store_sem.at[slot, k],
+                    store_sem.at[slot, j],
                 )
-                for k, (p, q, z, off, n, at) in enumerate(row_runs(dims, slabs[a][0], row, D))
+                for j, (p, q, z, off, n, at) in enumerate(row_runs(dims, slabs[a][0], row, D))
             ]
             for one in storing[i]:
                 one.start()
-            state["jobs"] += 1
             yield cost
+        state["lefts"] += len(groups)
+        state["jobs"] += len(batch)
         for i in list(storing):
             finish_stores(i)
 
@@ -1170,21 +1209,24 @@
         swap("d_attn")
         layered = pltpu.make_async_copy(layer, layer_out, layer_sem)
         layered.start()
+        dmixed = rights["d_out"]
         for view in range(3):
             rows = pl.ds(*spans[view])
             dmixed[rows] = matmul_nt(rights["d_attn"][rows], weight((1, view * D, 0))).astype(BF)
             weights.give_back()
             yield 0.7
-        yield from multiply("up", 0.8)
+        yield from multiply("up", 0.6)
         ready.add(2)
         for name in ("q", "kx", "vx"):
             holding[name].wait()
+        layered.wait()
+        dkf = layer
         halo = {}
         up, down = place.slab < count - 1, place.slab > 0
         for view in range(3):
             r0, n = spans[view]
             rows, keys = pl.ds(r0, n), pl.ds(bases[view], n + 2 * u)
-            bias = slab_bias(place, count, n + 2 * u, u)
+            bias = slab_bias(place, count, n + 2 * u, u, 0)
             for h in range(HEADS // 2):
                 cols = pl.ds(h * 128, 128)
                 dq, dk, dv = attend_pair_back(
@@ -1202,7 +1244,7 @@
                         halo_out.at[k, view, side], halo_in.at[k, view, side], halo_device(place, count, step), ok
                     )
         swap("dq")
-        yield from multiply("out", 0.8)
+        yield from multiply("out", 0.6)
         for view in range(3):
             r0, n = spans[view]
             rows = pl.ds(r0, n)
@@ -1231,7 +1273,7 @@
         swap("d_cross")
         for name in ("cq", "ck", "cv"):
             holding[name].wait()
-        yield from multiply("qkv", 0.8)
+        yield from multiply("qkv", 0.6)
         for c in range(2):
             r0, n = spans[c]
             k0, m = spans[c + 1]
@@ -1267,7 +1309,7 @@
             yield 1.0
         for name in ("dcq", "dck", "dcv"):
             swap(name)
-        yield from multiply("cout", 0.8)
+        yield from multiply("cout", 0.6)
         ready.add(1)
         token = pltpu.make_async_copy(flow, token_out, final_sem.at[4])
         token.start()
@@ -1275,18 +1317,17 @@
         g_own[...] = gain_tiles(g_sum[...], 2 * dims[0] * dims[1] * dims[2] * 8, own_gains).reshape(g_own.shape)
         coming["gain"] = copies.start(g_own, g_far, place.sibling())
         yield 1.0
-        yield from multiply("cqkv", 0.8)
+        yield from multiply("cqkv", 0.6)
         ready.add(0)
         state["gain"] = True
         token.wait()
-        layered.wait()
-
-    flat = [piece for group in sets for piece in group if piece != "gain"]
-    owners = {}
-    kinds = [0 if piece[3][1] == 2 else 1 for piece in flat[:SLOTS]]
-    left_in = {a: sum(1 for piece in flat if piece[0] == a) for a in range(4)}
+
+    left_in = {a: sum(1 for piece in pieces if piece[0] == a) for a in range(4)}
+    count_pieces = sum(left_in.values())
+    bases_of = [sum(POOLS[:k]) for k in range(len(POOLS))]
+    free = {k: [[bases_of[k] + j, None, None] for j in range(POOLS[k])] for k in range(len(POOLS))}
+    owners = []
     ending = []
-    begun = {"n": 0}
 
     def gains():
         coming["gain"].wait_recv()
@@ -1300,25 +1341,26 @@
             copy.wait()
 
         yield from reduce_piece(
-            copies, place, source, (0, 1, 2), g_acc, g_first, g_turns, g_last, local.at[SLOTS], Credits(None, False, False), finish
+            copies, place, source, (0, 1, 2), g_acc, g_first, g_turns, g_last, local.at[SLOTS], Credits(None, False), finish
         )
 
     def begin(piece):
-        if piece == "gain":
+        if piece[0] == "gain":
             return gains()
-        a, row, block, order = piece
-        i = begun["n"]
-        begun["n"] += 1
-        slot = i % SLOTS
-        if i >= SLOTS:
-            owners[i - SLOTS].drain()
+        a, row, block, order, _ = piece
+        kind = ORDERS.index(order)
+        buffer = free[kind].pop(0)
+        slot, before, _ = buffer
+        if before is not None:
+            before.drain()
         mine = Copies(send, recv)
-        mine.used = COPIES - 9 * (len(flat) - i)
-        owners[i] = mine
+        mine.used = COPIES - 9 * (count_pieces - len(owners))
+        owners.append(mine)
+        buffer[1] = mine
         cols = pl.ds(block * BLOCK, BLOCK)
-        kind = kinds[slot]
-        k = kinds[:slot].count(kind)
-        turns, last = ((turns_a, last_a), (turns_b, last_b))[kind]
+        single = order[1] != 2
+        k = slot - sum(POOLS[:4]) if single else slot
+        turns, last = ((turns_a, last_a), (turns_b, last_b))[single]
 
         def source(dim, value):
             index = [slice(None)] * 3
@@ -1328,10 +1370,12 @@
         def finish(value):
             finals[a][pl.ds(row, ROWS), cols] = value
             left_in[a] -= 1
+            free[kind].append(buffer)
             if left_in[a] == 0:
                 deliver(a)
 
-        credits = Credits(credit.at[slot], i >= SLOTS, i + SLOTS < len(flat))
+        credits = Credits(credit.at[slot], before is not None)
+        buffer[2] = credits
         return reduce_piece(
             mine, place, source, order[::-1], acc.at[slot], first.at[slot], turns.at[k], last.at[k], local.at[slot], credits, finish
         )
@@ -1350,26 +1394,30 @@
         keep.start()
         keep.wait()
 
-    def set_ready(group):
-        return state["gain"] if group[0] == "gain" else all(piece[0] in ready for piece in group)
-
-    weave(march_ready(sets, begin, set_ready, SLOTS), work(), EACH)
+    def piece_ready(piece):
+        if piece[0] == "gain":
+            return state["gain"]
+        return piece[0] in ready and bool(free[ORDERS.index(piece[3])])
+
+    weave(march_ready(pieces, begin, piece_ready), work(), lambda: EACH[min(len(ready) - 1, 2)])
+    for buffers in free.values():
+        for slot, user, credits in buffers:
+            if user is not None:
+                credits.settle(place)
     for one in ending:
         one.wait_recv()
     copies.drain()
-    for one in owners.values():
+    for one in owners:
         one.drain()
-    assert copies.used <= COPIES - 9 * len(flat)
+    assert copies.used <= COPIES - 9 * count_pieces
 
 
 def reduce_all(dims, slabs, own_gains, wholes, down_part, cot, gain, x, kept):
     anywhere = pl.BlockSpec(memory_space=pl.ANY)
     vmem = pl.BlockSpec(memory_space=pltpu.VMEM)
-    sets = pieces_of(slabs, (3, 2, 1, 0))
-    flat = [piece for group in sets for piece in group]
-    sets.insert(len(sets) - 3, ["gain"])
-    kinds = [0 if piece[3][1] == 2 else 1 for piece in flat[:SLOTS]]
-    bundled, single = kinds.count(0), kinds.count(1)
+    pieces = pieces_of(slabs, (3, 2, 1, 0), REDUCE_PLAN)
+    pieces.insert(len(pieces) - 8, ("gain", 0, 0, None, pieces[-9][4]))
+    bundled, single = sum(POOLS[:4]), sum(POOLS[4:])
     z = dims[2]
     rows = cot.shape[0]
     u = rows // 7
@@ -1379,7 +1427,7 @@
     held = [kept[k] for k in HELD]
     rights = right_shapes(rows)
     outs = pl.pallas_call(
-        functools.partial(reduce_kernel, dims, slabs, sets, own_gains),
+        functools.partial(reduce_kernel, dims, slabs, pieces, own_gains),
         out_shape=[jax.ShapeDtypeStruct((rows, D), F32)] * 2
         + [jax.ShapeDtypeStruct((s[0] // 2, s[1]), F32) for s in slabs]
         + [jax.ShapeDtypeStruct((8, 128), F32)]
@@ -1401,7 +1449,7 @@
         + [pltpu.VMEM((s[0], s[1] // 2), F32) for s in slabs]
         + [
             pltpu.VMEM((2, 8 * u, D), BF),
-            pltpu.VMEM((2, 8 * u, BLOCK), BF),
+            pltpu.VMEM((3, 8 * u, BLOCK), BF),
             pltpu.VMEM((2, D, BLOCK), BF),
             pltpu.VMEM((*dims, 2, 8, 128), F32),
             pltpu.VMEM((*dims, 2, 8, 128), F32),
@@ -1417,15 +1465,14 @@
             pltpu.VMEM((rows, D), F32),
             pltpu.VMEM((rows, D), F32),
             pltpu.VMEM((4 * u, D), F32),
-            pltpu.VMEM((rows, D), BF),
-            pltpu.VMEM((rows, D), F32),
             pltpu.VMEM((rows, D), F32),
             pltpu.VMEM((2, 3, 2, u, D), BF),
             pltpu.VMEM((2, 3, 2, u, D), BF),
             pltpu.SemaphoreType.DMA((COPIES,)),
             pltpu.SemaphoreType.DMA((COPIES,)),
             pltpu.SemaphoreType.DMA((SLOTS + 1,)),
-            pltpu.SemaphoreType.DMA((2, 4)),
+            pltpu.SemaphoreType.DMA((2, 2)),
+            pltpu.SemaphoreType.DMA((3, 2)),
             pltpu.SemaphoreType.DMA((2, segments)),
             pltpu.SemaphoreType.DMA((6,)),
             pltpu.SemaphoreType.DMA((4, segments)),
@@ -1435,7 +1482,7 @@
             pltpu.SemaphoreType.DMA,
             pltpu.SemaphoreType.REGULAR((SLOTS, 2 + 2 * (z - 1))),
         ],
-        compiler_params=pltpu.CompilerParams(collective_id=1, has_side_effects=True, vmem_limit_bytes=62 << 20),
+        compiler_params=pltpu.CompilerParams(collective_id=1, has_side_effects=True, vmem_limit_bytes=63 << 20),
     )(*wholes, cot, gain, x, kept["joined"], kept["middle"], kept["slope"], kept["active"], down_part, *lefts, *held)
     return outs[:7]
 

time: 537 us -> 488 us (0.909)
  Pallas kernels: 517 us -> 468 us
    pallas_call x1, Pallas kernels: 246 us -> 218 us  [gather_all(): pl.pallas_call(functools.partial(gather_kernel, dims, own_gains), out_sha...]
    pallas_call x1, Pallas kernels: 271 us -> 250 us  [reduce_all(): pl.pallas_call(functools.partial(reduce_kernel, dims, slabs, pieces, own_...]
where the time goes in v5:
time: 488 us; the launch traced here: 480 us
  Pallas kernels  468 us (96%)
  local copies, waits for them, and re-layouts  10.2 us (2%)
    pallas_call x1, Pallas kernels, reduce_all(): pl.pallas_call(functools.partial(reduce_kernel, dims, slabs, pieces, own_...  250 us
    pallas_call x1, Pallas kernels, gather_all(): pl.pallas_call(functools.partial(gather_kernel, dims, own_gains), out_sha...  218 us

profile of v5, /device:TPU:0, one launch (start us, length us, event | category | flops | bytes accessed | tf_op | source)
XLA Modules:
  0.0 480.0 jit_solution(1468673333397632652)
XLA Ops:
  0.6 0.7 reshape.21
  1.4 0.6 pad_convert_fusion.refs_4_
  2.0 218.4 %shard_map.126 = (bf16[2,2,4,720,768]{4,3,2,1,0:T(8,128)(2,1)}, bf16[2,2,4,240,768]{4,3,2,1,0:T(8,128)(2,1)}, bf16[2,2,4,144,3072]{4,3,2,1,0:T(8,128)(2,1)}, bf1...) custom-call(bf16[360,768]{1,0:T(8,128)(2,1)} %refs_0_.1, ...), custom_call_target="tpu_custom_call" | custom-call | tf_op jit(solution)/shard_map/pallas_call | solution.py:752
  220.4 249.7 %shard_map.127 = (f32[448,768]{1,0:T(8,128)}, f32[448,768]{1,0:T(8,128)}, f32[360,768]{1,0:T(8,128)}, f32[120,768]{1,0:T(8,128)}, f32[72,3072]{1,0:T(8,128)}, /*...) custom-call(bf16[2,2,4,720,768]{4,3,2,1,0:T(8,128)(2,1)} %get-tuple-, ...), custom_call_target="tpu_custom_call" | custom-call | tf_op jit(solution)/shard_map/pallas_call | solution.py:1429
  470.1 1.3 reshape.22
  471.4 0.0 copy-start
  471.4 2.6 copy.20
  474.0 0.0 copy-done
  474.0 0.0 copy-start.1
  474.0 1.1 copy.21
  475.1 0.7 copy-done.1
  475.8 0.0 copy-start.4
  475.8 0.0 copy-start.3
  475.8 1.0 copy.22
  476.8 0.2 copy-done.4
  477.0 0.0 copy-start.2
  477.0 0.7 copy.23
  477.7 0.0 copy-done.3
  477.7 0.9 copy.24
  478.6 0.0 copy-done.2
  478.6 0.9 copy.25
Async XLA Ops:
  471.4 2.6 copy-start
  474.0 1.7 copy-start.1
  475.8 1.2 copy-start.4
  475.8 1.9 copy-start.3
  477.0 1.7 copy-start.2

commit v6 on v5

--- a/solution.py
+++ b/solution.py
@@ -20,7 +20,7 @@
 ROWS = 48
 POOLS = (0, 0, 8, 8, 4, 4)
 SLOTS = sum(POOLS)
-EACH = (6.48, 0.8, 12.38)
+EACH = (1.51, 0.49, 0.68, 0.42)
 EACH_FORWARD = 1.07
 COPIES = 480
 
@@ -264,10 +264,10 @@
     (5, 6), (4, 6), (5, 6), (5, 7), (1, 7), (2, 7), (1, 7), (4, 7), (0, 7), (0, 7), (5, 7),
 )
 REDUCE_PLAN = (
-    (2, 0), (3, 0), (3, 0), (2, 0), (5, 0), (4, 0), (2, 0), (3, 0), (2, 0), (3, 1), (2, 1),
-    (3, 1), (5, 2), (2, 2), (5, 2), (4, 2), (3, 3), (4, 3), (4, 4), (5, 4), (3, 4), (2, 4),
-    (2, 4), (3, 4), (3, 5), (4, 6), (2, 6), (2, 6), (3, 6), (5, 6), (2, 6), (3, 6), (5, 7),
-    (2, 7), (4, 7), (5, 7), (2, 7), (3, 7), (3, 7), (2, 8), (5, 9), (2, 10), (4, 10), (3, 10),
+    (3, 0), (2, 0), (3, 0), (3, 0), (2, 0), (2, 0), (3, 0), (2, 0), (2, 1), (5, 1), (3, 2),
+    (3, 2), (2, 2), (3, 2), (2, 2), (4, 2), (5, 2), (3, 4), (5, 4), (4, 4), (4, 4), (5, 4),
+    (2, 4), (2, 4), (3, 4), (3, 4), (2, 4), (2, 4), (3, 5), (2, 6), (3, 6), (2, 6), (2, 6),
+    (4, 6), (5, 6), (3, 6), (3, 6), (4, 6), (5, 6), (2, 6), (5, 6), (4, 6), (4, 6), (5, 6),
 )
 
 
@@ -959,8 +959,9 @@
             blocks += [(3, view * FF + j * D, 0), (2, view * D, j)]
     blocks += [(1, view * D, 0) for view in range(3)]
     blocks += [(0, i * D, 0) for i in range(9)]
-    for c in range(2):
-        blocks += [(1, (3 + c) * D, 0)] + [(0, (9 + 3 * c + j) * D, 0) for j in range(3)]
+    blocks += [(1, (3 + c) * D, 0) for c in range(2)]
+    blocks += [(0, (9 + j) * D, 0) for j in range(6)]
+    blocks += [(3, view * FF + j * D, 0) for view in range(3) for j in range(FF // D)]
     return blocks
 
 
@@ -1029,7 +1030,7 @@
     xs, ys, made = take(3)
     g_far, g_own, g_acc, g_first, g_turns, g_last, g_sum = take(7)
     ring, rowring, preing, acting, layer, flow, total, dvf, halo_out, halo_in = take(10)
-    send, recv, local, left_sem, right_sem, store_sem, final_sem, ring_sem, row_sem, pre_sem, held_sem, layer_sem, credit = take(13)
+    send, recv, local, left_sem, right_sem, store_sem, final_sem, ring_sem, row_sem, pre_sem, act_sem, held_sem, layer_sem, credit = take(14)
     place = Place(dims)
     core = place.core
     copies = Copies(send, recv)
@@ -1069,18 +1070,22 @@
     def pre_maker(view, j):
         r0, n = spans[view]
         block = (pl.ds(r0, n), pl.ds(j * D, D))
-        return lambda slot: [
-            (slope.at[block], preing.at[slot, pl.ds(0, n)]),
-            (active.at[block], acting.at[slot, pl.ds(0, n)]),
-        ]
+        return lambda slot: [(slope.at[block], preing.at[slot, pl.ds(0, n)])]
+
+    def act_maker(view, j):
+        r0, n = spans[view]
+        block = (pl.ds(r0, n), pl.ds(j * D, D))
+        return lambda slot: [(active.at[block], acting.at[slot, pl.ds(0, n)])]
 
     rights["d_out"][...] = cot[...].astype(BF)
     blocks = backward_blocks()
     weights = Stream(ring.shape[0], ring_sem, [weight_maker(b) for b in blocks])
     pres = Stream(2, pre_sem, [pre_maker(view, j) for view in range(3) for j in range(FF // D)])
+    acts = Stream(2, act_sem, [act_maker(view, j) for view in range(3) for j in range(FF // D)])
     row_list = [(middle, *spans[view]) for view in range(3)] + [(joined, *spans[view]) for view in range(3)]
     for c in range(2):
         row_list += [(x, *spans[c]), (x, *spans[c + 1])]
+    row_list += [(middle, *spans[view]) for view in range(3)]
     rowed = Stream(2, row_sem, [row_maker(*one) for one in row_list])
     used_blocks = []
 
@@ -1182,33 +1187,26 @@
         for view in range(3):
             r0, n = spans[view]
             rows = pl.ds(r0, n)
-            cost = (2.0, 1.2, 0.9)[view]
+            cost = (1.5, 0.9, 0.7)[view]
             for j in range(FF // D):
                 cols = pl.ds(j * D, D)
-                down_block = weight((3, view * FF + j * D, 0))
-                dactive = matmul_nt(rights["d_out"][rows], down_block)
+                dactive = matmul_nt(rights["d_out"][rows], weight((3, view * FF + j * D, 0)))
+                weights.give_back()
                 slot = pres.take()
                 rights["d_pre"][rows, cols] = (dactive * preing[slot, :n]).astype(BF)
-                term = matmul(acting[slot, :n], down_block)
-                layer[rows] = term if j == 0 else layer[rows] + term
-                weights.give_back()
                 pres.give_back()
                 term = matmul_nt(rights["d_pre"][rows, cols], weight((2, view * D, j)))
                 weights.give_back()
                 total[:n] = term if j == 0 else total[:n] + term
                 yield cost
             slot = rowed.take()
-            mid = rowring[slot, :n]
-            layer[rows] = layer[rows] + mid
-            pulled, g_sum[pl.ds(2 * view + 1, 1), :] = norm_pull(mid, g(view, 1), total[:n])
+            pulled, g_sum[pl.ds(2 * view + 1, 1), :] = norm_pull(rowring[slot, :n], g(view, 1), total[:n])
             rowed.give_back()
             flow[rows] = cot[rows] + pulled
             rights["d_attn"][rows] = flow[rows].astype(BF)
             yield 0.8
         swap("d_pre")
         swap("d_attn")
-        layered = pltpu.make_async_copy(layer, layer_out, layer_sem)
-        layered.start()
         dmixed = rights["d_out"]
         for view in range(3):
             rows = pl.ds(*spans[view])
@@ -1219,7 +1217,6 @@
         ready.add(2)
         for name in ("q", "kx", "vx"):
             holding[name].wait()
-        layered.wait()
         dkf = layer
         halo = {}
         up, down = place.slab < count - 1, place.slab > 0
@@ -1237,7 +1234,7 @@
                     halo_out[k, view, 0, :, cols] = whole[:u].astype(BF)
                     own[rows, cols] = whole[u : u + n]
                     halo_out[k, view, 1, :, cols] = whole[u + n :].astype(BF)
-                yield (3.0, 1.3, 0.7)[view]
+                yield (2.0, 0.9, 0.5)[view]
             for k in range(2):
                 for side, step, ok in ((0, -1, down), (1, 1, up)):
                     halo[k, view, side] = copies.start(
@@ -1273,14 +1270,15 @@
         swap("d_cross")
         for name in ("cq", "ck", "cv"):
             holding[name].wait()
-        yield from multiply("qkv", 0.6)
+        yield from multiply("cout", 0.6)
+        ready.add(1)
         for c in range(2):
-            r0, n = spans[c]
-            k0, m = spans[c + 1]
-            rows, keys = pl.ds(r0, n), pl.ds(k0 - 4 * u, m)
+            rows = pl.ds(*spans[c])
             dmixed[rows] = matmul_nt(rights["d_cross"][rows], weight((1, (3 + c) * D, 0))).astype(BF)
             weights.give_back()
             yield 0.7
+        for c in range(2):
+            rows, keys = pl.ds(*spans[c]), pl.ds(spans[c + 1][0] - 4 * u, spans[c + 1][1])
             for h in range(HEADS // 2):
                 cols = pl.ds(h * 128, 128)
                 dq, dk, dv = attend_pair_back(
@@ -1289,7 +1287,16 @@
                 rights["dcq"][rows, cols] = dq.astype(BF)
                 rights["dck"][keys, cols] = dk.astype(BF)
                 rights["dcv"][keys, cols] = dv.astype(BF)
-                yield (1.5, 0.6)[c]
+                yield (1.0, 0.45)[c]
+        for name in ("dcq", "dck", "dcv"):
+            swap(name)
+        yield from multiply("qkv", 0.6)
+        yield from multiply("cqkv", 0.6)
+        ready.add(0)
+        for c in range(2):
+            r0, n = spans[c]
+            k0, m = spans[c + 1]
+            rows, keys, late = pl.ds(r0, n), pl.ds(k0 - 4 * u, m), pl.ds(k0, m)
             term = matmul_nt(rights["dcq"][rows], weight((0, (9 + 3 * c) * D, 0)))
             weights.give_back()
             slot = rowed.take()
@@ -1304,23 +1311,32 @@
             slot = rowed.take()
             pulled, g_sum[pl.ds(2 * (3 + c) + 1, 1), :] = norm_pull(rowring[slot, :m], g(3 + c, 1), term)
             rowed.give_back()
-            late = pl.ds(k0, m)
             flow[late] = flow[late] + pulled
             yield 1.0
-        for name in ("dcq", "dck", "dcv"):
-            swap(name)
-        yield from multiply("cout", 0.6)
-        ready.add(1)
         token = pltpu.make_async_copy(flow, token_out, final_sem.at[4])
         token.start()
         g_sum[pl.ds(10, 6), :] = jnp.zeros((6, D), F32)
         g_own[...] = gain_tiles(g_sum[...], 2 * dims[0] * dims[1] * dims[2] * 8, own_gains).reshape(g_own.shape)
         coming["gain"] = copies.start(g_own, g_far, place.sibling())
+        state["gain"] = True
         yield 1.0
-        yield from multiply("cqkv", 0.6)
-        ready.add(0)
-        state["gain"] = True
+        for view in range(3):
+            r0, n = spans[view]
+            rows = pl.ds(r0, n)
+            for j in range(FF // D):
+                slot = acts.take()
+                term = matmul(acting[slot, :n], weight((3, view * FF + j * D, 0)))
+                acts.give_back()
+                weights.give_back()
+                layer[rows] = term if j == 0 else layer[rows] + term
+                yield 0.6
+            slot = rowed.take()
+            layer[rows] = layer[rows] + rowring[slot, :n]
+            rowed.give_back()
+        layered = pltpu.make_async_copy(layer, layer_out, layer_sem)
+        layered.start()
         token.wait()
+        layered.wait()
 
     left_in = {a: sum(1 for piece in pieces if piece[0] == a) for a in range(4)}
     count_pieces = sum(left_in.values())
@@ -1399,7 +1415,7 @@
             return state["gain"]
         return piece[0] in ready and bool(free[ORDERS.index(piece[3])])
 
-    weave(march_ready(pieces, begin, piece_ready), work(), lambda: EACH[min(len(ready) - 1, 2)])
+    weave(march_ready(pieces, begin, piece_ready), work(), lambda: EACH[len(ready) - 1])
     for buffers in free.values():
         for slot, user, credits in buffers:
             if user is not None:
@@ -1416,7 +1432,7 @@
     anywhere = pl.BlockSpec(memory_space=pl.ANY)
     vmem = pl.BlockSpec(memory_space=pltpu.VMEM)
     pieces = pieces_of(slabs, (3, 2, 1, 0), REDUCE_PLAN)
-    pieces.insert(len(pieces) - 8, ("gain", 0, 0, None, pieces[-9][4]))
+    pieces.append(("gain", 0, 0, None, pieces[-1][4]))
     bundled, single = sum(POOLS[:4]), sum(POOLS[4:])
     z = dims[2]
     rows = cot.shape[0]
@@ -1477,7 +1493,8 @@
             pltpu.SemaphoreType.DMA((6,)),
             pltpu.SemaphoreType.DMA((4, segments)),
             pltpu.SemaphoreType.DMA((2, 1)),
-            pltpu.SemaphoreType.DMA((2, 2)),
+            pltpu.SemaphoreType.DMA((2, 1)),
+            pltpu.SemaphoreType.DMA((2, 1)),
             pltpu.SemaphoreType.DMA((6,)),
             pltpu.SemaphoreType.DMA,
             pltpu.SemaphoreType.REGULAR((SLOTS, 2 + 2 * (z - 1))),

time: 488 us -> 474 us (0.971)
  Pallas kernels: 468 us -> 454 us
    pallas_call x1, Pallas kernels: 250 us -> 236 us  [reduce_all(): pl.pallas_call(functools.partial(reduce_kernel, dims, slabs, pieces, own_...]
where the time goes in v6:
time: 474 us; the launch traced here: 466 us
  Pallas kernels  454 us (96%)
  local copies, waits for them, and re-layouts  10.2 us (2%)
    pallas_call x1, Pallas kernels, reduce_all(): pl.pallas_call(functools.partial(reduce_kernel, dims, slabs, pieces, own_...  236 us
    pallas_call x1, Pallas kernels, gather_all(): pl.pallas_call(functools.partial(gather_kernel, dims, own_gains), out_sha...  218 us

profile of v6, /device:TPU:0, one launch (start us, length us, event | category | flops | bytes accessed | tf_op | source)
XLA Modules:
  0.0 466.2 jit_solution(592923101450342342)
XLA Ops:
  0.6 0.7 reshape.21
  1.4 0.6 pad_convert_fusion.refs_4_
  2.0 218.4 %shard_map.126 = (bf16[2,2,4,720,768]{4,3,2,1,0:T(8,128)(2,1)}, bf16[2,2,4,240,768]{4,3,2,1,0:T(8,128)(2,1)}, bf16[2,2,4,144,3072]{4,3,2,1,0:T(8,128)(2,1)}, bf1...) custom-call(bf16[360,768]{1,0:T(8,128)(2,1)} %refs_0_.1, ...), custom_call_target="tpu_custom_call" | custom-call | tf_op jit(solution)/shard_map/pallas_call | solution.py:752
  220.4 235.9 %shard_map.127 = (f32[448,768]{1,0:T(8,128)}, f32[448,768]{1,0:T(8,128)}, f32[360,768]{1,0:T(8,128)}, f32[120,768]{1,0:T(8,128)}, f32[72,3072]{1,0:T(8,128)}, /*...) custom-call(bf16[2,2,4,720,768]{4,3,2,1,0:T(8,128)(2,1)} %get-tuple-, ...), custom_call_target="tpu_custom_call" | custom-call | tf_op jit(solution)/shard_map/pallas_call | solution.py:1445
  456.3 1.3 reshape.22
  457.6 0.0 copy-start
  457.6 2.6 copy.20
  460.2 0.0 copy-done
  460.2 0.0 copy-start.1
  460.2 1.1 copy.21
  461.3 0.7 copy-done.1
  462.0 0.0 copy-start.4
  462.0 0.0 copy-start.3
  462.0 1.0 copy.22
  463.0 0.2 copy-done.4
  463.2 0.0 copy-start.2
  463.2 0.7 copy.23
  463.9 0.0 copy-done.3
  463.9 0.9 copy.24
  464.8 0.0 copy-done.2
  464.8 0.9 copy.25
Async XLA Ops:
  457.6 2.6 copy-start
  460.2 1.7 copy-start.1
  462.0 1.2 copy-start.4
  462.0 1.9 copy-start.3
  463.2 1.7 copy-start.2

commit v7 on v6

--- a/solution.py
+++ b/solution.py
@@ -18,9 +18,9 @@
 F32 = jnp.float32
 BLOCK = D // 2
 ROWS = 48
-POOLS = (0, 0, 8, 8, 4, 4)
+POOLS = (0, 0, 10, 10, 4, 4)
 SLOTS = sum(POOLS)
-EACH = (1.51, 0.49, 0.68, 0.42)
+EACH = (1.78, 0.49, 0.58, 0.14)
 EACH_FORWARD = 1.07
 COPIES = 480
 
@@ -264,10 +264,10 @@
     (5, 6), (4, 6), (5, 6), (5, 7), (1, 7), (2, 7), (1, 7), (4, 7), (0, 7), (0, 7), (5, 7),
 )
 REDUCE_PLAN = (
-    (3, 0), (2, 0), (3, 0), (3, 0), (2, 0), (2, 0), (3, 0), (2, 0), (2, 1), (5, 1), (3, 2),
-    (3, 2), (2, 2), (3, 2), (2, 2), (4, 2), (5, 2), (3, 4), (5, 4), (4, 4), (4, 4), (5, 4),
-    (2, 4), (2, 4), (3, 4), (3, 4), (2, 4), (2, 4), (3, 5), (2, 6), (3, 6), (2, 6), (2, 6),
-    (4, 6), (5, 6), (3, 6), (3, 6), (4, 6), (5, 6), (2, 6), (5, 6), (4, 6), (4, 6), (5, 6),
+    (5, 0), (2, 0), (3, 0), (2, 0), (4, 0), (3, 0), (5, 0), (2, 0), (3, 0), (3, 1), (2, 1),
+    (5, 2), (2, 2), (3, 2), (2, 3), (3, 3), (3, 3), (2, 3), (4, 3), (5, 3), (3, 4), (2, 4),
+    (3, 4), (4, 4), (2, 4), (3, 4), (2, 4), (3, 4), (2, 4), (2, 4), (3, 5), (4, 6), (5, 6),
+    (3, 6), (2, 6), (2, 6), (3, 6), (2, 6), (5, 6), (4, 6), (3, 6), (4, 6), (5, 6), (5, 6),
 )
 
 
@@ -869,6 +869,7 @@
     rest = 1 - lead
     me, mine = place.at[lead], place.at[rest]
     z = place.at[2]
+    z_last = place.dims[2] - 1
     beside, across = place.along(lead, 1 - me), place.along(rest, 1 - mine)
     credits.wait(0)
     copy = copies.start(source(lead, 1 - me), first, beside)
@@ -879,7 +880,7 @@
     copy.wait_recv()
     add_to(acc, first)
     credits.give(0, beside)
-    slots = lambda turn, step: turns.at[turn, (1 - step) // 2]
+    slots = lambda turn, step: turns.at[turn if step == 1 or turn == 0 else z_last + turn - 1]
     if order[1] == 2:
         yield from reduce_line(copies, place, lambda v: acc.at[:, v], slots, credits)
         credits.wait(1)
@@ -1077,7 +1078,8 @@
         block = (pl.ds(r0, n), pl.ds(j * D, D))
         return lambda slot: [(active.at[block], acting.at[slot, pl.ds(0, n)])]
 
-    rights["d_out"][...] = cot[...].astype(BF)
+    incoming = pltpu.make_async_copy(cot, flow, final_sem.at[4])
+    incoming.start()
     blocks = backward_blocks()
     weights = Stream(ring.shape[0], ring_sem, [weight_maker(b) for b in blocks])
     pres = Stream(2, pre_sem, [pre_maker(view, j) for view in range(3) for j in range(FF // D)])
@@ -1184,6 +1186,8 @@
     g = lambda e, j: gain[pl.ds(2 * e + j, 1), :]
 
     def work():
+        incoming.wait()
+        rights["d_out"][...] = flow[...].astype(BF)
         for view in range(3):
             r0, n = spans[view]
             rows = pl.ds(r0, n)
@@ -1202,7 +1206,7 @@
             slot = rowed.take()
             pulled, g_sum[pl.ds(2 * view + 1, 1), :] = norm_pull(rowring[slot, :n], g(view, 1), total[:n])
             rowed.give_back()
-            flow[rows] = cot[rows] + pulled
+            flow[rows] = flow[rows] + pulled
             rights["d_attn"][rows] = flow[rows].astype(BF)
             yield 0.8
         swap("d_pre")
@@ -1450,15 +1454,15 @@
         + [jax.ShapeDtypeStruct((*dims, s[0], s[1] // 2), BF) for s in slabs[:3]]
         + [jax.ShapeDtypeStruct(one.shape, BF) for one in lefts]
         + [jax.ShapeDtypeStruct((r, w // 2), BF) for r, w in rights],
-        in_specs=[anywhere] * 4 + [vmem] * 2 + [anywhere] * 18,
+        in_specs=[anywhere] * 5 + [vmem] + [anywhere] * 18,
         out_specs=[anywhere] * 26,
         scratch_shapes=[pltpu.VMEM(s, BF) for s in rights]
         + [pltpu.VMEM(one.shape, BF) for one in held]
         + [
             pltpu.VMEM((SLOTS, 2, z, *tile), BF),
             pltpu.VMEM((SLOTS, 2, z, *tile), BF),
-            pltpu.VMEM((bundled, z - 1, 2, 2, *tile), BF),
-            pltpu.VMEM((single, z - 1, 2, *tile), BF),
+            pltpu.VMEM((bundled, 2 * z - 3, 2, *tile), BF),
+            pltpu.VMEM((single, 2 * z - 3, *tile), BF),
             pltpu.VMEM((bundled, *tile), BF),
             pltpu.VMEM((single, z, *tile), BF),
         ]
@@ -1471,10 +1475,10 @@
             pltpu.VMEM((*dims, 2, 8, 128), F32),
             pltpu.VMEM((2, z, 8, 128), F32),
             pltpu.VMEM((2, z, 8, 128), F32),
-            pltpu.VMEM((z - 1, 2, 8, 128), F32),
+            pltpu.VMEM((2 * z - 3, 8, 128), F32),
             pltpu.VMEM((z, 8, 128), F32),
             pltpu.VMEM((16, D), F32),
-            pltpu.VMEM((4, D, D), BF),
+            pltpu.VMEM((3, D, D), BF),
             pltpu.VMEM((2, 4 * u, D), F32),
             pltpu.VMEM((2, 4 * u, D), F32),
             pltpu.VMEM((2, 4 * u, D), BF),
@@ -1491,7 +1495,7 @@
             pltpu.SemaphoreType.DMA((3, 2)),
             pltpu.SemaphoreType.DMA((2, segments)),
             pltpu.SemaphoreType.DMA((6,)),
-            pltpu.SemaphoreType.DMA((4, segments)),
+            pltpu.SemaphoreType.DMA((3, segments)),
             pltpu.SemaphoreType.DMA((2, 1)),
             pltpu.SemaphoreType.DMA((2, 1)),
             pltpu.SemaphoreType.DMA((2, 1)),
@@ -1728,7 +1732,7 @@
 def fits(mesh, dims):
     chips = dims[0] * dims[1] * dims[2]
     rows = (15 * D, 5 * D, 3 * D, 3 * FF)
-    return dims[:2] == (2, 2) and all(r % (chips * ROWS) == 0 for r in rows) and (10 * D) % (2 * chips * 48) == 0 and 10 * D // (2 * chips) <= 384
+    return dims[:2] == (2, 2) and dims[2] > 3 and all(r % (chips * ROWS) == 0 for r in rows) and (10 * D) % (2 * chips * 48) == 0 and 10 * D // (2 * chips) <= 384
 
 
 def solution(mesh):

time: 474 us -> 468 us (0.987)
  Pallas kernels: 454 us -> 449 us
    pallas_call x1, Pallas kernels: 236 us -> 230 us  [reduce_all(): pl.pallas_call(functools.partial(reduce_kernel, dims, slabs, pieces, own_...]
where the time goes in v7:
time: 468 us; the launch traced here: 460 us
  Pallas kernels  449 us (96%)
  local copies, waits for them, and re-layouts  10.2 us (2%)
    pallas_call x1, Pallas kernels, reduce_all(): pl.pallas_call(functools.partial(reduce_kernel, dims, slabs, pieces, own_...  230 us
    pallas_call x1, Pallas kernels, gather_all(): pl.pallas_call(functools.partial(gather_kernel, dims, own_gains), out_sha...  218 us

profile of v7, /device:TPU:0, one launch (start us, length us, event | category | flops | bytes accessed | tf_op | source)
XLA Modules:
  0.0 460.3 jit_solution(8438132690803654062)
XLA Ops:
  0.6 0.7 reshape.21
  1.4 0.6 pad_convert_fusion.refs_4_
  2.0 218.2 %shard_map.126 = (bf16[2,2,4,720,768]{4,3,2,1,0:T(8,128)(2,1)}, bf16[2,2,4,240,768]{4,3,2,1,0:T(8,128)(2,1)}, bf16[2,2,4,144,3072]{4,3,2,1,0:T(8,128)(2,1)}, bf1...) custom-call(bf16[360,768]{1,0:T(8,128)(2,1)} %refs_0_.1, ...), custom_call_target="tpu_custom_call" | custom-call | tf_op jit(solution)/shard_map/pallas_call | solution.py:752
  220.1 230.5 %shard_map.127 = (f32[448,768]{1,0:T(8,128)}, f32[448,768]{1,0:T(8,128)}, f32[360,768]{1,0:T(8,128)}, f32[120,768]{1,0:T(8,128)}, f32[72,3072]{1,0:T(8,128)}, /*...) custom-call(bf16[2,2,4,720,768]{4,3,2,1,0:T(8,128)(2,1)} %get-tuple-, ...), custom_call_target="tpu_custom_call" | custom-call | tf_op jit(solution)/shard_map/pallas_call | solution.py:1449
  450.7 1.3 reshape.22
  452.0 0.0 copy-start
  452.0 2.6 copy.20
  454.6 0.0 copy-done
  454.6 0.0 copy-start.1
  454.6 1.1 copy.21
  455.7 0.7 copy-done.1
  456.3 0.0 copy-start.4
  456.3 0.0 copy-start.3
  456.3 1.0 copy.22
  457.3 0.2 copy-done.4
  457.5 0.0 copy-start.2
  457.5 0.7 copy.23
  458.3 0.0 copy-done.3
  458.3 0.9 copy.24
  459.2 0.0 copy-done.2
  459.2 0.9 copy.25
Async XLA Ops:
  452.0 2.6 copy-start
  454.6 1.7 copy-start.1
  456.3 1.2 copy-start.4
  456.3 1.9 copy-start.3
  457.5 1.7 copy-start.2
